TPU v7x, 256 devices: a whole 4x4x8 slice. The times are simulated.
256 devices in a mesh: member: 16 (over y, x_lo, core), space: 16 (over x_hi, z).
Axes of the slice: x: 4 (x_hi: 2, x_lo: 2; x = x_hi * 2 + x_lo), y: 4, z: 8, core: 2. Of those that a mesh axis runs over, the one named last changes fastest.
Arguments:
- layer_input: bfloat16 [64, 4096, 256], P('member', 'space'), may hold values from -6 to 6
- out_grad: bfloat16 [64, 4096, 256], P('member', 'space'), may hold values from -6 to 6
- norm1_gain: float32 [256], replicated, as said below
- w_query: bfloat16 [256, 256], replicated, as said below
- w_key: bfloat16 [256, 256], replicated, as said below
- w_value: bfloat16 [256, 256], replicated, may hold values from -0.375 to 0.375
- w_out: bfloat16 [256, 256], replicated, may hold values from -0.375 to 0.375
- norm2_gain: float32 [256], replicated, may hold values from 0.5 to 1.5
- w_up: bfloat16 [256, 1024], replicated, may hold values from -0.375 to 0.375
- w_down: bfloat16 [1024, 256], replicated, may hold values from -0.1875 to 0.1875
Outputs:
- input_grad: float32 [64, 4096, 256], P('member', 'space')
- grad_query: float32 [256, 256], replicated
- grad_key: float32 [256, 256], replicated
- grad_value: float32 [256, 256], replicated
- grad_wout: float32 [256, 256], replicated
- grad_up: float32 [256, 1024], replicated
- grad_down: float32 [1024, 256], replicated
- grad_gain1: float32 [256], replicated
- grad_gain2: float32 [256], replicated
Inputs may be any that keep to these rules, and one draw needn't show every extreme that they name: `norm1_gain`: positive gains, between 0.5 and 3. `w_query`: entries of a query projection. `w_key`: entries of a key projection.
All inputs are finite; a program needn't handle non-finite values.
Results may differ from a plain program's by a relative error of at most 0.008.
The roundings to bfloat16 on the way count: a program that leaves them out, or rounds other values in their place, can miss the bound.
Values may be sent and summed in bfloat16 or wider, within the bound.
No kernel may reach another device: no remote copies, remote signals or barrier semaphores. Data moves between devices by JAX's collectives and lax.ppermute only.
A program may use at most 128 MiB of HBM per device.

v0:
```python
import math

import jax
import jax.numpy as jnp
from jax import lax
from jax.sharding import PartitionSpec as P

HEAD_DIM = 32


EPS = 1e-06
GELU_C = 0.7978845608028654
GELU_A = 0.044715


def multiply(form, left, right):
    return jnp.einsum(form, left, right, preferred_element_type=jnp.float32)


def norm_rows(values):
    inverse = lax.rsqrt(jnp.mean(values * values, axis=-1, keepdims=True) + EPS)
    return (values * inverse, inverse)


def norm_back(unit_rows, inverse, gains, upstream):
    scaled = upstream * gains
    into = inverse * (scaled - unit_rows * jnp.mean(scaled * unit_rows, axis=-1, keepdims=True))
    return (into, jnp.sum(upstream * unit_rows, axis=(0, 1)))


def gelu_pair(preact):
    tangent = jnp.tanh(GELU_C * (preact + GELU_A * preact * preact * preact))
    result = 0.5 * preact * (1.0 + tangent)
    slopes = 0.5 * (1.0 + tangent) + 0.5 * preact * (1.0 - tangent * tangent) * GELU_C * (
        1.0 + 3.0 * GELU_A * preact * preact
    )
    return (result, slopes)


def attend(query, keys, values, heads):
    members, count, width = query.shape
    shape_four = (members, count, heads, width // heads)
    scale = 1.0 / math.sqrt(width // heads)
    scores = (
        multiply("mphe,nphe->phmn", query.reshape(shape_four), keys.reshape(shape_four)) * scale
    )
    scores = scores - jnp.max(scores, axis=-1, keepdims=True)
    weights = jnp.exp(scores)
    weights = weights / jnp.sum(weights, axis=-1, keepdims=True)
    rounded = weights.astype(jnp.bfloat16)
    mixed = multiply("phmn,nphe->mphe", rounded, values.reshape(shape_four)).astype(jnp.bfloat16)
    return (weights, rounded, mixed.reshape(members, count, width))


def attend_back(query, keys, values, weights, rounded, upstream, heads):
    members, count, width = query.shape
    shape_four = (members, count, heads, width // heads)
    scale = 1.0 / math.sqrt(width // heads)
    up_four = upstream.reshape(shape_four)
    dprob = multiply("mphe,nphe->phmn", up_four, values.reshape(shape_four))
    grad_v = multiply("phmn,mphe->nphe", rounded, up_four).astype(jnp.bfloat16)
    dscore = (weights * (dprob - jnp.sum(weights * dprob, axis=-1, keepdims=True)) * scale).astype(
        jnp.bfloat16
    )
    grad_q = multiply("phmn,nphe->mphe", dscore, keys.reshape(shape_four)).astype(jnp.bfloat16)
    grad_k = multiply("phmn,mphe->nphe", dscore, query.reshape(shape_four)).astype(jnp.bfloat16)
    return (
        grad_q.reshape(members, count, width),
        grad_k.reshape(members, count, width),
        grad_v.reshape(members, count, width),
    )


def on_device(
    layer_input, out_grad, norm1_gain, w_query, w_key, w_value, w_out, norm2_gain, w_up, w_down
):
    groups = lax.axis_size("member")
    own_members, own_patches, width = layer_input.shape
    spread = own_patches // groups
    everyone = own_members * groups
    heads = width // HEAD_DIM

    def patchwise(array):
        return array.reshape(own_members, groups, spread, array.shape[-1])

    def memberwise(array):
        return array.reshape(everyone, 1, spread, array.shape[-1])

    wide = layer_input.astype(jnp.float32)
    unit1, inverse1 = norm_rows(wide)
    normed1 = (unit1 * norm1_gain).astype(jnp.bfloat16)
    query = multiply("mpd,de->mpe", normed1, w_query).astype(jnp.bfloat16)
    keys = multiply("mpd,de->mpe", normed1, w_key).astype(jnp.bfloat16)
    values = multiply("mpd,de->mpe", normed1, w_value).astype(jnp.bfloat16)
    moved = (
        lax.all_to_all(patchwise(query), "member", split_axis=1, concat_axis=0, tiled=True),
        lax.all_to_all(patchwise(keys), "member", split_axis=1, concat_axis=0, tiled=True),
        lax.all_to_all(patchwise(values), "member", split_axis=1, concat_axis=0, tiled=True),
    )
    query_here = moved[0].reshape(everyone, spread, width)
    keys_here = moved[1].reshape(everyone, spread, width)
    values_here = moved[2].reshape(everyone, spread, width)
    weights, rounded, mixed_here = attend(query_here, keys_here, values_here, heads)
    mixed = lax.all_to_all(
        memberwise(mixed_here), "member", split_axis=0, concat_axis=1, tiled=True
    ).reshape(own_members, own_patches, width)
    hidden_state = wide + multiply("mpd,de->mpe", mixed, w_out)
    unit2, inverse2 = norm_rows(hidden_state)
    normed2 = (unit2 * norm2_gain).astype(jnp.bfloat16)
    preact = multiply("mpd,df->mpf", normed2, w_up)
    activated, slopes = gelu_pair(preact)
    activated = activated.astype(jnp.bfloat16)
    part_down = multiply("mpf,mpd->fd", activated, out_grad)
    grad_act = multiply("mpd,fd->mpf", out_grad, w_down)
    grad_pre = (grad_act * slopes).astype(jnp.bfloat16)
    part_up = multiply("mpd,mpf->df", normed2, grad_pre)
    grad_normed2 = multiply("mpf,df->mpd", grad_pre, w_up)
    back_two, part_gain2 = norm_back(unit2, inverse2, norm2_gain, grad_normed2)
    grad_hidden = out_grad.astype(jnp.float32) + back_two
    grad_attn = grad_hidden.astype(jnp.bfloat16)
    part_wout = multiply("mpd,mpe->de", mixed, grad_attn)
    grad_mixed = multiply("mpe,de->mpd", grad_attn, w_out).astype(jnp.bfloat16)
    grad_mixed_here = lax.all_to_all(
        patchwise(grad_mixed), "member", split_axis=1, concat_axis=0, tiled=True
    ).reshape(everyone, spread, width)
    grad_q, grad_k, grad_v = attend_back(
        query_here, keys_here, values_here, weights, rounded, grad_mixed_here, heads
    )
    moved_back = (
        lax.all_to_all(memberwise(grad_q), "member", split_axis=0, concat_axis=1, tiled=True),
        lax.all_to_all(memberwise(grad_k), "member", split_axis=0, concat_axis=1, tiled=True),
        lax.all_to_all(memberwise(grad_v), "member", split_axis=0, concat_axis=1, tiled=True),
    )
    grad_q = moved_back[0].reshape(own_members, own_patches, width)
    grad_k = moved_back[1].reshape(own_members, own_patches, width)
    grad_v = moved_back[2].reshape(own_members, own_patches, width)
    part_query = multiply("mpd,mpe->de", normed1, grad_q)
    part_key = multiply("mpd,mpe->de", normed1, grad_k)
    part_value = multiply("mpd,mpe->de", normed1, grad_v)
    grad_normed1 = (
        multiply("mpe,de->mpd", grad_q, w_query)
        + multiply("mpe,de->mpd", grad_k, w_key)
        + multiply("mpe,de->mpd", grad_v, w_value)
    )
    back_one, part_gain1 = norm_back(unit1, inverse1, norm1_gain, grad_normed1)
    input_grad = grad_hidden + back_one
    totals = lax.psum(
        (part_query, part_key, part_value, part_wout, part_up, part_down, part_gain1, part_gain2),
        ("member", "space"),
    )
    scale = 1.0 / math.sqrt(everyone * own_patches * lax.axis_size("space"))
    return (
        input_grad,
        totals[0] * scale,
        totals[1] * scale,
        totals[2] * scale,
        totals[3] * scale,
        totals[4] * scale,
        totals[5] * scale,
        totals[6] * scale,
        totals[7] * scale,
    )


def solution(mesh):
    in_specs = (
        P("member", "space", None),
        P("member", "space", None),
        P(),
        P(),
        P(),
        P(),
        P(),
        P(),
        P(),
        P(),
    )
    out_specs = (P("member", "space", None), P(), P(), P(), P(), P(), P(), P(), P())
    return jax.shard_map(
        on_device, mesh=mesh, in_specs=in_specs, out_specs=out_specs, check_vma=False
    )
```

profile of v0, /device:TPU:1, one launch (start us, length us, event | category | flops | bytes accessed | tf_op | source)
XLA Modules:
  0.0 469.4 jit_solution(16457893717433521840)
XLA Ops:
  10.9 6.9 %all-to-all-start.1 = ((bf16[4,16,16,256]{3,2,0,1:T(8,128)(2,1)}), bf16[4,16,16,256]{3,2,0,1:T(8,128)(2,1)S(1)}, u32[]{:S(2)}, u32[]{:S(2)}) async-start(bf16[4,16,16,256]{3,2,0,1:T(8,128)(2,1)} %copy.94), calls=%async_computation.1 | async-start | bytes 1048576 | tf_op jit(solution)/shard_map/all_to_all | solution.py:96
  19.1 8.5 %all-to-all-done.1 = bf16[4,16,16,256]{3,2,0,1:T(8,128)(2,1)S(1)} async-done(((bf16[4,16,16,256]{3,2,0,1:T(8,128)(2,1)}), bf16[4,16,16,256]{3,2,0,1:T(8,128)(2,1)S(1)}, u32[]{:S(2)}, u32[]{:S(2)}) %all-to-all-start.1) | async-done | bytes 524320 | tf_op jit(solution)/shard_map/all_to_all | solution.py:96
  27.6 4.5 all-to-all-start
  33.4 8.6 %all-to-all-done = bf16[4,16,16,256]{3,2,0,1:T(8,128)(2,1)S(1)} async-done(((bf16[4,16,16,256]{3,2,0,1:T(8,128)(2,1)}), bf16[4,16,16,256]{3,2,0,1:T(8,128)(2,1)S(1)}, u32[]{:S(2)}, u32[]{:S(2)}) %all-to-all-start) | async-done | bytes 524320 | tf_op jit(solution)/shard_map/all_to_all | solution.py:98
  42.0 5.1 %all-to-all-start.2 = ((bf16[4,16,16,256]{3,2,0,1:T(8,128)(2,1)}), bf16[4,16,16,256]{3,2,0,1:T(8,128)(2,1)}, u32[]{:S(2)}, u32[]{:S(2)}) async-start(bf16[4,16,16,256]{3,2,0,1:T(8,128)(2,1)} %copy.96), calls=%async_computation.2 | async-start | bytes 1048576 | tf_op jit(solution)/shard_map/all_to_all | solution.py:97
  47.2 2.7 reshape_reshape.27
  49.8 3.0 copy.99
  55.5 3.0 copy.97
  58.4 2.6 reshape_reshape.29
  61.1 3.0 copy.98
  64.1 5.3 %fusion.78 = (f32[16,8,64]{2,1,0:T(8,128)S(1)}, f32[16,8,64,64]{2,3,1,0:T(8,128)}) fusion(bf16[64,16,8,32]{0,3,2,1:T(8,128)(2,1)} %copy.97, bf16[64,16,8,32]{0,3,2,1:T(8,128)(2,1)} %copy.98), kind=kOutput, calls=%fused_computation.100 | convolution fusion | flops 35127360 | bytes 3178496 | tf_op jit(solution)/shard_map/sub | solution.py:47
  70.0 2.9 convolution_convert_fusion.1
  74.5 5.8 %all-to-all-start.3 = ((bf16[64,1,16,256]{3,2,1,0:T(8,128)(2,1)}), bf16[64,1,16,256]{3,2,1,0:T(8,128)(2,1)S(1)}, u32[]{:S(2)}, u32[]{:S(2)}) async-start(bf16[64,1,16,256]{3,2,1,0:T(8,128)(2,1)} %copy.101), calls=%async_computation.3 | async-start | bytes 1048576 | tf_op jit(solution)/shard_map/all_to_all | solution.py:104
  82.4 7.8 %all-to-all-done.3 = bf16[64,1,16,256]{3,2,1,0:T(8,128)(2,1)S(1)} async-done(((bf16[64,1,16,256]{3,2,1,0:T(8,128)(2,1)}), bf16[64,1,16,256]{3,2,1,0:T(8,128)(2,1)S(1)}, u32[]{:S(2)}, u32[]{:S(2)}) %all-to-all-start.3) | async-done | bytes 524320 | tf_op jit(solution)/shard_map/all_to_all | solution.py:104
  91.6 2.9 fusion.8
  96.8 14.2 %all_to_all.120 = bf16[4,16,16,256]{3,2,0,1:T(8,128)(2,1)} all-to-all(bf16[4,16,16,256]{3,2,0,1:T(8,128)(2,1)S(1)} %copy.107), channel_id=1, replica_groups=mesh['member'=16,'space'=16] {'member'}, dimensions={1} | all-to-all | bytes 1048576 | tf_op jit(solution)/shard_map/all_to_all | solution.py:123
  110.9 3.5 reshape_reshape.31
  114.5 4.1 copy.108
  118.6 4.8 %convolution_convert_fusion = bf16[16,8,32,64]{3,2,1,0:T(8,128)(2,1)} fusion(bf16[64,16,8,32]{0,3,2,1:T(8,128)(2,1)} %copy.108, f32[16,8,64,64]{2,3,1,0:T(8,128)} %get-tuple-element.49, f32[16,8,64]{2,1,0:T(8,128)S(1)} %copy-done.26), kind=kOutput, calls=%fused_computation.34 | convolution fusion | flops 34865152 | bytes 3178496 | tf_op jit(solution)/shard_map/phmn,mphe->nphe/dot_general | solution.py:17
  123.3 2.7 copy.122
  126.1 5.1 %all-to-all-start.7 = ((bf16[64,1,16,256]{3,2,1,0:T(8,128)(2,1)}), bf16[64,1,16,256]{3,2,1,0:T(8,128)(2,1)}, u32[]{:S(2)}, u32[]{:S(2)}) async-start(bf16[64,1,16,256]{3,2,1,0:T(8,128)(2,1)} %copy.122), calls=%async_computation.7 | async-start | bytes 1048576 | tf_op jit(solution)/shard_map/all_to_all | solution.py:132
  131.2 4.3 fusion.79
  135.5 8.5 %fusion.29 = bf16[16,8,32,64]{3,2,1,0:T(8,128)(2,1)} fusion(bf16[64,16,8,32]{0,3,2,1:T(8,128)(2,1)} %copy.98, f32[16,8,64,64]{2,3,1,0:T(8,128)} %fusion.79, f32[16,8,64,64]{2,3,1,0:T(8,128)} %get-tuple-element.49, f32[16,8,64]{2,1,0:T(8,128)S(1)} %copy-done.26), kind=kOutput, calls=%fused_computation.32 | convolution fusion | flops 37494848 | bytes 5275648 | tf_op jit(solution)/shard_map/phmn,nphe->mphe/dot_general | solution.py:17
  144.0 2.7 copy.112
  146.7 5.8 %all-to-all-start.5 = ((bf16[64,1,16,256]{3,2,1,0:T(8,128)(2,1)}), bf16[64,1,16,256]{3,2,1,0:T(8,128)(2,1)}, u32[]{:S(2)}, u32[]{:S(2)}) async-start(bf16[64,1,16,256]{3,2,1,0:T(8,128)(2,1)} %copy.112), calls=%async_computation.5 | async-start | bytes 1048576 | tf_op jit(solution)/shard_map/all_to_all | solution.py:130
  152.5 4.8 %fusion.35 = f32[1024,256]{1,0:T(8,128)} fusion(bf16[4,256,256]{2,1,0:T(8,128)(2,1)} %param.11, f32[4,256,1024]{2,1,0:T(8,128)} %copy-done.2), kind=kOutput, calls=%fused_computation.36 | convolution fusion | flops 546308096 | bytes 5767168 | tf_op jit(solution)/shard_map/mpf,mpd->fd/dot_general | solution.py:17
  157.3 8.5 %fusion.32 = bf16[16,8,32,64]{3,2,1,0:T(8,128)(2,1)} fusion(bf16[64,16,8,32]{0,3,2,1:T(8,128)(2,1)} %copy.97, f32[16,8,64,64]{2,3,1,0:T(8,128)} %fusion.79, f32[16,8,64,64]{2,3,1,0:T(8,128)} %get-tuple-element.49, f32[16,8,64]{2,1,0:T(8,128)S(1)} %copy-done.26), kind=kOutput, calls=%fused_computation.33 | convolution fusion | flops 37494848 | bytes 5275648 | tf_op jit(solution)/shard_map/phmn,mphe->nphe/dot_general | solution.py:17
  165.8 2.7 copy.116
  168.5 5.7 %all-to-all-start.6 = ((bf16[64,1,16,256]{3,2,1,0:T(8,128)(2,1)}), bf16[64,1,16,256]{3,2,1,0:T(8,128)(2,1)}, u32[]{:S(2)}, u32[]{:S(2)}) async-start(bf16[64,1,16,256]{3,2,1,0:T(8,128)(2,1)} %copy.116), calls=%async_computation.6 | async-start | bytes 1048576 | tf_op jit(solution)/shard_map/all_to_all | solution.py:131
  176.4 3.3 convolution_bitcast_fusion
  193.2 80.0 %all-reduce = (f32[256]{0:T(256)S(1)}, f32[256]{0:T(256)S(1)}) all-reduce(f32[256]{0:T(256)S(1)} %get-tuple-element.38, f32[256]{0:T(256)S(1)} %copy-done.23), channel_id=1, replica_groups=mesh['member'=16,'space'=16] {'member','space'}, use_global_device_ids=true, to_apply=%region_14.0 | all-reduce | flops 512 | bytes 4096 | tf_op jit(solution)/shard_map/psum | solution.py:147
  273.8 182.4 %all-reduce.4.cloned.1.call-done = (f32[256,256]{1,0:T(8,128)}, f32[256,256]{1,0:T(8,128)}, f32[256,256]{1,0:T(8,128)}, f32[256,256]{1,0:T(8,128)}, f32[256,1024]{1,0:T(8,128)}, /*index=5*/f32[1024,256]{1,0:T(8,128)}) async-done(((f32[256,256]{1,0:T(8,128)}, f32[256,256]{1,0:T(8,128)}, f32[256,256]{1,0:T(8,128)}, f32[256,256]{1,0:T(8,128)}, f32[256,1024]{1,0:T(8,128)}, /*index=5*/f32[1024,256]{1,0:T(8,128)}), ...) | async-done | bytes 3145744 | tf_op jit(solution)/shard_map/psum | solution.py:147
  (99 shorter events, 39.2 us)
Async XLA Ops:
  7.2 83.4 %copy-start = (bf16[256,1024]{1,0:T(8,128)(2,1)S(1)}, bf16[256,1024]{1,0:T(8,128)(2,1)}, u32[]{:S(2)}) copy-start(bf16[256,1024]{1,0:T(8,128)(2,1)} %param.18) | copy-start | bytes 1572868
  7.2 10.6 %copy-start.22 = (f32[256]{0:T(256)S(1)}, f32[256]{0:T(256)}, u32[]{:S(2)}) copy-start(f32[256]{0:T(256)} %param.12) | copy-start | bytes 3076
  7.2 10.6 %copy-start.18 = (bf16[256,256]{1,0:T(8,128)(2,1)S(1)}, bf16[256,256]{1,0:T(8,128)(2,1)}, u32[]{:S(2)}) copy-start(bf16[256,256]{1,0:T(8,128)(2,1)} %param.15) | copy-start | bytes 393220
  8.5 23.6 %copy-start.20 = (bf16[256,256]{1,0:T(8,128)(2,1)S(1)}, bf16[256,256]{1,0:T(8,128)(2,1)}, u32[]{:S(2)}) copy-start(bf16[256,256]{1,0:T(8,128)(2,1)} %param.14) | copy-start | bytes 393220
  10.9 16.7 %all-to-all-start.1 = ((bf16[4,16,16,256]{3,2,0,1:T(8,128)(2,1)}), bf16[4,16,16,256]{3,2,0,1:T(8,128)(2,1)S(1)}, u32[]{:S(2)}, u32[]{:S(2)}) async-start(bf16[4,16,16,256]{3,2,0,1:T(8,128)(2,1)} %copy.94), calls=%async_computation.1 | async-start | bytes 1048576 | tf_op jit(solution)/shard_map/all_to_all | solution.py:96
  27.6 19.6 %copy-start.5 = (bf16[4,16,16,256]{3,2,0,1:T(8,128)(2,1)}, bf16[4,16,16,256]{3,2,0,1:T(8,128)(2,1)S(1)}, u32[]{:S(2)}) copy-start(bf16[4,16,16,256]{3,2,0,1:T(8,128)(2,1)S(1)} %all-to-all-done.1) | copy-start | bytes 1572868
  27.6 14.4 %all-to-all-start = ((bf16[4,16,16,256]{3,2,0,1:T(8,128)(2,1)}), bf16[4,16,16,256]{3,2,0,1:T(8,128)(2,1)S(1)}, u32[]{:S(2)}, u32[]{:S(2)}) async-start(bf16[4,16,16,256]{3,2,0,1:T(8,128)(2,1)} %copy.92), calls=%async_computation | async-start | bytes 1048576 | tf_op jit(solution)/shard_map/all_to_all | solution.py:98
  42.0 5.2 %copy-start.6 = (bf16[4,16,16,256]{3,2,0,1:T(8,128)(2,1)}, bf16[4,16,16,256]{3,2,0,1:T(8,128)(2,1)S(1)}, u32[]{:S(2)}) copy-start(bf16[4,16,16,256]{3,2,0,1:T(8,128)(2,1)S(1)} %all-to-all-done) | copy-start | bytes 1572868
  42.0 16.4 %all-to-all-start.2 = ((bf16[4,16,16,256]{3,2,0,1:T(8,128)(2,1)}), bf16[4,16,16,256]{3,2,0,1:T(8,128)(2,1)}, u32[]{:S(2)}, u32[]{:S(2)}) async-start(bf16[4,16,16,256]{3,2,0,1:T(8,128)(2,1)} %copy.96), calls=%async_computation.2 | async-start | bytes 1048576 | tf_op jit(solution)/shard_map/all_to_all | solution.py:97
  64.1 6.0 %copy-start.3 = (bf16[64,16,8,32]{0,3,2,1:T(8,128)(2,1)S(1)}, bf16[64,16,8,32]{0,3,2,1:T(8,128)(2,1)}, u32[]{:S(2)}) copy-start(bf16[64,16,8,32]{0,3,2,1:T(8,128)(2,1)} %copy.99) | copy-start | bytes 1572868
  72.9 17.3 %copy-start.13 = (bf16[256,256]{1,0:T(8,128)(2,1)S(1)}, bf16[256,256]{1,0:T(8,128)(2,1)}, u32[]{:S(2)}) copy-start(bf16[256,256]{1,0:T(8,128)(2,1)} %param.16) | copy-start | bytes 393220
  72.9 17.7 %copy-start.21 = (f32[256]{0:T(256)S(1)}, f32[256]{0:T(256)}, u32[]{:S(2)}) copy-start(f32[256]{0:T(256)} %param.17) | copy-start | bytes 3076
  74.5 15.6 %all-to-all-start.3 = ((bf16[64,1,16,256]{3,2,1,0:T(8,128)(2,1)}), bf16[64,1,16,256]{3,2,1,0:T(8,128)(2,1)S(1)}, u32[]{:S(2)}, u32[]{:S(2)}) async-start(bf16[64,1,16,256]{3,2,1,0:T(8,128)(2,1)} %copy.101), calls=%async_computation.3 | async-start | bytes 1048576 | tf_op jit(solution)/shard_map/all_to_all | solution.py:104
  90.2 4.3 copy-start.1
  90.2 1.4 copy-start.24
  91.6 2.9 copy-start.2
  94.5 1.9 copy-start.4
  94.5 1.5 copy-start.10
  96.7 21.8 %copy-start.26 = (f32[16,8,64]{2,1,0:T(8,128)S(1)}, f32[16,8,64]{2,1,0:T(8,128)}, u32[]{:S(2)}) copy-start(f32[16,8,64]{2,1,0:T(8,128)} %copy-done.25) | copy-start | bytes 98308
  126.1 20.6 %all-to-all-start.7 = ((bf16[64,1,16,256]{3,2,1,0:T(8,128)(2,1)}), bf16[64,1,16,256]{3,2,1,0:T(8,128)(2,1)}, u32[]{:S(2)}, u32[]{:S(2)}) async-start(bf16[64,1,16,256]{3,2,1,0:T(8,128)(2,1)} %copy.122), calls=%async_computation.7 | async-start | bytes 1048576 | tf_op jit(solution)/shard_map/all_to_all | solution.py:132
  146.7 21.8 %all-to-all-start.5 = ((bf16[64,1,16,256]{3,2,1,0:T(8,128)(2,1)}), bf16[64,1,16,256]{3,2,1,0:T(8,128)(2,1)}, u32[]{:S(2)}, u32[]{:S(2)}) async-start(bf16[64,1,16,256]{3,2,1,0:T(8,128)(2,1)} %copy.112), calls=%async_computation.5 | async-start | bytes 1048576 | tf_op jit(solution)/shard_map/all_to_all | solution.py:130
  168.5 15.6 %all-to-all-start.6 = ((bf16[64,1,16,256]{3,2,1,0:T(8,128)(2,1)}), bf16[64,1,16,256]{3,2,1,0:T(8,128)(2,1)}, u32[]{:S(2)}, u32[]{:S(2)}) async-start(bf16[64,1,16,256]{3,2,1,0:T(8,128)(2,1)} %copy.116), calls=%async_computation.6 | async-start | bytes 1048576 | tf_op jit(solution)/shard_map/all_to_all | solution.py:131
  174.3 281.9 %all-reduce.4.cloned.1.call-start = ((), (), s32[]{:S(2)}) async-start(), calls=%async_computation.8 | async-start | bytes 6291456 | tf_op jit(solution)/shard_map/psum | solution.py:147
  180.8 7.3 %copy-start.8 = (bf16[4,16,1,16,256]{4,3,1,0,2:T(8,128)(2,1)}, bf16[4,16,1,16,256]{4,3,1,0,2:T(8,128)(2,1)S(1)}, u32[]{:S(2)}) copy-start(bf16[4,16,1,16,256]{4,3,1,0,2:T(8,128)(2,1)S(1)} %copy.123) | copy-start | bytes 1572868
  182.1 6.1 %copy-start.7 = (bf16[4,16,1,16,256]{4,3,1,0,2:T(8,128)(2,1)}, bf16[4,16,1,16,256]{4,3,1,0,2:T(8,128)(2,1)S(1)}, u32[]{:S(2)}) copy-start(bf16[4,16,1,16,256]{4,3,1,0,2:T(8,128)(2,1)S(1)} %copy.113) | copy-start | bytes 1572868
  182.1 6.1 %copy-start.19 = (bf16[256,256]{1,0:T(8,128)(2,1)S(1)}, bf16[256,256]{1,0:T(8,128)(2,1)}, u32[]{:S(2)}) copy-start(bf16[256,256]{1,0:T(8,128)(2,1)} %param.13) | copy-start | bytes 393220
  188.2 2.8 copy-start.9
  191.0 2.2 copy-start.23
  456.2 4.7 copy-start.16
  456.2 4.7 copy-start.17
  456.2 5.5 %copy-start.14 = (f32[256,256]{1,0:T(8,128)S(1)}, f32[256,256]{1,0:T(8,128)}, u32[]{:S(2)}) copy-start(f32[256,256]{1,0:T(8,128)} %get-tuple-element.44) | copy-start | bytes 786436
  456.2 5.5 %copy-start.15 = (f32[256,256]{1,0:T(8,128)S(1)}, f32[256,256]{1,0:T(8,128)}, u32[]{:S(2)}) copy-start(f32[256,256]{1,0:T(8,128)} %get-tuple-element.45) | copy-start | bytes 786436
  (3 other events, 2.7 us)
Sparse Core Ops, SparseCore 0:
  188.3 267.8 all-reduce.3
where the time goes:
time: 472 us; the launch traced here: 469 us
  waiting for transfers between devices  208 us (44%)
  blocking collectives  94.2 us (20%)
  matrix products  59.1 us (13%)
  local copies, waits for them, and re-layouts  46.7 us (10%)
  starting transfers between devices  39 us (8%)
  between operations  14.5 us (3%)
  other arithmetic  7.66 us (2%)
    psum x1, waiting for transfers between devices, on_device(): lax.psum((part_query, part_key, part_value, part_wout, part_up, part_down...  182 us
    psum x1, blocking collectives, on_device(): lax.psum((part_query, part_key, part_value, part_wout, part_up, part_down...  80 us
    dot_general x22, matrix products, multiply(): return jnp.einsum(form, left, right, preferred_element_type=jnp.float32)  53.8 us
    all_to_all x1, blocking collectives, on_device(): lax.all_to_all(patchwise(grad_mixed), 'member', split_axis=1, concat_axis...  14.2 us
    another operation x4, local copies, waits for them, and re-layouts, memberwise(): return array.reshape(everyone, 1, spread, array.shape[-1])  9.82 us
  transfers between devices with their start and end apart: 8, of which 5 were waited for; matrix products, arithmetic and copies ran while one was open for 13% of the time, Pallas kernels for 0%

commit v1 on v0

--- a/solution.py
+++ b/solution.py
@@ -71,39 +71,17 @@
     )
 
 
-def on_device(
+def layer(
     layer_input, out_grad, norm1_gain, w_query, w_key, w_value, w_out, norm2_gain, w_up, w_down
 ):
-    groups = lax.axis_size("member")
-    own_members, own_patches, width = layer_input.shape
-    spread = own_patches // groups
-    everyone = own_members * groups
-    heads = width // HEAD_DIM
-
-    def patchwise(array):
-        return array.reshape(own_members, groups, spread, array.shape[-1])
-
-    def memberwise(array):
-        return array.reshape(everyone, 1, spread, array.shape[-1])
-
+    heads = layer_input.shape[-1] // HEAD_DIM
     wide = layer_input.astype(jnp.float32)
     unit1, inverse1 = norm_rows(wide)
     normed1 = (unit1 * norm1_gain).astype(jnp.bfloat16)
     query = multiply("mpd,de->mpe", normed1, w_query).astype(jnp.bfloat16)
     keys = multiply("mpd,de->mpe", normed1, w_key).astype(jnp.bfloat16)
     values = multiply("mpd,de->mpe", normed1, w_value).astype(jnp.bfloat16)
-    moved = (
-        lax.all_to_all(patchwise(query), "member", split_axis=1, concat_axis=0, tiled=True),
-        lax.all_to_all(patchwise(keys), "member", split_axis=1, concat_axis=0, tiled=True),
-        lax.all_to_all(patchwise(values), "member", split_axis=1, concat_axis=0, tiled=True),
-    )
-    query_here = moved[0].reshape(everyone, spread, width)
-    keys_here = moved[1].reshape(everyone, spread, width)
-    values_here = moved[2].reshape(everyone, spread, width)
-    weights, rounded, mixed_here = attend(query_here, keys_here, values_here, heads)
-    mixed = lax.all_to_all(
-        memberwise(mixed_here), "member", split_axis=0, concat_axis=1, tiled=True
-    ).reshape(own_members, own_patches, width)
+    weights, rounded, mixed = attend(query, keys, values, heads)
     hidden_state = wide + multiply("mpd,de->mpe", mixed, w_out)
     unit2, inverse2 = norm_rows(hidden_state)
     normed2 = (unit2 * norm2_gain).astype(jnp.bfloat16)
@@ -120,20 +98,7 @@
     grad_attn = grad_hidden.astype(jnp.bfloat16)
     part_wout = multiply("mpd,mpe->de", mixed, grad_attn)
     grad_mixed = multiply("mpe,de->mpd", grad_attn, w_out).astype(jnp.bfloat16)
-    grad_mixed_here = lax.all_to_all(
-        patchwise(grad_mixed), "member", split_axis=1, concat_axis=0, tiled=True
-    ).reshape(everyone, spread, width)
-    grad_q, grad_k, grad_v = attend_back(
-        query_here, keys_here, values_here, weights, rounded, grad_mixed_here, heads
-    )
-    moved_back = (
-        lax.all_to_all(memberwise(grad_q), "member", split_axis=0, concat_axis=1, tiled=True),
-        lax.all_to_all(memberwise(grad_k), "member", split_axis=0, concat_axis=1, tiled=True),
-        lax.all_to_all(memberwise(grad_v), "member", split_axis=0, concat_axis=1, tiled=True),
-    )
-    grad_q = moved_back[0].reshape(own_members, own_patches, width)
-    grad_k = moved_back[1].reshape(own_members, own_patches, width)
-    grad_v = moved_back[2].reshape(own_members, own_patches, width)
+    grad_q, grad_k, grad_v = attend_back(query, keys, values, weights, rounded, grad_mixed, heads)
     part_query = multiply("mpd,mpe->de", normed1, grad_q)
     part_key = multiply("mpd,mpe->de", normed1, grad_k)
     part_value = multiply("mpd,mpe->de", normed1, grad_v)
@@ -143,22 +108,117 @@
         + multiply("mpe,de->mpd", grad_v, w_value)
     )
     back_one, part_gain1 = norm_back(unit1, inverse1, norm1_gain, grad_normed1)
-    input_grad = grad_hidden + back_one
-    totals = lax.psum(
-        (part_query, part_key, part_value, part_wout, part_up, part_down, part_gain1, part_gain2),
-        ("member", "space"),
-    )
+    moved = (back_two + back_one).astype(jnp.bfloat16)
+    up_blocks = part_up.reshape(256, 4, 256).transpose(1, 0, 2).reshape(1024, 256)
+    weights_all = jnp.concatenate(
+        [part_query, part_key, part_value, part_wout, up_blocks, part_down], axis=0
+    ).astype(jnp.bfloat16)
+    gains = jnp.stack([part_gain1, part_gain2])
+    return moved, weights_all, gains
+
+
+def two_parts(values):
+    high = values.astype(jnp.bfloat16)
+    low = (values - high.astype(jnp.float32)).astype(jnp.bfloat16)
+    return jnp.concatenate([high, low], axis=0)
+
+
+def swap(array, axis, groups=None):
+    return lax.all_to_all(
+        array, axis, split_axis=0, concat_axis=0, tiled=True, axis_index_groups=groups
+    )
+
+
+def add_everywhere(weights_all, gains):
+    f32, b16 = jnp.float32, jnp.bfloat16
+    members = lax.axis_size("member")
+    spaces = lax.axis_size("space")
+    chips = members // 2
+    core = lax.axis_index("member") % 2
+    other_core = [(k, k ^ 1) for k in range(members)]
+    same_core = [[c + 2 * k for k in range(chips)] for c in range(2)]
+    rows = weights_all.shape[0]
+
+    def gain_rows(values):
+        return jnp.concatenate([two_parts(values), jnp.zeros((4, 256), b16)], axis=0)
+
+    halves = weights_all.reshape(2, rows // 2, 256)
+    keep = lax.dynamic_index_in_dim(halves, core, 0, keepdims=False)
+    give = lax.dynamic_index_in_dim(halves, 1 - core, 0, keepdims=False)
+    sent = jnp.concatenate([give, gain_rows(gains)], axis=0)
+    got = lax.ppermute(sent, "member", other_core)
+    total = keep.astype(f32) + got[: rows // 2].astype(f32)
+    gains = gains + got[rows // 2 : rows // 2 + 2].astype(f32) + got[rows // 2 + 2 : rows // 2 + 4].astype(f32)
+
+    each = rows // 2 // chips
+    sent = jnp.concatenate(
+        [
+            total.astype(b16).reshape(chips, each, 256),
+            jnp.broadcast_to(gain_rows(gains), (chips, 8, 256)),
+        ],
+        axis=1,
+    )
+    got = swap(sent, "member", same_core).astype(f32).sum(axis=0)
+    total = got[:each]
+    gains = got[each : each + 2] + got[each + 2 : each + 4]
+
+    small = each * 2 // spaces
+    sent = jnp.concatenate(
+        [
+            total.astype(b16).reshape(spaces, small, 128),
+            jnp.broadcast_to(two_parts(gains.reshape(4, 128)), (spaces, 8, 128)),
+        ],
+        axis=1,
+    )
+    got = swap(sent, "space").astype(f32).sum(axis=0)
+    total = got[:small].astype(b16)
+    gains = (got[small : small + 4] + got[small + 4 : small + 8]).reshape(2, 256)
+
+    everywhere = swap(jnp.broadcast_to(total, (spaces, small, 128)), "space")
+    everywhere = everywhere.reshape(each, 256)
+    everywhere = swap(jnp.broadcast_to(everywhere, (chips, each, 256)), "member", same_core)
+    mine = everywhere.reshape(rows // 2, 256)
+    theirs = lax.ppermute(mine, "member", other_core)
+    first = jnp.where(core == 0, mine, theirs)
+    second = jnp.where(core == 0, theirs, mine)
+    return jnp.concatenate([first, second], axis=0).astype(f32), gains
+
+
+def on_device(
+    layer_input, out_grad, norm1_gain, w_query, w_key, w_value, w_out, norm2_gain, w_up, w_down
+):
+    groups = lax.axis_size("member")
+    own_members, own_patches, width = layer_input.shape
+    spread = own_patches // groups
+    everyone = own_members * groups
+
+    def patchwise(array):
+        return array.reshape(own_members, groups, spread, width).transpose(1, 0, 2, 3)
+
+    both = jnp.concatenate([patchwise(layer_input), patchwise(out_grad)], axis=1)
+    both = swap(both, "member")
+    inputs_here = both[:, :own_members].reshape(everyone, spread, width)
+    out_grad_here = both[:, own_members:].reshape(everyone, spread, width)
+    moved, weights_all, gains = layer(
+        inputs_here, out_grad_here, norm1_gain, w_query, w_key, w_value, w_out, norm2_gain, w_up, w_down
+    )
+    home = swap(moved.reshape(groups, own_members, spread, width), "member")
+    home = home.transpose(1, 0, 2, 3).reshape(own_members, own_patches, width)
+    input_grad = out_grad.astype(jnp.float32) + home.astype(jnp.float32)
+    totals, gains = add_everywhere(weights_all, gains)
     scale = 1.0 / math.sqrt(everyone * own_patches * lax.axis_size("space"))
+    totals = totals * scale
+    gains = gains * scale
     return (
         input_grad,
-        totals[0] * scale,
-        totals[1] * scale,
-        totals[2] * scale,
-        totals[3] * scale,
-        totals[4] * scale,
-        totals[5] * scale,
-        totals[6] * scale,
-        totals[7] * scale,
+        totals[0:256],
+        totals[256:512],
+        totals[512:768],
+        totals[768:1024],
+        totals[1024:2048].reshape(4, 256, 256).transpose(1, 0, 2).reshape(256, 1024),
+        totals[2048:3072],
+        gains[0],
+        gains[1],
     )
 
 

time: 472 us -> 196 us (0.42)
  waiting for transfers between devices: 208 us -> 34 us
  blocking collectives: 94.2 us -> 46.7 us
  starting transfers between devices: 39 us -> 20.4 us
  local copies, waits for them, and re-layouts: 46.7 us -> 29.5 us
  between operations: 14.5 us -> 1.29 us
  matrix products: 59.1 us -> 51.7 us
    psum x1 -> x0, waiting for transfers between devices: 182 us -> none  [on_device(): lax.psum((part_query, part_key, part_value, part_wout, part_up, part_down...]
    psum x1 -> x0, blocking collectives: 80 us -> none  [on_device(): lax.psum((part_query, part_key, part_value, part_wout, part_up, part_down...]
    another operation x12 -> x1, local copies, waits for them, and re-layouts: 34.3 us -> 0.01 us  [the longest x4 9.82 us: memberwise(): return array.reshape(everyone, 1, spread, array.shape[-1])]
    all_to_all x1 -> x3, blocking collectives: 14.2 us -> 46.7 us  [swap(): lax.all_to_all(array, axis, split_axis=0, concat_axis=0, tiled=True, axis...]
    all_to_all x7 -> x3, starting transfers between devices: 39 us -> 19.1 us  [swap(): lax.all_to_all(array, axis, split_axis=0, concat_axis=0, tiled=True, axis...]
    reshape x4 -> x9, local copies, waits for them, and re-layouts: 2.6 us -> 10.9 us  [the longest x1 2.77 us: attend_back(): grad_v.reshape(members, count, width)]
    dot_general x22, matrix products: 53.8 us -> 46.5 us  [multiply(): return jnp.einsum(form, left, right, preferred_element_type=jnp.float32)]
    convert_element_type x0 -> x5, local copies, waits for them, and re-layouts: none -> 6.42 us  [the longest x1 1.69 us: layer(): values = multiply('mpd,de->mpe', normed1, w_value).astype(jnp.bfloat16)]
  transfers between devices with their start and end apart: 8 -> 5, of which waited for: 5 -> 4; matrix products, arithmetic and copies ran while one was open for 13% -> 2% of each run, Pallas kernels for 0% -> 0%
where the time goes in v1:
time: 196 us; the launch traced here: 195 us
  matrix products  51.7 us (26%)
  blocking collectives  46.7 us (24%)
  waiting for transfers between devices  34 us (17%)
  local copies, waits for them, and re-layouts  29.5 us (15%)
  starting transfers between devices  20.4 us (10%)
  other arithmetic  11.8 us (6%)
    all_to_all x3, blocking collectives, swap(): lax.all_to_all(array, axis, split_axis=0, concat_axis=0, tiled=True, axis...  46.7 us
    dot_general x22, matrix products, multiply(): return jnp.einsum(form, left, right, preferred_element_type=jnp.float32)  46.5 us
    all_to_all x3, waiting for transfers between devices, swap(): lax.all_to_all(array, axis, split_axis=0, concat_axis=0, tiled=True, axis...  31.8 us
    all_to_all x3, starting transfers between devices, swap(): lax.all_to_all(array, axis, split_axis=0, concat_axis=0, tiled=True, axis...  19.1 us
    sub x1, matrix products, attend(): scores = scores - jnp.max(scores, axis=-1, keepdims=True)  5.26 us
    unnamed x63, local copies, waits for them, and re-layouts  4.26 us
  transfers between devices with their start and end apart: 5, of which 4 were waited for; matrix products, arithmetic and copies ran while one was open for 2% of the time, Pallas kernels for 0%

profile of v1, /device:TPU:1, one launch (start us, length us, event | category | flops | bytes accessed | tf_op | source)
XLA Modules:
  0.0 195.3 jit_solution(18357645249608623680)
XLA Ops:
  3.2 7.0 %all-to-all-start = ((bf16[16,8,16,256]{3,2,1,0:T(8,128)(2,1)}), bf16[16,8,16,256]{3,2,1,0:T(8,128)(2,1)S(1)}, u32[]{:S(2)}, u32[]{:S(2)}) async-start(bf16[16,8,16,256]{3,2,1,0:T(8,128)(2,1)} %pad_maximum_fusion), calls=%async_computation | async-start | bytes 2097152 | tf_op jit(solution)/shard_map/all_to_all | solution.py:127
  10.2 15.8 %all-to-all-done = bf16[16,8,16,256]{3,2,1,0:T(8,128)(2,1)S(1)} async-done(((bf16[16,8,16,256]{3,2,1,0:T(8,128)(2,1)}), bf16[16,8,16,256]{3,2,1,0:T(8,128)(2,1)S(1)}, u32[]{:S(2)}, u32[]{:S(2)}) %all-to-all-start) | async-done | bytes 1048608 | tf_op jit(solution)/shard_map/all_to_all | solution.py:127
  27.8 1.5 copy.81
  30.7 1.7 copy.79
  32.4 1.5 copy.80
  34.0 5.3 %fusion.80 = (f32[16,8,64]{2,1,0:T(8,128)S(1)}, f32[16,8,64,64]{2,3,1,0:T(8,128)}) fusion(bf16[64,16,8,32]{0,3,2,1:T(8,128)(2,1)} %bitcast.175, bf16[64,16,8,32]{0,3,2,1:T(8,128)(2,1)} %bitcast.173), kind=kOutput, calls=%fused_computation.135 | convolution fusion | flops 35127360 | bytes 3178496 | tf_op jit(solution)/shard_map/sub | solution.py:47
  39.9 3.8 %convolution_convert_fusion.1 = bf16[16,8,32,64]{3,2,1,0:T(8,128)(2,1)} fusion(bf16[64,16,8,32]{0,3,2,1:T(8,128)(2,1)S(1)} %bitcast.157, f32[16,8,64,64]{2,3,1,0:T(8,128)} %get-tuple-element.32, f32[16,8,64]{2,1,0:T(8,128)S(1)} %get-tuple-element.31), kind=kOutput, calls=%fused_computation.32 | convolution fusion | flops 34865152 | bytes 3178496 | tf_op jit(solution)/shard_map/phmn,nphe->mphe/dot_general | solution.py:17
  43.7 2.0 %copy.83 = bf16[64,16,256]{2,1,0:T(8,128)(2,1)S(1)} copy(bf16[64,16,256]{0,2,1:T(8,128)(2,1)} %bitcast.171) | data formatting | bytes 1048576 | tf_op jit(solution)/shard_map/reshape | solution.py:52
  47.1 3.1 %fusion.8 = bf16[64,16,1024]{2,1,0:T(8,128)(2,1)S(1)} fusion(f32[64,16,1024]{2,1,0:T(8,128)S(1)} %fusion.48, bf16[64,16,256]{2,1,0:T(8,128)(2,1)S(1)} %bitcast.165, bf16[1024,256]{1,0:T(8,128)(2,1)S(1)} %copy-done.28), kind=kOutput, calls=%fused_computation.10 | convolution fusion | flops 556793856 | bytes 7340032 | tf_op jit(solution)/shard_map/mpd,fd->mpf/dot_general | solution.py:17
  54.5 1.6 copy.84
  56.1 4.8 %convolution_convert_fusion = bf16[16,8,32,64]{3,2,1,0:T(8,128)(2,1)} fusion(bf16[64,16,8,32]{0,3,2,1:T(8,128)(2,1)} %bitcast.159, f32[16,8,64,64]{2,3,1,0:T(8,128)} %get-tuple-element.32, f32[16,8,64]{2,1,0:T(8,128)} %copy-done.29), kind=kOutput, calls=%fused_computation.31 | convolution fusion | flops 34865152 | bytes 3178496 | tf_op jit(solution)/shard_map/phmn,mphe->nphe/dot_general | solution.py:17
  60.9 2.7 %fusion.81 = f32[16,8,64,64]{2,3,1,0:T(8,128)} fusion(bf16[64,16,8,32]{0,3,2,1:T(8,128)(2,1)S(1)} %bitcast.160, bf16[64,16,8,32]{0,3,2,1:T(8,128)(2,1)S(1)} %bitcast.158), kind=kOutput, calls=%fused_computation.136 | convolution fusion | flops 33554432 | bytes 3145728 | tf_op jit(solution)/shard_map/mphe,nphe->phmn/dot_general | solution.py:17
  63.7 8.7 %fusion.26 = bf16[16,8,32,64]{3,2,1,0:T(8,128)(2,1)} fusion(bf16[64,16,8,32]{0,3,2,1:T(8,128)(2,1)} %bitcast.174, f32[16,8,64,64]{2,3,1,0:T(8,128)} %fusion.81, f32[16,8,64,64]{2,3,1,0:T(8,128)} %get-tuple-element.32, f32[16,8,64]{2,1,0:T(8,128)S(1)} %copy-done.30), kind=kOutput, calls=%fused_computation.29 | convolution fusion | flops 37494848 | bytes 5275648 | tf_op jit(solution)/shard_map/phmn,nphe->mphe/dot_general | solution.py:17
  72.3 8.7 %fusion.29 = bf16[16,8,32,64]{3,2,1,0:T(8,128)(2,1)} fusion(bf16[64,16,8,32]{0,3,2,1:T(8,128)(2,1)} %bitcast.176, f32[16,8,64,64]{2,3,1,0:T(8,128)} %fusion.81, f32[16,8,64,64]{2,3,1,0:T(8,128)} %get-tuple-element.32, f32[16,8,64]{2,1,0:T(8,128)S(1)} %copy-done.30), kind=kOutput, calls=%fused_computation.30 | convolution fusion | flops 37494848 | bytes 5275648 | tf_op jit(solution)/shard_map/phmn,mphe->nphe/dot_general | solution.py:17
  81.0 2.8 %copy.90 = bf16[64,16,256]{2,1,0:T(8,128)(2,1)} copy(bf16[64,16,256]{0,2,1:T(8,128)(2,1)} %bitcast.177) | data formatting | bytes 1048576 | tf_op jit(solution)/shard_map/reshape | solution.py:70
  83.8 1.9 copy.86
  85.7 2.7 %copy.88 = bf16[64,16,256]{2,1,0:T(8,128)(2,1)} copy(bf16[64,16,256]{0,2,1:T(8,128)(2,1)} %bitcast.181) | data formatting | bytes 1048576 | tf_op jit(solution)/shard_map/reshape | solution.py:69
  88.8 1.4 convolution_add_fusion.1
  90.2 2.6 %multiply_reduce_fusion.3 = (f32[256]{0:T(256)S(1)}, f32[64,16]{1,0:T(8,128)S(1)}, f32[64,16,256]{2,1,0:T(8,128)}) fusion(f32[64,16]{1,0:T(8,128)S(1)} %bitcast.185, bf16[16,8,16,256]{3,2,1,0:T(8,128)(2,1)S(1)} %all-to-all-done, f32[64,16,256]{2,1,0:T(8,128)} %get-tuple-element.25, f32[256]{0:T(256)S(1)} %copy-done.25, ...), kind=kOutput, calls=%fused_computation.62 | convolution fusion | flops 136313600 | bytes 4335616 | tf_op jit(solution)/shard_map/mpe,de->mpd/dot_general | solution.py:17
  94.2 1.9 fusion.43
  98.4 1.8 fusion.35
  101.4 2.7 %concatenate.27 = bf16[1544,256]{1,0:T(8,128)(2,1)} concatenate(bf16[1536,256]{1,0:T(8,128)(2,1)S(1)} %dynamic-slice_bitcast_fusion, bf16[2,256]{1,0:T(2,128)(2,1)S(1)} %copy-done.27, bf16[2,256]{1,0:T(2,128)(2,1)S(1)} %subtract_convert_fusion.2, bf16[4,256]{1,0:T(4,128)(2,1)S(1)} %broadcast.87), dimensions={0} | concatenate | bytes 1581056 | tf_op jit(solution)/shard_map/concatenate | solution.py:148
  105.0 2.3 %collective-permute-done = bf16[1544,256]{1,0:T(8,128)(2,1)} collective-permute-done((bf16[1544,256]{1,0:T(8,128)(2,1)}, bf16[1544,256]{1,0:T(8,128)(2,1)}, u32[]{:S(2)}, u32[]{:S(2)}) %collective-permute-start) | collective-permute-done | bytes 790560 | tf_op jit(solution)/shard_map/ppermute | solution.py:149
  108.1 1.6 fusion.25
  109.8 15.5 %all_to_all.30 = bf16[8,200,256]{2,1,0:T(8,128)(2,1)S(1)} all-to-all(bf16[8,200,256]{2,1,0:T(8,128)(2,1)S(1)} %pad_maximum_fusion.1), channel_id=1, replica_groups={{0,32,64,96,128,160,192,224},{16,48,80,112,144,176,208,240},{1,33,65,97..., dimensions={0} | all-to-all | bytes 1638400 | tf_op jit(solution)/shard_map/all_to_all | solution.py:127
  125.5 19.2 %all_to_all.31 = bf16[16,32,128]{2,1,0:T(8,128)(2,1)S(1)} all-to-all(bf16[16,32,128]{2,1,0:T(8,128)(2,1)S(1)} %pad_maximum_fusion.2), channel_id=1, replica_groups=mesh['member'=16,'space'=16] {'space'}, dimensions={0} | all-to-all | bytes 262144 | tf_op jit(solution)/shard_map/all_to_all | solution.py:127
  144.8 12.0 %all_to_all.32 = bf16[16,24,128]{2,1,0:T(8,128)(2,1)S(1)} all-to-all(bf16[16,24,128]{2,1,0:T(8,128)(2,1)S(1)} %broadcast_in_dim.10), channel_id=1, replica_groups=mesh['member'=16,'space'=16] {'space'}, dimensions={0} | all-to-all | bytes 196608 | tf_op jit(solution)/shard_map/all_to_all | solution.py:127
  157.7 3.5 %all-to-all-start.5 = ((bf16[8,192,256]{2,1,0:T(8,128)(2,1)}), bf16[8,192,256]{2,1,0:T(8,128)(2,1)S(1)}, u32[]{:S(2)}, u32[]{:S(2)}) async-start(bf16[8,192,256]{2,1,0:T(8,128)(2,1)} %broadcast_in_dim.11), calls=%async_computation.5 | async-start | bytes 1572864 | tf_op jit(solution)/shard_map/all_to_all | solution.py:127
  161.3 2.6 %add_convert_fusion = bf16[64,16,256]{2,1,0:T(8,128)(2,1)} fusion(f32[64,16,256]{2,1,0:T(8,128)} %get-tuple-element.36, f32[64,16]{1,0:T(8,128)S(1)} %broadcast_multiply_fusion, f32[256]{0:T(256)S(1)} %copy-done.26, f32[64,16]{1,0:T(8,128)S(1)} %bitcast.186, f32[64,16]{1,0:T(8,128)S(1)} %broadcast_multiply_fusion.1, ...), kind=kLoop, calls=%fused_computation.64 | loop fusion | flops 3407872 | bytes 4212736 | tf_op jit(solution)/shard_map/convert_element_type | solution.py:111
  163.9 6.4 %all-to-all-done.5 = bf16[8,192,256]{2,1,0:T(8,128)(2,1)S(1)} async-done(((bf16[8,192,256]{2,1,0:T(8,128)(2,1)}), bf16[8,192,256]{2,1,0:T(8,128)(2,1)S(1)}, u32[]{:S(2)}, u32[]{:S(2)}) %all-to-all-start.5) | async-done | bytes 786464 | tf_op jit(solution)/shard_map/all_to_all | solution.py:127
  170.3 8.6 %all-to-all-start.1 = ((bf16[16,4,16,256]{3,2,1,0:T(8,128)(2,1)}), bf16[16,4,16,256]{3,2,1,0:T(8,128)(2,1)S(1)}, u32[]{:S(2)}, u32[]{:S(2)}) async-start(bf16[16,4,16,256]{3,2,1,0:T(8,128)(2,1)} %bitcast.25), calls=%async_computation.1 | async-start | bytes 1048576 | tf_op jit(solution)/shard_map/all_to_all | solution.py:127
  179.2 9.6 %all-to-all-done.1 = bf16[16,4,16,256]{3,2,1,0:T(8,128)(2,1)S(1)} async-done(((bf16[16,4,16,256]{3,2,1,0:T(8,128)(2,1)}), bf16[16,4,16,256]{3,2,1,0:T(8,128)(2,1)S(1)}, u32[]{:S(2)}, u32[]{:S(2)}) %all-to-all-start.1) | async-done | bytes 524320 | tf_op jit(solution)/shard_map/all_to_all | solution.py:127
  (123 shorter events, 26.7 us)
Async XLA Ops:
  0.6 45.6 %copy-start = (bf16[256,1024]{1,0:T(8,128)(2,1)S(1)}, bf16[256,1024]{1,0:T(8,128)(2,1)}, u32[]{:S(2)}) copy-start(bf16[256,1024]{1,0:T(8,128)(2,1)} %param.18) | copy-start | bytes 1572868
  0.7 25.6 %copy-start.25 = (f32[256]{0:T(256)S(1)}, f32[256]{0:T(256)}, u32[]{:S(2)}) copy-start(f32[256]{0:T(256)} %param.12) | copy-start | bytes 3076
  0.7 26.8 %copy-start.22 = (bf16[256,256]{1,0:T(8,128)(2,1)S(1)}, bf16[256,256]{1,0:T(8,128)(2,1)}, u32[]{:S(2)}) copy-start(bf16[256,256]{1,0:T(8,128)(2,1)} %param.14) | copy-start | bytes 393220
  3.1 26.2 %copy-start.20 = (bf16[256,256]{1,0:T(8,128)(2,1)S(1)}, bf16[256,256]{1,0:T(8,128)(2,1)}, u32[]{:S(2)}) copy-start(bf16[256,256]{1,0:T(8,128)(2,1)} %param.13) | copy-start | bytes 393220
  3.1 26.5 %copy-start.19 = (bf16[256,256]{1,0:T(8,128)(2,1)S(1)}, bf16[256,256]{1,0:T(8,128)(2,1)}, u32[]{:S(2)}) copy-start(bf16[256,256]{1,0:T(8,128)(2,1)} %param.15) | copy-start | bytes 393220
  3.2 22.9 %all-to-all-start = ((bf16[16,8,16,256]{3,2,1,0:T(8,128)(2,1)}), bf16[16,8,16,256]{3,2,1,0:T(8,128)(2,1)S(1)}, u32[]{:S(2)}, u32[]{:S(2)}) async-start(bf16[16,8,16,256]{3,2,1,0:T(8,128)(2,1)} %pad_maximum_fusion), calls=%async_computation | async-start | bytes 2097152 | tf_op jit(solution)/shard_map/all_to_all | solution.py:127
  32.4 6.8 %copy-start.5 = (bf16[64,16,256]{0,2,1:T(8,128)(2,1)}, bf16[64,16,256]{0,2,1:T(8,128)(2,1)S(1)}, u32[]{:S(2)}) copy-start(bf16[64,16,256]{0,2,1:T(8,128)(2,1)S(1)} %copy.79) | copy-start | bytes 1572868
  43.7 2.2 %copy-start.18 = (bf16[256,256]{1,0:T(8,128)(2,1)S(1)}, bf16[256,256]{1,0:T(8,128)(2,1)}, u32[]{:S(2)}) copy-start(bf16[256,256]{1,0:T(8,128)(2,1)} %param.16) | copy-start | bytes 393220
  43.7 2.6 %copy-start.23 = (f32[256]{0:T(256)S(1)}, f32[256]{0:T(256)}, u32[]{:S(2)}) copy-start(f32[256]{0:T(256)} %param.17) | copy-start | bytes 3076
  45.8 6.1 %copy-start.9 = (bf16[16,4,16,256]{3,2,1,0:T(8,128)(2,1)}, bf16[16,4,16,256]{3,2,1,0:T(8,128)(2,1)S(1)}, u32[]{:S(2)}) copy-start(bf16[16,4,16,256]{3,2,1,0:T(8,128)(2,1)S(1)} %get-tuple-element.27) | copy-start | bytes 1572868
  45.9 1.2 copy-start.28
  47.0 3.2 %copy-start.2 = (f32[64,16,1024]{2,1,0:T(8,128)}, f32[64,16,1024]{2,1,0:T(8,128)S(1)}, u32[]{:S(2)}) copy-start(f32[64,16,1024]{2,1,0:T(8,128)S(1)} %fusion.48) | copy-start | bytes 12582916
  56.1 4.8 %copy-start.6 = (bf16[64,16,256]{0,2,1:T(8,128)(2,1)S(1)}, bf16[64,16,256]{0,2,1:T(8,128)(2,1)}, u32[]{:S(2)}) copy-start(bf16[64,16,256]{0,2,1:T(8,128)(2,1)} %copy-done.5) | copy-start | bytes 1572868
  56.1 4.8 %copy-start.7 = (bf16[64,16,256]{0,2,1:T(8,128)(2,1)S(1)}, bf16[64,16,256]{0,2,1:T(8,128)(2,1)}, u32[]{:S(2)}) copy-start(bf16[64,16,256]{0,2,1:T(8,128)(2,1)} %copy.84) | copy-start | bytes 1572868
  60.9 2.7 %copy-start.30 = (f32[16,8,64]{2,1,0:T(8,128)S(1)}, f32[16,8,64]{2,1,0:T(8,128)}, u32[]{:S(2)}) copy-start(f32[16,8,64]{2,1,0:T(8,128)} %copy-done.29) | copy-start | bytes 98308
  81.0 7.4 %copy-start.21 = (bf16[256,256]{1,0:T(8,128)(2,1)S(1)}, bf16[256,256]{1,0:T(8,128)(2,1)}, u32[]{:S(2)}) copy-start(bf16[256,256]{1,0:T(8,128)(2,1)} %param.13) | copy-start | bytes 393220
  88.5 1.7 copy-start.13
  93.8 2.2 %copy-start.17 = (bf16[16,8,32,64]{3,2,1,0:T(8,128)(2,1)S(1)}, bf16[16,8,32,64]{3,2,1,0:T(8,128)(2,1)}, u32[]{:S(2)}) copy-start(bf16[16,8,32,64]{3,2,1,0:T(8,128)(2,1)} %fusion.29) | copy-start | bytes 1572868
  93.8 2.8 %copy-start.16 = (bf16[16,8,32,64]{3,2,1,0:T(8,128)(2,1)S(1)}, bf16[16,8,32,64]{3,2,1,0:T(8,128)(2,1)}, u32[]{:S(2)}) copy-start(bf16[16,8,32,64]{3,2,1,0:T(8,128)(2,1)} %convolution_convert_fusion) | copy-start | bytes 1572868
  93.8 3.3 %copy-start.12 = (bf16[64,16,256]{2,1,0:T(8,128)(2,1)S(1)}, bf16[64,16,256]{2,1,0:T(8,128)(2,1)}, u32[]{:S(2)}) copy-start(bf16[64,16,256]{2,1,0:T(8,128)(2,1)} %copy-done.11) | copy-start | bytes 1572868
  93.8 3.3 %copy-start.15 = (bf16[16,8,32,64]{3,2,1,0:T(8,128)(2,1)S(1)}, bf16[16,8,32,64]{3,2,1,0:T(8,128)(2,1)}, u32[]{:S(2)}) copy-start(bf16[16,8,32,64]{3,2,1,0:T(8,128)(2,1)} %convolution_convert_fusion.1) | copy-start | bytes 1572868
  96.1 2.2 %copy-start.3 = (f32[64,16,1024]{2,1,0:T(8,128)S(1)}, f32[64,16,1024]{2,1,0:T(8,128)}, u32[]{:S(2)}) copy-start(f32[64,16,1024]{2,1,0:T(8,128)} %copy-done.2) | copy-start | bytes 12582916
  96.1 2.3 %copy-start.10 = (bf16[16,4,16,256]{3,2,1,0:T(8,128)(2,1)S(1)}, bf16[16,4,16,256]{3,2,1,0:T(8,128)(2,1)}, u32[]{:S(2)}) copy-start(bf16[16,4,16,256]{3,2,1,0:T(8,128)(2,1)} %copy-done.9) | copy-start | bytes 1572868
  98.4 3.1 %copy-start.27 = (bf16[2,256]{1,0:T(2,128)(2,1)S(1)}, bf16[2,256]{1,0:T(2,128)(2,1)}, u32[]{:S(2)}) copy-start(bf16[2,256]{1,0:T(2,128)(2,1)} %fusion.76) | copy-start | bytes 3076
  104.1 3.2 %collective-permute-start = (bf16[1544,256]{1,0:T(8,128)(2,1)}, bf16[1544,256]{1,0:T(8,128)(2,1)}, u32[]{:S(2)}, u32[]{:S(2)}) collective-permute-start(bf16[1544,256]{1,0:T(8,128)(2,1)} %concatenate.27), channel_id=1, source_target_pairs={{0,16},{16,0},{32,48},{48,32},{64,80},{80,64},{96,112},{112,96},{1... | collective-permute-start | bytes 2371592 | tf_op jit(solution)/shard_map/ppermute | solution.py:149
  109.7 51.6 %copy-start.24 = (f32[256]{0:T(256)S(1)}, f32[256]{0:T(256)}, u32[]{:S(2)}) copy-start(f32[256]{0:T(256)} %param.17) | copy-start | bytes 3076
  109.7 51.6 %copy-start.26 = (f32[256]{0:T(256)S(1)}, f32[256]{0:T(256)}, u32[]{:S(2)}) copy-start(f32[256]{0:T(256)} %param.12) | copy-start | bytes 3076
  157.7 12.6 %all-to-all-start.5 = ((bf16[8,192,256]{2,1,0:T(8,128)(2,1)}), bf16[8,192,256]{2,1,0:T(8,128)(2,1)S(1)}, u32[]{:S(2)}, u32[]{:S(2)}) async-start(bf16[8,192,256]{2,1,0:T(8,128)(2,1)} %broadcast_in_dim.11), calls=%async_computation.5 | async-start | bytes 1572864 | tf_op jit(solution)/shard_map/all_to_all | solution.py:127
  163.9 25.0 %copy-start.8 = (bf16[4,256,256]{2,1,0:T(8,128)(2,1)S(1)}, bf16[4,256,256]{2,1,0:T(8,128)(2,1)}, u32[]{:S(2)}) copy-start(bf16[4,256,256]{2,1,0:T(8,128)(2,1)} %param.11) | copy-start | bytes 1572868
  170.3 18.4 %all-to-all-start.1 = ((bf16[16,4,16,256]{3,2,1,0:T(8,128)(2,1)}), bf16[16,4,16,256]{3,2,1,0:T(8,128)(2,1)S(1)}, u32[]{:S(2)}, u32[]{:S(2)}) async-start(bf16[16,4,16,256]{3,2,1,0:T(8,128)(2,1)} %bitcast.25), calls=%async_computation.1 | async-start | bytes 1048576 | tf_op jit(solution)/shard_map/all_to_all | solution.py:127
  178.8 11.8 %collective-permute-start.1 = (bf16[1536,256]{1,0:T(8,128)(2,1)S(1)}, bf16[1536,256]{1,0:T(8,128)(2,1)}, u32[]{:S(2)}, u32[]{:S(2)}) collective-permute-start(bf16[1536,256]{1,0:T(8,128)(2,1)S(1)} %bitcast.163), channel_id=1, source_target_pairs={{0,16},{16,0},{32,48},{48,32},{64,80},{80,64},{96,112},{112,96},{1... | collective-permute-start | bytes 2359304 | tf_op jit(solution)/shard_map/ppermute | solution.py:181
  191.9 3.4 %copy-start.1 = (bf16[256,1024]{1,0:T(8,128)(2,1)S(1)}, bf16[256,1024]{1,0:T(8,128)(2,1)}, u32[]{:S(2)}) copy-start(bf16[256,1024]{1,0:T(8,128)(2,1)} %param.18) | copy-start | bytes 1572868
  (4 other events, 3.6 us)

commit v2 on v0

v2 whole, which is shorter than its diff:
```python
import functools
import math

import jax
import jax.numpy as jnp
from jax import lax
from jax.experimental import pallas as pl
from jax.experimental.pallas import tpu as pltpu
from jax.sharding import PartitionSpec as P

HEAD_DIM = 32
WIDTH = 256
HIDDEN = 1024
HEADS = WIDTH // HEAD_DIM
GROUPS = 16
CHIPS = 8
OWN = 4
SPREAD = 16
MEMBERS = GROUPS * OWN
TOKENS = MEMBERS * SPREAD
PIECE = OWN * SPREAD
LANES = HEADS * MEMBERS
BLOCK = 256
PER_BLOCK = BLOCK // MEMBERS
ROWS = 192
GAIN_ROWS = 8
CHUNK = ROWS + GAIN_ROWS
SLAB = 24
SMALL = SLAB + GAIN_ROWS

EPS = 1e-06
GELU_C = 0.7978845608028654
GELU_A = 0.044715
SCALE = 1.0 / math.sqrt(HEAD_DIM)

F32 = jnp.float32
B16 = jnp.bfloat16
VMEM = pl.BlockSpec(memory_space=pltpu.VMEM)
SMEM = pl.BlockSpec(memory_space=pltpu.SMEM)


def dot(left, right, contract):
    return lax.dot_general(left, right, ((contract[:1], contract[1:]), ((), ())), preferred_element_type=F32)


def norm_rows(values):
    inverse = lax.rsqrt(jnp.mean(values * values, axis=-1, keepdims=True) + EPS)
    return values * inverse, inverse


def norm_back(unit_rows, inverse, gains, upstream):
    scaled = upstream * gains
    return inverse * (scaled - unit_rows * jnp.mean(scaled * unit_rows, axis=-1, keepdims=True))


def gelu_pair(preact):
    square = preact * preact
    tangent = jnp.tanh(GELU_C * (preact + GELU_A * preact * square))
    half = 0.5 * (1.0 + tangent)
    slopes = half + 0.5 * preact * (1.0 - tangent * tangent) * (
        GELU_C * (1.0 + 3.0 * GELU_A * square)
    )
    return preact * half, slopes


def own_heads(stacked):
    lane_head = lax.broadcasted_iota(jnp.int32, (MEMBERS, WIDTH), 1) // HEAD_DIM
    result = stacked[:MEMBERS]
    for head in range(1, HEADS):
        result = jnp.where(lane_head == head, stacked[head * MEMBERS : (head + 1) * MEMBERS], result)
    return result


def layer_kernel(
    core_ref,
    both_ref,
    gain1_ref,
    wqkv_ref,
    wout_ref,
    gain2_ref,
    wup_ref,
    wdown_ref,
    keep_ref,
    give_ref,
    xs,
    gs,
    ds,
    mask,
    qkv,
    expanded,
    probs,
    rounded,
    mixs,
    gmix,
    n1s,
    n2s,
    gas,
    ogs,
    gqkv,
    gpre,
    acts,
    gain_sums,
    parts,
):
    core = core_ref[0]
    for group in range(GROUPS):
        rows = slice(group * PIECE, (group + 1) * PIECE)
        for side in range(2):
            lanes = slice(side * 128, (side + 1) * 128)
            xs[side, rows] = both_ref[group, :PIECE, lanes].astype(F32)
            gs[side, rows] = both_ref[group, PIECE:, lanes].astype(F32)
    mask[...] = (
        lax.broadcasted_iota(jnp.int32, (LANES, WIDTH), 0) // MEMBERS
        == lax.broadcasted_iota(jnp.int32, (LANES, WIDTH), 1) // HEAD_DIM
    ).astype(F32).astype(B16)
    gain_sums[...] = jnp.zeros_like(gain_sums)
    gain1 = gain1_ref[...]
    gain2 = gain2_ref[...]

    def block(step, carry):
        base = pl.multiple_of(step * BLOCK, BLOCK)
        here = pl.ds(base, BLOCK)

        def patches(ref):
            return jnp.concatenate(
                [
                    jnp.concatenate(
                        [ref[side, pl.ds(step * PER_BLOCK + j, MEMBERS, stride=SPREAD), :] for j in range(PER_BLOCK)],
                        axis=0,
                    )
                    for side in range(2)
                ],
                axis=1,
            )

        wide = patches(xs)
        unit1, inverse1 = norm_rows(wide)
        normed1 = (unit1 * gain1).astype(B16)
        n1s[here] = normed1
        qkv[...] = jnp.dot(normed1, wqkv_ref[...], preferred_element_type=F32).astype(B16)
        for j in range(PER_BLOCK):
            rows = slice(j * MEMBERS, (j + 1) * MEMBERS)
            query, keys, values = (qkv[rows, i * WIDTH : (i + 1) * WIDTH] for i in range(3))
            spread_query = jnp.concatenate([query] * HEADS, axis=0) * mask[...]
            expanded[j] = spread_query
            scores = dot(keys, spread_query, (1, 1)) * SCALE
            scores = jnp.exp(scores - jnp.max(scores, axis=0, keepdims=True))
            weights = scores * (1.0 / jnp.sum(scores, axis=0, keepdims=True))
            probs[j] = weights
            narrow = weights.astype(B16)
            rounded[j] = narrow
            mixs[pl.ds(base + j * MEMBERS, MEMBERS)] = own_heads(dot(narrow, values, (0, 0))).astype(B16)

        cotangent = patches(gs)
        cotangent_narrow = cotangent.astype(B16)
        ogs[here] = cotangent_narrow
        hidden = wide + jnp.dot(mixs[here], wout_ref[...], preferred_element_type=F32)
        unit2, inverse2 = norm_rows(hidden)
        normed2 = (unit2 * gain2).astype(B16)
        n2s[here] = normed2
        activated, slopes = gelu_pair(jnp.dot(normed2, wup_ref[...], preferred_element_type=F32))
        acts[here] = activated.astype(B16)
        grad_pre = (dot(cotangent_narrow, wdown_ref[...], (1, 1)) * slopes).astype(B16)
        gpre[here] = grad_pre
        grad_normed2 = dot(grad_pre, wup_ref[...], (1, 1))
        gain_sums[1:2] += jnp.sum(grad_normed2 * unit2, axis=0, keepdims=True)
        back_two = norm_back(unit2, inverse2, gain2, grad_normed2)
        grad_attn = (cotangent + back_two).astype(B16)
        gas[here] = grad_attn
        gmix[...] = dot(grad_attn, wout_ref[...], (1, 1)).astype(B16)
        for j in range(PER_BLOCK):
            rows = slice(j * MEMBERS, (j + 1) * MEMBERS)
            there = pl.ds(base + j * MEMBERS, MEMBERS)
            keys, values = (qkv[rows, i * WIDTH : (i + 1) * WIDTH] for i in (1, 2))
            spread_grad = jnp.concatenate([gmix[rows]] * HEADS, axis=0) * mask[...]
            dprob = dot(values, spread_grad, (1, 1))
            grad_v = jnp.dot(rounded[j], spread_grad, preferred_element_type=F32)
            weights = probs[j]
            product = weights * dprob
            dscore = (
                (product - weights * jnp.sum(product, axis=0, keepdims=True)) * SCALE
            ).astype(B16)
            grad_k = jnp.dot(dscore, expanded[j], preferred_element_type=F32)
            grad_q = own_heads(dot(dscore, keys, (0, 0)))
            gqkv[there, :WIDTH] = grad_q.astype(B16)
            gqkv[there, WIDTH : 2 * WIDTH] = grad_k.astype(B16)
            gqkv[there, 2 * WIDTH :] = grad_v.astype(B16)
        grad_normed1 = dot(gqkv[here], wqkv_ref[...], (1, 1))
        gain_sums[0:1] += jnp.sum(grad_normed1 * unit1, axis=0, keepdims=True)
        delta = back_two + norm_back(unit1, inverse1, gain1, grad_normed1)
        for j in range(PER_BLOCK):
            for side in range(2):
                ds[side, pl.ds(step * PER_BLOCK + j, MEMBERS, stride=SPREAD), :] = delta[
                    j * MEMBERS : (j + 1) * MEMBERS, side * 128 : (side + 1) * 128
                ]
        return carry

    lax.fori_loop(0, TOKENS // BLOCK, block, 0)

    part_qkv = dot(n1s[...], gqkv[...], (0, 0)).astype(B16)
    for i in range(3):
        parts[i * WIDTH : (i + 1) * WIDTH] = part_qkv[:, i * WIDTH : (i + 1) * WIDTH]
    parts[3 * WIDTH : 4 * WIDTH] = dot(mixs[...], gas[...], (0, 0)).astype(B16)
    part_up = dot(n2s[...], gpre[...], (0, 0)).astype(B16)
    for i in range(4):
        parts[(4 + i) * WIDTH : (5 + i) * WIDTH] = part_up[:, i * WIDTH : (i + 1) * WIDTH]
    part_down = dot(ogs[...], acts[...], (0, 0))
    for i in range(4):
        parts[(8 + i) * WIDTH : (9 + i) * WIDTH] = part_down[:, i * WIDTH : (i + 1) * WIDTH].T.astype(B16)
    gain_rows = gain_sums[...].astype(B16)
    for target, side in ((keep_ref, core), (give_ref, 1 - core)):
        for chip in range(CHIPS):
            start = pl.multiple_of(side * (CHIPS * ROWS) + chip * ROWS, ROWS)
            target[chip, :ROWS] = parts[pl.ds(start, ROWS)]
            target[chip, ROWS:CHUNK] = gain_rows
            start = pl.multiple_of((2 * chip + side) * PIECE, PIECE)
            for lane in range(2):
                target[chip, CHUNK:, lane * 128 : (lane + 1) * 128] = ds[lane, pl.ds(start, PIECE)].astype(B16)


def run_layer(core, both, gain1, wqkv, wout, gain2, wup, wdown):
    scratch = [
        pltpu.VMEM((2, TOKENS, 128), F32),
        pltpu.VMEM((2, TOKENS, 128), F32),
        pltpu.VMEM((2, TOKENS, 128), F32),
        pltpu.VMEM((LANES, WIDTH), B16),
        pltpu.VMEM((BLOCK, 3 * WIDTH), B16),
        pltpu.VMEM((PER_BLOCK, LANES, WIDTH), B16),
        pltpu.VMEM((PER_BLOCK, MEMBERS, LANES), F32),
        pltpu.VMEM((PER_BLOCK, MEMBERS, LANES), B16),
        pltpu.VMEM((TOKENS, WIDTH), B16),
        pltpu.VMEM((BLOCK, WIDTH), B16),
        pltpu.VMEM((TOKENS, WIDTH), B16),
        pltpu.VMEM((TOKENS, WIDTH), B16),
        pltpu.VMEM((TOKENS, WIDTH), B16),
        pltpu.VMEM((TOKENS, WIDTH), B16),
        pltpu.VMEM((TOKENS, 3 * WIDTH), B16),
        pltpu.VMEM((TOKENS, HIDDEN), B16),
        pltpu.VMEM((TOKENS, HIDDEN), B16),
        pltpu.VMEM((GAIN_ROWS, WIDTH), F32),
        pltpu.VMEM((2 * CHIPS * ROWS, WIDTH), B16),
    ]
    shape = jax.ShapeDtypeStruct((CHIPS, CHUNK + PIECE, WIDTH), B16)
    return pl.pallas_call(
        layer_kernel,
        out_shape=(shape, shape),
        in_specs=[SMEM] + [VMEM] * 7,
        out_specs=(VMEM, VMEM),
        scratch_shapes=scratch,
        compiler_params=pltpu.CompilerParams(vmem_limit_bytes=48 * 1024 * 1024),
        cost_estimate=pl.CostEstimate(flops=5_000_000_000, bytes_accessed=6_000_000, transcendentals=2_000_000),
    )(core, both, gain1, wqkv, wout, gain2, wup, wdown)


def pack_kernel(input_ref, grad_ref, out_ref):
    for group in range(GROUPS):
        for own in range(OWN):
            there = slice(group * SPREAD, (group + 1) * SPREAD)
            out_ref[group, own * SPREAD : (own + 1) * SPREAD] = input_ref[own, there]
            out_ref[group, PIECE + own * SPREAD : PIECE + (own + 1) * SPREAD] = grad_ref[own, there]


def pair_kernel(keep_ref, got_ref, out_ref):
    for chip in range(CHIPS):
        total = keep_ref[chip, :CHUNK].astype(F32) + got_ref[chip, :CHUNK].astype(F32)
        out_ref[chip, :CHUNK] = total.astype(B16)
        out_ref[chip, CHUNK : CHUNK + PIECE] = keep_ref[chip, CHUNK:]
        out_ref[chip, CHUNK + PIECE :] = got_ref[chip, CHUNK:]


def sum_kernel(got_ref, out_ref):
    total = got_ref[0, :CHUNK].astype(F32)
    for chip in range(1, CHIPS):
        total = total + got_ref[chip, :CHUNK].astype(F32)
    for slab in range(CHIPS):
        for side in range(2):
            lanes = slice(side * 128, (side + 1) * 128)
            out_ref[2 * slab + side, :SLAB] = total[slab * SLAB : (slab + 1) * SLAB, lanes].astype(B16)
            out_ref[2 * slab + side, SLAB:] = total[ROWS:, lanes].astype(B16)


def home_kernel(core_ref, got_ref, grad_ref, out_ref):
    core = core_ref[0]
    for chip in range(CHIPS):
        for part in range(2):
            index = 2 * chip + (core if part == 0 else 1 - core)
            there = pl.ds(pl.multiple_of(index * SPREAD, SPREAD), SPREAD)
            first = CHUNK + part * PIECE
            for own in range(OWN):
                moved = got_ref[chip, first + own * SPREAD : first + (own + 1) * SPREAD]
                out_ref[own, there] = grad_ref[own, there].astype(F32) + moved.astype(F32)


def spread_kernel(got_ref, out_ref, gains_ref):
    for slab in range(CHIPS):
        for side in range(2):
            lanes = slice(side * 128, (side + 1) * 128)
            piece = got_ref[2 * slab + side, :SLAB]
            for chip in range(CHIPS):
                out_ref[chip, slab * SLAB : (slab + 1) * SLAB, lanes] = piece
    for side in range(2):
        gains_ref[:, side * 128 : (side + 1) * 128] = got_ref[side, SLAB:]


def final_kernel(
    scale, core_ref, mine_ref, theirs_ref, gains_ref, q_ref, k_ref, v_ref, o_ref, up_ref, down_ref, g1_ref, g2_ref
):
    core = core_ref[0]

    def fill(low_ref, high_ref):
        def low(index):
            return low_ref[index * WIDTH : (index + 1) * WIDTH].astype(F32) * scale

        def high(index):
            return high_ref[index * WIDTH : (index + 1) * WIDTH].astype(F32) * scale

        for index, ref in enumerate((q_ref, k_ref, v_ref, o_ref)):
            ref[...] = low(index)
        for index in range(2):
            up_ref[:, index * WIDTH : (index + 1) * WIDTH] = low(4 + index)
            up_ref[:, (2 + index) * WIDTH : (3 + index) * WIDTH] = high(index)
        for index in range(4):
            down_ref[index * WIDTH : (index + 1) * WIDTH] = high(2 + index)

    @pl.when(core == 0)
    def _():
        fill(mine_ref, theirs_ref)

    @pl.when(core != 0)
    def _():
        fill(theirs_ref, mine_ref)

    gains = gains_ref[...].astype(F32) * scale
    g1_ref[...] = gains[0:1]
    g2_ref[...] = gains[1:2]


def local(kernel, out_shape, specs, *operands):
    return pl.pallas_call(
        kernel,
        out_shape=out_shape,
        in_specs=specs,
        out_specs=jax.tree.map(lambda _: VMEM, out_shape),
        compiler_params=pltpu.CompilerParams(vmem_limit_bytes=32 * 1024 * 1024),
    )(*operands)


def shaped(*shape, dtype=B16):
    return jax.ShapeDtypeStruct(shape, dtype)


def swap(array, axis, groups=None):
    return lax.all_to_all(
        array, axis, split_axis=0, concat_axis=0, tiled=True, axis_index_groups=groups
    )


def on_device(
    layer_input, out_grad, norm1_gain, w_query, w_key, w_value, w_out, norm2_gain, w_up, w_down
):
    members = lax.axis_size("member")
    spaces = lax.axis_size("space")
    core = (lax.axis_index("member") % 2).astype(jnp.int32).reshape(1)
    other_core = [(k, k ^ 1) for k in range(members)]
    same_core = [[c + 2 * k for k in range(CHIPS)] for c in range(2)]

    both = local(pack_kernel, shaped(GROUPS, 2 * PIECE, WIDTH), [VMEM] * 2, layer_input, out_grad)
    both = swap(both, "member")
    wqkv = jnp.concatenate([w_query, w_key, w_value], axis=1)
    keep, give = run_layer(
        core, both, norm1_gain.reshape(1, WIDTH), wqkv, w_out, norm2_gain.reshape(1, WIDTH), w_up, w_down
    )
    got = lax.ppermute(give, "member", other_core)
    sent = local(pair_kernel, shaped(CHIPS, CHUNK + 2 * PIECE, WIDTH), [VMEM] * 2, keep, got)
    got = swap(sent, "member", same_core)
    input_grad = local(
        home_kernel, shaped(OWN, GROUPS * SPREAD, WIDTH, dtype=F32), [SMEM, VMEM, VMEM], core, got, out_grad
    )
    sent = local(sum_kernel, shaped(spaces, SMALL, 128), [VMEM], got)
    total = swap(sent, "space").astype(F32).sum(axis=0).astype(B16)
    everywhere = swap(jnp.broadcast_to(total, (spaces, SMALL, 128)), "space")
    sent, gains = local(
        spread_kernel, (shaped(CHIPS, ROWS, WIDTH), shaped(GAIN_ROWS, WIDTH)), [VMEM], everywhere
    )
    mine = swap(sent, "member", same_core).reshape(CHIPS * ROWS, WIDTH)
    theirs = lax.ppermute(mine, "member", other_core)
    scale = 1.0 / math.sqrt(MEMBERS * GROUPS * SPREAD * spaces)
    square = shaped(WIDTH, WIDTH, dtype=F32)
    row = shaped(1, WIDTH, dtype=F32)
    grads = local(
        functools.partial(final_kernel, scale),
        (square, square, square, square, shaped(WIDTH, HIDDEN, dtype=F32), shaped(HIDDEN, WIDTH, dtype=F32), row, row),
        [SMEM, VMEM, VMEM, VMEM],
        core,
        mine,
        theirs,
        gains,
    )
    return (input_grad, *grads[:6], grads[6].reshape(WIDTH), grads[7].reshape(WIDTH))


def solution(mesh):
    in_specs = (
        P("member", "space", None),
        P("member", "space", None),
        P(),
        P(),
        P(),
        P(),
        P(),
        P(),
        P(),
        P(),
    )
    out_specs = (P("member", "space", None), P(), P(), P(), P(), P(), P(), P(), P())
    return jax.shard_map(
        on_device, mesh=mesh, in_specs=in_specs, out_specs=out_specs, check_vma=False
    )
```

time: 472 us -> 127 us (0.27)
  waiting for transfers between devices: 208 us -> 18.9 us
  matrix products: 59.1 us -> 0 us
  local copies, waits for them, and re-layouts: 46.7 us -> 2.14 us
  blocking collectives: 94.2 us -> 63.8 us
  Pallas kernels: 0 us -> 28 us
  starting transfers between devices: 39 us -> 13 us
  between operations: 14.5 us -> 0.77 us
  other arithmetic: 7.66 us -> 0.05 us
    psum x1 -> x0, waiting for transfers between devices: 182 us -> none  [on_device(): lax.psum((part_query, part_key, part_value, part_wout, part_up, part_down...]
    psum x1 -> x0, blocking collectives: 80 us -> none  [on_device(): lax.psum((part_query, part_key, part_value, part_wout, part_up, part_down...]
    dot_general x22 -> x0, matrix products: 53.8 us -> none  [multiply(): return jnp.einsum(form, left, right, preferred_element_type=jnp.float32)]
    all_to_all x1 -> x4, blocking collectives: 14.2 us -> 63.8 us  [swap(): lax.all_to_all(array, axis, split_axis=0, concat_axis=0, tiled=True, axis...]
    another operation x12 -> x0, local copies, waits for them, and re-layouts: 34.3 us -> none  [the longest x4 9.82 us: memberwise(): return array.reshape(everyone, 1, spread, array.shape[-1])]
    all_to_all x7 -> x1, starting transfers between devices: 39 us -> 7.06 us  [swap(): lax.all_to_all(array, axis, split_axis=0, concat_axis=0, tiled=True, axis...]
    pallas_call x0 -> x7, Pallas kernels: none -> 28 us  [the longest x1 23.5 us: run_layer(): pl.pallas_call(layer_kernel, out_shape=(shape, shape), in_specs=[SMEM] +...]
    all_to_all x7 -> x1, waiting for transfers between devices: 25.8 us -> 15.8 us  [swap(): lax.all_to_all(array, axis, split_axis=0, concat_axis=0, tiled=True, axis...]
  transfers between devices with their start and end apart: 8 -> 3, of which waited for: 5 -> 3; matrix products, arithmetic and copies ran while one was open for 13% -> 0% of each run, Pallas kernels for 0% -> 1%
where the time goes in v2:
time: 127 us
  blocking collectives  63.8 us (50%)
  Pallas kernels  28 us (22%)
  waiting for transfers between devices  18.9 us (15%)
  starting transfers between devices  13 us (10%)
  local copies, waits for them, and re-layouts  2.14 us (2%)
    all_to_all x4, blocking collectives, swap(): lax.all_to_all(array, axis, split_axis=0, concat_axis=0, tiled=True, axis...  63.8 us
    pallas_call x1, Pallas kernels, run_layer(): pl.pallas_call(layer_kernel, out_shape=(shape, shape), in_specs=[SMEM] +...  23.5 us
    all_to_all x1, waiting for transfers between devices, swap(): lax.all_to_all(array, axis, split_axis=0, concat_axis=0, tiled=True, axis...  15.8 us
    all_to_all x1, starting transfers between devices, swap(): lax.all_to_all(array, axis, split_axis=0, concat_axis=0, tiled=True, axis...  7.06 us
    ppermute x1, starting transfers between devices, on_device(): theirs = lax.ppermute(mine, 'member', other_core)  4.96 us
    pallas_call x6, Pallas kernels, local(): pl.pallas_call(kernel, out_shape=out_shape, in_specs=specs, out_specs=jax...  4.43 us
  transfers between devices with their start and end apart: 3, of which 3 were waited for; matrix products, arithmetic and copies ran while one was open for 0% of the time, Pallas kernels for 1%

profile of v2, /device:TPU:1, one launch (start us, length us, event | category | flops | bytes accessed | tf_op | source)
XLA Modules:
  0.0 126.7 jit_solution(14274509476528322680)
XLA Ops:
  0.6 0.0 copy-start
  0.7 1.0 copy-done
  1.7 1.0 copy-done.2
  2.7 1.0 shard_map.169
  3.8 0.0 copy-start.4
  3.8 0.0 copy-start.5
  3.8 0.0 copy-start.6
  3.8 0.0 copy-start.7
  3.8 7.1 %all-to-all-start = ((bf16[16,128,256]{2,1,0:T(8,128)(2,1)}), bf16[16,128,256]{2,1,0:T(8,128)(2,1)S(1)}, u32[]{:S(2)}, u32[]{:S(2)}) async-start(bf16[16,128,256]{2,1,0:T(8,128)(2,1)} %shard_map.169), calls=%async_computation | async-start | bytes 2097152 | tf_op jit(solution)/shard_map/all_to_all | solution.py:353
  10.9 0.0 copy-done.8
  10.9 0.0 copy-done.9
  10.9 0.0 copy-done.10
  10.9 15.8 %all-to-all-done.both_ref = bf16[16,128,256]{2,1,0:T(8,128)(2,1)S(1)} async-done(((bf16[16,128,256]{2,1,0:T(8,128)(2,1)}), bf16[16,128,256]{2,1,0:T(8,128)(2,1)S(1)}, u32[]{:S(2)}, u32[]{:S(2)}) %all-to-all-start) | async-done | bytes 1048608 | tf_op jit(solution)/shard_map/all_to_all | solution.py:353
  26.7 0.0 copy-done.3
  26.7 0.0 copy-done.4
  26.7 0.0 copy-done.5
  26.7 0.0 copy-done.6
  26.7 23.5 %shard_map.170 = (bf16[8,264,256]{2,1,0:T(8,128)(2,1)S(1)}, bf16[8,264,256]{2,1,0:T(8,128)(2,1)S(1)}) custom-call(s32[1]{0:T(128)} %bitcast.core_ref, bf16[16,128,256]{2,1,0:T(8,128)(2,1)S(1)} %all-to-all-done.both_ref, f32[1,256]{1,0:T(1,128)S(1)} %bitcast.8, bf16[256,768]{1,0:T(8,128)(2,1)S(1)} %pad_maximum_fusion.wqkv_ref, ...), custom_call_target="tpu_custom_call" | custom-call | flops 5000000000 | bytes 6000000 | tf_op jit(solution)/shard_map/pallas_call | solution.py:244
  50.3 1.0 collective-permute-start
  51.2 2.3 %collective-permute-done.got_ref = bf16[8,264,256]{2,1,0:T(8,128)(2,1)S(1)} collective-permute-done((bf16[8,264,256]{2,1,0:T(8,128)(2,1)S(1)}, bf16[8,264,256]{2,1,0:T(8,128)(2,1)S(1)}, u32[]{:S(2)}, u32[]{:S(2)}) %collective-permute-start) | collective-permute-done | bytes 1081376 | tf_op jit(solution)/shard_map/ppermute | solution.py:373
  53.6 0.2 shard_map.171
  53.8 21.1 %all_to_all.25.got_ref = bf16[8,328,256]{2,1,0:T(8,128)(2,1)S(1)} all-to-all(bf16[8,328,256]{2,1,0:T(8,128)(2,1)S(1)} %shard_map.171), channel_id=1, replica_groups={{0,32,64,96,128,160,192,224},{16,48,80,112,144,176,208,240},{1,33,65,97..., dimensions={0} | all-to-all | bytes 2686976 | tf_op jit(solution)/shard_map/all_to_all | solution.py:353
  74.9 0.1 shard_map.173
  75.0 19.2 %all_to_all.26 = bf16[16,32,128]{2,1,0:T(8,128)(2,1)S(1)} all-to-all(bf16[16,32,128]{2,1,0:T(8,128)(2,1)S(1)} %shard_map.173), channel_id=1, replica_groups=mesh['member'=16,'space'=16] {'space'}, dimensions={0} | all-to-all | bytes 262144 | tf_op jit(solution)/shard_map/all_to_all | solution.py:353
  94.2 0.0 copy-start.1
  94.3 12.1 %all_to_all.27.got_ref = bf16[16,32,128]{2,1,0:T(8,128)(2,1)S(1)} all-to-all(bf16[16,32,128]{2,1,0:T(8,128)(2,1)S(1)} %broadcast_in_dim.3), channel_id=1, replica_groups=mesh['member'=16,'space'=16] {'space'}, dimensions={0} | all-to-all | bytes 262144 | tf_op jit(solution)/shard_map/all_to_all | solution.py:353
  106.4 0.1 shard_map.174
  106.5 11.4 %all_to_all.28 = bf16[8,192,256]{2,1,0:T(8,128)(2,1)S(1)} all-to-all(bf16[8,192,256]{2,1,0:T(8,128)(2,1)S(1)} %get-tuple-element.23), channel_id=1, replica_groups={{0,32,64,96,128,160,192,224},{16,48,80,112,144,176,208,240},{1,33,65,97..., dimensions={0} | all-to-all | bytes 1572864 | tf_op jit(solution)/shard_map/all_to_all | solution.py:353
  117.9 5.0 %collective-permute-start.1 = (bf16[1536,256]{1,0:T(8,128)(2,1)S(1)}, bf16[1536,256]{1,0:T(8,128)(2,1)S(1)}, u32[]{:S(2)}, u32[]{:S(2)}) collective-permute-start(bf16[1536,256]{1,0:T(8,128)(2,1)S(1)} %bitcast.6), channel_id=1, source_target_pairs={{0,16},{16,0},{32,48},{48,32},{64,80},{80,64},{96,112},{112,96},{1... | collective-permute-start | bytes 2359304 | tf_op jit(solution)/shard_map/ppermute | solution.py:386
  122.9 1.1 shard_map.172
  124.0 0.8 collective-permute-done.1.theirs_ref
  124.8 1.9 %shard_map.175 = (f32[256,256]{1,0:T(8,128)}, f32[256,256]{1,0:T(8,128)}, f32[256,256]{1,0:T(8,128)}, f32[256,256]{1,0:T(8,128)}, f32[256,1024]{1,0:T(8,128)}, /...) custom-call(s32[1]{0:T(128)} %bitcast.core_ref, bf16[1536,256]{1,0:T(8,128)(2,1)S(1)} %bitcast.7, ...), custom_call_target="tpu_custom_call" | custom-call | tf_op jit(solution)/shard_map/pallas_call | solution.py:339
  (10 shorter events, 0.1 us)
Async XLA Ops:
  0.6 1.0 copy-start
  1.7 1.0 copy-start.2
  3.8 7.1 %copy-start.8 = (bf16[256,256]{1,0:T(8,128)(2,1)S(1)}, bf16[256,256]{1,0:T(8,128)(2,1)}, u32[]{:S(2)}) copy-start(bf16[256,256]{1,0:T(8,128)(2,1)} %param.15) | copy-start | bytes 393220
  3.8 7.1 %copy-start.9 = (bf16[256,256]{1,0:T(8,128)(2,1)S(1)}, bf16[256,256]{1,0:T(8,128)(2,1)}, u32[]{:S(2)}) copy-start(bf16[256,256]{1,0:T(8,128)(2,1)} %param.14) | copy-start | bytes 393220
  3.8 7.1 %copy-start.10 = (bf16[256,256]{1,0:T(8,128)(2,1)S(1)}, bf16[256,256]{1,0:T(8,128)(2,1)}, u32[]{:S(2)}) copy-start(bf16[256,256]{1,0:T(8,128)(2,1)} %param.13) | copy-start | bytes 393220
  3.8 22.9 %copy-start.3 = (bf16[256,1024]{1,0:T(8,128)(2,1)S(1)}, bf16[256,1024]{1,0:T(8,128)(2,1)}, u32[]{:S(2)}) copy-start(bf16[256,1024]{1,0:T(8,128)(2,1)} %wup_ref.1) | copy-start | bytes 1572868
  3.8 22.9 %copy-start.4 = (bf16[1024,256]{1,0:T(8,128)(2,1)S(1)}, bf16[1024,256]{1,0:T(8,128)(2,1)}, u32[]{:S(2)}) copy-start(bf16[1024,256]{1,0:T(8,128)(2,1)} %wdown_ref.1) | copy-start | bytes 1572868
  3.8 22.9 %copy-start.5 = (bf16[256,256]{1,0:T(8,128)(2,1)S(1)}, bf16[256,256]{1,0:T(8,128)(2,1)}, u32[]{:S(2)}) copy-start(bf16[256,256]{1,0:T(8,128)(2,1)} %wout_ref.1) | copy-start | bytes 393220
  3.8 22.9 %copy-start.6 = (f32[256]{0:T(256)S(1)}, f32[256]{0:T(256)}, u32[]{:S(2)}) copy-start(f32[256]{0:T(256)} %param.12) | copy-start | bytes 3076
  3.8 22.9 %copy-start.7 = (f32[256]{0:T(256)S(1)}, f32[256]{0:T(256)}, u32[]{:S(2)}) copy-start(f32[256]{0:T(256)} %param.17) | copy-start | bytes 3076
  3.8 22.9 %all-to-all-start = ((bf16[16,128,256]{2,1,0:T(8,128)(2,1)}), bf16[16,128,256]{2,1,0:T(8,128)(2,1)S(1)}, u32[]{:S(2)}, u32[]{:S(2)}) async-start(bf16[16,128,256]{2,1,0:T(8,128)(2,1)} %shard_map.169), calls=%async_computation | async-start | bytes 2097152 | tf_op jit(solution)/shard_map/all_to_all | solution.py:353
  50.3 3.3 %collective-permute-start = (bf16[8,264,256]{2,1,0:T(8,128)(2,1)S(1)}, bf16[8,264,256]{2,1,0:T(8,128)(2,1)S(1)}, u32[]{:S(2)}, u32[]{:S(2)}) collective-permute-start(bf16[8,264,256]{2,1,0:T(8,128)(2,1)S(1)} %get-tuple-element.22), channel_id=1, source_target_pairs={{0,16},{16,0},{32,48},{48,32},{64,80},{80,64},{96,112},{112,96},{1... | collective-permute-start | bytes 3244040 | tf_op jit(solution)/shard_map/ppermute | solution.py:373
  94.2 28.6 %copy-start.1 = (bf16[4,256,256]{2,1,0:T(8,128)(2,1)S(1)}, bf16[4,256,256]{2,1,0:T(8,128)(2,1)}, u32[]{:S(2)}) copy-start(bf16[4,256,256]{2,1,0:T(8,128)(2,1)} %grad_ref.3) | copy-start | bytes 1572868
  117.9 6.9 %collective-permute-start.1 = (bf16[1536,256]{1,0:T(8,128)(2,1)S(1)}, bf16[1536,256]{1,0:T(8,128)(2,1)S(1)}, u32[]{:S(2)}, u32[]{:S(2)}) collective-permute-start(bf16[1536,256]{1,0:T(8,128)(2,1)S(1)} %bitcast.6), channel_id=1, source_target_pairs={{0,16},{16,0},{32,48},{48,32},{64,80},{80,64},{96,112},{112,96},{1... | collective-permute-start | bytes 2359304 | tf_op jit(solution)/shard_map/ppermute | solution.py:386

commit v3 on v2

v3 whole, which is shorter than its diff:
```python
import functools
import math

import jax
import jax.numpy as jnp
from jax import lax
from jax.experimental import pallas as pl
from jax.experimental.pallas import tpu as pltpu
from jax.sharding import PartitionSpec as P

HEAD_DIM = 32
WIDTH = 256
HIDDEN = 1024
HEADS = WIDTH // HEAD_DIM
GROUPS = 16
CHIPS = 8
OWN = 4
SPREAD = 16
MEMBERS = GROUPS * OWN
TOKENS = MEMBERS * SPREAD
PIECE = OWN * SPREAD
HALF = WIDTH // 2
HALF_HEADS = HEADS // 2
LANES = HALF_HEADS * MEMBERS
ROWS = 192
GAIN_ROWS = 8
CHUNK = ROWS + GAIN_ROWS
SLAB = 24
SMALL = SLAB + GAIN_ROWS

EPS = 1e-06
GELU_C = 0.7978845608028654
GELU_A = 0.044715
SCALE = 1.0 / math.sqrt(HEAD_DIM)

F32 = jnp.float32
B16 = jnp.bfloat16
VMEM = pl.BlockSpec(memory_space=pltpu.VMEM)
ANY = pl.BlockSpec(memory_space=pl.ANY)
SMEM = pl.BlockSpec(memory_space=pltpu.SMEM)


def dot(left, right, contract):
    return lax.dot_general(left, right, ((contract[:1], contract[1:]), ((), ())), preferred_element_type=F32)


def norm_rows(values):
    inverse = lax.rsqrt(jnp.mean(values * values, axis=-1, keepdims=True) + EPS)
    return values * inverse, inverse


def norm_back(unit_rows, inverse, gains, upstream):
    scaled = upstream * gains
    return inverse * (scaled - unit_rows * jnp.mean(scaled * unit_rows, axis=-1, keepdims=True))


def gelu_pair(preact):
    square = preact * preact
    half = 0.5 + 0.5 * jnp.tanh(preact * (GELU_C + (GELU_C * GELU_A) * square))
    bend = preact * (2.0 * GELU_C + (6.0 * GELU_C * GELU_A) * square)
    return preact * half, half + (half - half * half) * bend


def own_heads(stacked):
    lane_head = lax.broadcasted_iota(jnp.int32, (MEMBERS, HALF), 1) // HEAD_DIM
    result = stacked[:MEMBERS]
    for head in range(1, HALF_HEADS):
        result = jnp.where(lane_head == head, stacked[head * MEMBERS : (head + 1) * MEMBERS], result)
    return result


def layer_kernel(
    core_ref,
    both_ref,
    gain1_ref,
    wqkv_ref,
    wout_ref,
    gain2_ref,
    wup_ref,
    wdown_ref,
    keep_ref,
    give_ref,
    xs,
    gs,
    ds,
    mask,
    qkv,
    expanded,
    probs,
    dprobs,
    rounded,
    mixs,
    gmix,
    n1s,
    n2s,
    gas,
    ogs,
    gqkv,
    gpre,
    acts,
    unit1s,
    unit2s,
    backs,
    products,
    wide_products,
    parts,
):
    core = core_ref[0]
    halves = [slice(side * HALF, (side + 1) * HALF) for side in range(2)]
    blocks = [slice(patch * MEMBERS, (patch + 1) * MEMBERS) for patch in range(SPREAD)]
    for group in range(GROUPS):
        rows = slice(group * PIECE, (group + 1) * PIECE)
        for side, lanes in enumerate(halves):
            xs[side, rows] = both_ref[group, 0, :, :, lanes].astype(F32).reshape(PIECE, HALF)
            gs[side, rows] = both_ref[group, 1, :, :, lanes].astype(F32).reshape(PIECE, HALF)
    mask[...] = (
        lax.broadcasted_iota(jnp.int32, (LANES, HALF), 0) // MEMBERS
        == lax.broadcasted_iota(jnp.int32, (LANES, HALF), 1) // HEAD_DIM
    ).astype(F32).astype(B16)
    gain1 = gain1_ref[...]
    gain2 = gain2_ref[...]

    def patch_rows(ref, patch):
        return jnp.concatenate(
            [ref[side, pl.ds(patch, MEMBERS, stride=SPREAD), :] for side in range(2)], axis=1
        )

    def spread_heads(rows):
        return jnp.concatenate([rows] * HALF_HEADS, axis=0) * mask[...]

    inverse1 = []
    for patch, rows in enumerate(blocks):
        unit, inverse = norm_rows(patch_rows(xs, patch))
        unit1s[rows] = unit
        inverse1.append(inverse)
        n1s[rows] = (unit * gain1).astype(B16)
        ogs[rows] = patch_rows(gs, patch).astype(B16)
    for i in range(3):
        lanes = slice(i * WIDTH, (i + 1) * WIDTH)
        qkv[:, lanes] = jnp.dot(n1s[...], wqkv_ref[:, lanes], preferred_element_type=F32).astype(B16)

    units = [(patch, side) for patch in range(SPREAD) for side in range(2)]

    def part(ref, index, patch, side):
        return ref[blocks[patch], index * WIDTH + side * HALF : index * WIDTH + (side + 1) * HALF]

    def staged(stages):
        lag = 4
        for step in range(0, len(units) + lag * (len(stages) - 1), lag):
            for late, stage in enumerate(stages):
                for unit in units[max(step - lag * late, 0) : max(step - lag * late + lag, 0)]:
                    stage(*unit)

    def score(patch, side):
        spread_query = spread_heads(part(qkv, 0, patch, side))
        expanded[patch, side] = spread_query
        probs[patch, side] = dot(part(qkv, 1, patch, side), spread_query, (1, 1)) * SCALE

    def soften(patch, side):
        scores = probs[patch, side]
        scores = jnp.exp(scores - jnp.max(scores, axis=0, keepdims=True))
        weights = scores * (1.0 / jnp.sum(scores, axis=0, keepdims=True))
        probs[patch, side] = weights
        rounded[patch, side] = weights.astype(B16)

    def mix(patch, side):
        mixed = own_heads(dot(rounded[patch, side], part(qkv, 2, patch, side), (0, 0)))
        mixs[blocks[patch], halves[side]] = mixed.astype(B16)

    staged((score, soften, mix))
    products[...] = jnp.dot(mixs[...], wout_ref[...], preferred_element_type=F32)
    inverse2 = []
    for patch, rows in enumerate(blocks):
        unit, inverse = norm_rows(patch_rows(xs, patch) + products[rows])
        unit2s[rows] = unit
        inverse2.append(inverse)
        n2s[rows] = (unit * gain2).astype(B16)

    for i in range(HIDDEN // WIDTH):
        lanes = slice(i * WIDTH, (i + 1) * WIDTH)
        wide_products[i % 2, 0] = jnp.dot(n2s[...], wup_ref[:, lanes], preferred_element_type=F32)
        wide_products[i % 2, 1] = dot(ogs[...], wdown_ref[lanes], (1, 1))
        for rows in blocks:
            activated, slopes = gelu_pair(wide_products[i % 2, 0, rows])
            acts[rows, lanes] = activated.astype(B16)
            gpre[rows, lanes] = (wide_products[i % 2, 1, rows] * slopes).astype(B16)
    products[...] = dot(gpre[...], wup_ref[...], (1, 1))
    gain2_sum = jnp.zeros((MEMBERS, WIDTH), F32)
    for patch, rows in enumerate(blocks):
        unit, grad = unit2s[rows], products[rows]
        gain2_sum = gain2_sum + grad * unit
        back = norm_back(unit, inverse2[patch], gain2, grad)
        backs[rows] = back
        gas[rows] = (ogs[rows].astype(F32) + back).astype(B16)
    gmix[...] = dot(gas[...], wout_ref[...], (1, 1)).astype(B16)

    def keep_grad(index, patch, side, grad):
        gqkv[blocks[patch], index * WIDTH + side * HALF : index * WIDTH + (side + 1) * HALF] = grad.astype(B16)

    def meet(patch, side):
        spread_grad = spread_heads(gmix[blocks[patch], halves[side]])
        dprobs[patch, side] = dot(part(qkv, 2, patch, side), spread_grad, (1, 1))
        keep_grad(2, patch, side, jnp.dot(rounded[patch, side], spread_grad, preferred_element_type=F32))

    def bend(patch, side):
        weights = probs[patch, side]
        product = weights * dprobs[patch, side]
        dscore = (product - weights * jnp.sum(product, axis=0, keepdims=True)) * SCALE
        rounded[patch, side] = dscore.astype(B16)

    def finish(patch, side):
        dscore = rounded[patch, side]
        keep_grad(1, patch, side, jnp.dot(dscore, expanded[patch, side], preferred_element_type=F32))
        keep_grad(0, patch, side, own_heads(dot(dscore, part(qkv, 1, patch, side), (0, 0))))

    staged((meet, bend, finish))
    products[...] = dot(gqkv[...], wqkv_ref[...], (1, 1))
    gain1_sum = jnp.zeros((MEMBERS, WIDTH), F32)
    for patch, rows in enumerate(blocks):
        unit, grad = unit1s[rows], products[rows]
        gain1_sum = gain1_sum + grad * unit
        delta = backs[rows] + norm_back(unit, inverse1[patch], gain1, grad)
        for side, lanes in enumerate(halves):
            ds[side, pl.ds(patch, MEMBERS, stride=SPREAD), :] = delta[:, lanes]

    for i in range(3):
        parts[i * WIDTH : (i + 1) * WIDTH] = dot(
            n1s[...], gqkv[:, i * WIDTH : (i + 1) * WIDTH], (0, 0)
        ).astype(B16)
    parts[3 * WIDTH : 4 * WIDTH] = dot(mixs[...], gas[...], (0, 0)).astype(B16)
    for i in range(4):
        parts[(4 + i) * WIDTH : (5 + i) * WIDTH] = dot(
            n2s[...], gpre[:, i * WIDTH : (i + 1) * WIDTH], (0, 0)
        ).astype(B16)
    for i in range(4):
        part_down = dot(ogs[...], acts[:, i * WIDTH : (i + 1) * WIDTH], (0, 0))
        parts[(8 + i) * WIDTH : (9 + i) * WIDTH] = part_down.T.astype(B16)
    gain_rows = jnp.concatenate(
        [jnp.sum(total, axis=0, keepdims=True) for total in (gain1_sum, gain2_sum)]
        + [jnp.zeros((GAIN_ROWS - 2, WIDTH), F32)],
        axis=0,
    ).astype(B16)
    for target, side in ((keep_ref, core), (give_ref, 1 - core)):
        for chip in range(CHIPS):
            start = pl.multiple_of(side * (CHIPS * ROWS) + chip * ROWS, ROWS)
            target[chip, :ROWS] = parts[pl.ds(start, ROWS)]
            target[chip, ROWS:CHUNK] = gain_rows
            start = pl.multiple_of((2 * chip + side) * PIECE, PIECE)
            for half, lanes in enumerate(halves):
                target[chip, CHUNK:, lanes] = ds[half, pl.ds(start, PIECE)].astype(B16)


def run_layer(core, both, gain1, wqkv, wout, gain2, wup, wdown):
    rows = (TOKENS, WIDTH)
    scratch = [
        pltpu.VMEM((2, TOKENS, HALF), F32),
        pltpu.VMEM((2, TOKENS, HALF), F32),
        pltpu.VMEM((2, TOKENS, HALF), F32),
        pltpu.VMEM((LANES, HALF), B16),
        pltpu.VMEM((TOKENS, 3 * WIDTH), B16),
        pltpu.VMEM((SPREAD, 2, LANES, HALF), B16),
        pltpu.VMEM((SPREAD, 2, MEMBERS, LANES), F32),
        pltpu.VMEM((SPREAD, 2, MEMBERS, LANES), F32),
        pltpu.VMEM((SPREAD, 2, MEMBERS, LANES), B16),
        pltpu.VMEM(rows, B16),
        pltpu.VMEM(rows, B16),
        pltpu.VMEM(rows, B16),
        pltpu.VMEM(rows, B16),
        pltpu.VMEM(rows, B16),
        pltpu.VMEM(rows, B16),
        pltpu.VMEM((TOKENS, 3 * WIDTH), B16),
        pltpu.VMEM((TOKENS, HIDDEN), B16),
        pltpu.VMEM((TOKENS, HIDDEN), B16),
        pltpu.VMEM(rows, F32),
        pltpu.VMEM(rows, F32),
        pltpu.VMEM(rows, F32),
        pltpu.VMEM(rows, F32),
        pltpu.VMEM((2, 2, *rows), F32),
        pltpu.VMEM((2 * CHIPS * ROWS, WIDTH), B16),
    ]
    shape = shaped(CHIPS, CHUNK + PIECE, WIDTH)
    return pl.pallas_call(
        layer_kernel,
        out_shape=(shape, shape),
        in_specs=[SMEM] + [VMEM] * 7,
        out_specs=(VMEM, VMEM),
        scratch_shapes=scratch,
        compiler_params=pltpu.CompilerParams(vmem_limit_bytes=48 * 1024 * 1024),
        cost_estimate=pl.CostEstimate(flops=5_000_000_000, bytes_accessed=6_000_000, transcendentals=2_000_000),
    )(core, both, gain1, wqkv, wout, gain2, wup, wdown)


def pack_kernel(input_ref, grad_ref, out_ref, sems):
    copies = []
    for group in range(GROUPS):
        there = slice(group * SPREAD, (group + 1) * SPREAD)
        for side, ref in enumerate((input_ref, grad_ref)):
            copies.append(
                pltpu.make_async_copy(ref.at[:, there], out_ref.at[group, side], sems.at[group, side])
            )
    for copy in copies:
        copy.start()
    for copy in copies:
        copy.wait()


def pack(layer_input, out_grad):
    return pl.pallas_call(
        pack_kernel,
        out_shape=shaped(GROUPS, 2, OWN, SPREAD, WIDTH),
        in_specs=[ANY, ANY],
        out_specs=VMEM,
        scratch_shapes=[pltpu.SemaphoreType.DMA((GROUPS, 2))],
    )(layer_input, out_grad)


def pair_kernel(keep_ref, got_ref, out_ref):
    for chip in range(CHIPS):
        total = keep_ref[chip, :CHUNK].astype(F32) + got_ref[chip, :CHUNK].astype(F32)
        out_ref[chip, :CHUNK] = total.astype(B16)
        out_ref[chip, CHUNK : CHUNK + PIECE] = keep_ref[chip, CHUNK:]
        out_ref[chip, CHUNK + PIECE :] = got_ref[chip, CHUNK:]


def sum_kernel(got_ref, out_ref):
    total = got_ref[0, :CHUNK].astype(F32)
    for chip in range(1, CHIPS):
        total = total + got_ref[chip, :CHUNK].astype(F32)
    out_ref[...] = total.astype(B16)


def four(refs):
    own, first, second, third = (ref[...].astype(F32) for ref in refs)
    return ((own + first) + (second + third)).astype(B16)


def round_kernel(own_ref, first_ref, second_ref, third_ref, out_ref):
    out_ref[...] = four((own_ref, first_ref, second_ref, third_ref))


def last_round_kernel(own_ref, first_ref, second_ref, third_ref, out_ref, gains_ref):
    total = four((own_ref, first_ref, second_ref, third_ref))
    for chip in range(CHIPS):
        out_ref[chip] = total[:ROWS]
    gains_ref[...] = total[ROWS:]


def home_kernel(core_ref, got_ref, grad_ref, out_ref):
    core = core_ref[0]
    for chip in range(CHIPS):
        for part in range(2):
            index = 2 * chip + (core if part == 0 else 1 - core)
            there = pl.ds(pl.multiple_of(index * SPREAD, SPREAD), SPREAD)
            first = CHUNK + part * PIECE
            for own in range(OWN):
                moved = got_ref[chip, first + own * SPREAD : first + (own + 1) * SPREAD]
                out_ref[own, there] = grad_ref[own, there].astype(F32) + moved.astype(F32)


def final_kernel(
    scale, core_ref, mine_ref, theirs_ref, gains_ref, q_ref, k_ref, v_ref, o_ref, up_ref, down_ref, g1_ref, g2_ref
):
    core = core_ref[0]

    def fill(low_ref, high_ref):
        def low(index):
            return low_ref[index * WIDTH : (index + 1) * WIDTH].astype(F32) * scale

        def high(index):
            return high_ref[index * WIDTH : (index + 1) * WIDTH].astype(F32) * scale

        for index, ref in enumerate((q_ref, k_ref, v_ref, o_ref)):
            ref[...] = low(index)
        for index in range(2):
            up_ref[:, index * WIDTH : (index + 1) * WIDTH] = low(4 + index)
            up_ref[:, (2 + index) * WIDTH : (3 + index) * WIDTH] = high(index)
        for index in range(4):
            down_ref[index * WIDTH : (index + 1) * WIDTH] = high(2 + index)

    @pl.when(core == 0)
    def _():
        fill(mine_ref, theirs_ref)

    @pl.when(core != 0)
    def _():
        fill(theirs_ref, mine_ref)

    gains = gains_ref[...].astype(F32) * scale
    g1_ref[...] = gains[0:1]
    g2_ref[...] = gains[1:2]


def local(kernel, out_shape, specs, *operands):
    return pl.pallas_call(
        kernel,
        out_shape=out_shape,
        in_specs=specs,
        out_specs=jax.tree.map(lambda _: VMEM, out_shape),
        compiler_params=pltpu.CompilerParams(vmem_limit_bytes=32 * 1024 * 1024),
    )(*operands)


def shaped(*shape, dtype=B16):
    return jax.ShapeDtypeStruct(shape, dtype)


def swap(array, axis, groups=None):
    return lax.all_to_all(
        array, axis, split_axis=0, concat_axis=0, tiled=True, axis_index_groups=groups
    )


def on_device(
    layer_input, out_grad, norm1_gain, w_query, w_key, w_value, w_out, norm2_gain, w_up, w_down
):
    members = lax.axis_size("member")
    spaces = lax.axis_size("space")
    core = (lax.axis_index("member") % 2).astype(jnp.int32).reshape(1)
    other_core = [(k, k ^ 1) for k in range(members)]
    same_core = [[c + 2 * k for k in range(CHIPS)] for c in range(2)]

    def across(array, steps):
        return [lax.ppermute(array, "space", [(k, k ^ step) for k in range(spaces)]) for step in steps]

    both = swap(pack(layer_input, out_grad), "member")
    wqkv = jnp.concatenate([w_query, w_key, w_value], axis=1)
    keep, give = run_layer(
        core, both, norm1_gain.reshape(1, WIDTH), wqkv, w_out, norm2_gain.reshape(1, WIDTH), w_up, w_down
    )
    got = lax.ppermute(give, "member", other_core)
    sent = local(pair_kernel, shaped(CHIPS, CHUNK + 2 * PIECE, WIDTH), [VMEM] * 2, keep, got)
    got = swap(sent, "member", same_core)
    input_grad = local(
        home_kernel, shaped(OWN, GROUPS * SPREAD, WIDTH, dtype=F32), [SMEM, VMEM, VMEM], core, got, out_grad
    )
    chunk = shaped(CHUNK, WIDTH)
    total = local(sum_kernel, chunk, [VMEM], got)
    total = local(round_kernel, chunk, [VMEM] * 4, total, *across(total, (1, 8, 9)))
    sent, gains = local(
        last_round_kernel,
        (shaped(CHIPS, ROWS, WIDTH), shaped(GAIN_ROWS, WIDTH)),
        [VMEM] * 4,
        total,
        *across(total, (2, 4, 6)),
    )
    mine = swap(sent, "member", same_core).reshape(CHIPS * ROWS, WIDTH)
    theirs = lax.ppermute(mine, "member", other_core)
    scale = 1.0 / math.sqrt(MEMBERS * GROUPS * SPREAD * spaces)
    square = shaped(WIDTH, WIDTH, dtype=F32)
    row = shaped(1, WIDTH, dtype=F32)
    grads = local(
        functools.partial(final_kernel, scale),
        (square, square, square, square, shaped(WIDTH, HIDDEN, dtype=F32), shaped(HIDDEN, WIDTH, dtype=F32), row, row),
        [SMEM, VMEM, VMEM, VMEM],
        core,
        mine,
        theirs,
        gains,
    )
    return (input_grad, *grads[:6], grads[6].reshape(WIDTH), grads[7].reshape(WIDTH))


def solution(mesh):
    in_specs = (
        P("member", "space", None),
        P("member", "space", None),
        P(),
        P(),
        P(),
        P(),
        P(),
        P(),
        P(),
        P(),
    )
    out_specs = (P("member", "space", None), P(), P(), P(), P(), P(), P(), P(), P())
    return jax.shard_map(
        on_device, mesh=mesh, in_specs=in_specs, out_specs=out_specs, check_vma=False
    )
```

time: 127 us -> 109 us (0.86)
  blocking collectives: 63.8 us -> 32.5 us
  starting transfers between devices: 13 us -> 27.9 us
  waiting for transfers between devices: 18.9 us -> 30 us
  Pallas kernels: 28 us -> 17.8 us
  local copies, waits for them, and re-layouts: 2.14 us -> 0.06 us
    all_to_all x4 -> x2, blocking collectives: 63.8 us -> 32.5 us  [swap(): lax.all_to_all(array, axis, split_axis=0, concat_axis=0, tiled=True, axis...]
    ppermute x0 -> x6, starting transfers between devices: none -> 12.7 us  [across(): lax.ppermute(array, 'space', [(k, k ^ step) for k in range(spaces)])]
    pallas_call x1, Pallas kernels: 23.5 us -> 12 us  [run_layer(): pl.pallas_call(layer_kernel, out_shape=(shape, shape), in_specs=[SMEM] +...]
    ppermute x0 -> x6, waiting for transfers between devices: none -> 11.1 us  [across(): lax.ppermute(array, 'space', [(k, k ^ step) for k in range(spaces)])]
    pallas_call x0 -> x1, Pallas kernels: none -> 2.43 us  [pack(): pl.pallas_call(pack_kernel, out_shape=shaped(GROUPS, 2, OWN, SPREAD, WIDT...]
    unnamed x22 -> x18, local copies, waits for them, and re-layouts: 2.12 us -> 0.06 us
    ppermute x1, starting transfers between devices: 4.96 us -> 7.02 us  [on_device(): theirs = lax.ppermute(mine, 'member', other_core)]
  transfers between devices with their start and end apart: 3 -> 9, of which waited for: 3 -> 7; matrix products, arithmetic and copies ran while one was open for 0% -> 0% of each run, Pallas kernels for 1% -> 1%
where the time goes in v3:
time: 109 us
  blocking collectives  32.5 us (30%)
  waiting for transfers between devices  30 us (28%)
  starting transfers between devices  27.9 us (26%)
  Pallas kernels  17.8 us (16%)
    all_to_all x2, blocking collectives, swap(): lax.all_to_all(array, axis, split_axis=0, concat_axis=0, tiled=True, axis...  32.5 us
    all_to_all x1, waiting for transfers between devices, swap(): lax.all_to_all(array, axis, split_axis=0, concat_axis=0, tiled=True, axis...  15.8 us
    ppermute x6, starting transfers between devices, across(): lax.ppermute(array, 'space', [(k, k ^ step) for k in range(spaces)])  12.7 us
    pallas_call x1, Pallas kernels, run_layer(): pl.pallas_call(layer_kernel, out_shape=(shape, shape), in_specs=[SMEM] +...  12 us
    ppermute x6, waiting for transfers between devices, across(): lax.ppermute(array, 'space', [(k, k ^ step) for k in range(spaces)])  11.1 us
    all_to_all x1, starting transfers between devices, swap(): lax.all_to_all(array, axis, split_axis=0, concat_axis=0, tiled=True, axis...  7.06 us
    ppermute x1, starting transfers between devices, on_device(): theirs = lax.ppermute(mine, 'member', other_core)  7.02 us
    pallas_call x6, Pallas kernels, local(): pl.pallas_call(kernel, out_shape=out_shape, in_specs=specs, out_specs=jax...  3.38 us
  transfers between devices with their start and end apart: 9, of which 7 were waited for; matrix products, arithmetic and copies ran while one was open for 0% of the time, Pallas kernels for 1%

profile of v3, /device:TPU:1, one launch (start us, length us, event | category | flops | bytes accessed | tf_op | source)
XLA Modules:
  0.0 109.1 jit_solution(17140204983460819788)
XLA Ops:
  0.6 2.4 %shard_map.169 = bf16[16,2,4,16,256]{4,3,2,1,0:T(8,128)(2,1)} custom-call(bf16[4,256,256]{2,1,0:T(8,128)(2,1)} %input_ref.1, bf16[4,256,256]{2,1,0:T(8,128)(2,1)} %grad_ref.3), custom_call_target="tpu_custom_call" | custom-call | tf_op jit(solution)/shard_map/pallas_call | solution.py:308
  3.1 0.0 copy-start.6
  3.1 0.0 copy-start.7
  3.1 0.0 copy-start.8
  3.1 0.0 copy-start.1
  3.1 0.0 copy-start.3
  3.1 0.0 copy-start.4
  3.2 7.1 %all-to-all-start = ((bf16[16,2,4,16,256]{4,3,2,1,0:T(8,128)(2,1)}), bf16[16,2,4,16,256]{4,3,2,1,0:T(8,128)(2,1)S(1)}, u32[]{:S(2)}, u32[]{:S(2)}) async-start(bf16[16,2,4,16,256]{4,3,2,1,0:T(8,128)(2,1)} %shard_map.169), calls=%async_computation | async-start | bytes 2097152 | tf_op jit(solution)/shard_map/all_to_all | solution.py:408
  10.3 15.8 %all-to-all-done.both_ref = bf16[16,2,4,16,256]{4,3,2,1,0:T(8,128)(2,1)S(1)} async-done(((bf16[16,2,4,16,256]{4,3,2,1,0:T(8,128)(2,1)}), bf16[16,2,4,16,256]{4,3,2,1,0:T(8,128)(2,1)S(1)}, u32[]{:S(2)}, u32[]{:S(2)}) %all-to-all-start) | async-done | bytes 1048608 | tf_op jit(solution)/shard_map/all_to_all | solution.py:408
  26.1 12.0 %shard_map.170 = (bf16[8,264,256]{2,1,0:T(8,128)(2,1)S(1)}, bf16[8,264,256]{2,1,0:T(8,128)(2,1)S(1)}) custom-call(s32[1]{0:T(128)} %bitcast.core_ref, bf16[16,2,4,16,256]{4,3,2,1,0:T(8,128)(2,1)S(1)} %all-to-all-done.both_ref, f32[1,256]{1,0:T(1,128)S(1)} %bitcast.8, bf16[256,768]{1,0:T(8,128)(2,1)S(1)} %pad_maximum_fusion.wqkv_ref, ...), custom_call_target="tpu_custom_call" | custom-call | flops 5000000000 | bytes 6000000 | tf_op jit(solution)/shard_map/pallas_call | solution.py:282
  38.1 1.1 %collective-permute-start = (bf16[8,264,256]{2,1,0:T(8,128)(2,1)S(1)}, bf16[8,264,256]{2,1,0:T(8,128)(2,1)S(1)}, u32[]{:S(2)}, u32[]{:S(2)}) collective-permute-start(bf16[8,264,256]{2,1,0:T(8,128)(2,1)S(1)} %get-tuple-element.22), channel_id=1, source_target_pairs={{0,16},{16,0},{32,48},{48,32},{64,80},{80,64},{96,112},{112,96},{1... | collective-permute-start | bytes 3244040 | tf_op jit(solution)/shard_map/ppermute | solution.py:430
  39.2 2.3 %collective-permute-done.got_ref = bf16[8,264,256]{2,1,0:T(8,128)(2,1)S(1)} collective-permute-done((bf16[8,264,256]{2,1,0:T(8,128)(2,1)S(1)}, bf16[8,264,256]{2,1,0:T(8,128)(2,1)S(1)}, u32[]{:S(2)}, u32[]{:S(2)}) %collective-permute-start) | collective-permute-done | bytes 1081376 | tf_op jit(solution)/shard_map/ppermute | solution.py:430
  41.6 0.2 shard_map.171
  41.8 21.1 %all_to_all.15.got_ref = bf16[8,328,256]{2,1,0:T(8,128)(2,1)S(1)} all-to-all(bf16[8,328,256]{2,1,0:T(8,128)(2,1)S(1)} %shard_map.171), channel_id=1, replica_groups={{0,32,64,96,128,160,192,224},{16,48,80,112,144,176,208,240},{1,33,65,97..., dimensions={0} | all-to-all | bytes 2686976 | tf_op jit(solution)/shard_map/all_to_all | solution.py:408
  62.9 0.1 shard_map.173.own_ref
  63.0 3.9 %collective-permute-start.3 = (bf16[200,256]{1,0:T(8,128)(2,1)S(1)}, bf16[200,256]{1,0:T(8,128)(2,1)S(1)}, u32[]{:S(2)}, u32[]{:S(2)}) collective-permute-start(bf16[200,256]{1,0:T(8,128)(2,1)S(1)} %shard_map.173.own_ref), channel_id=1, source_target_pairs={{0,9},{1,8},{2,11},{3,10},{4,13},{5,12},{6,15},{7,14},{8,1},{9,0},... | collective-permute-start | bytes 307208 | tf_op jit(solution)/shard_map/ppermute | solution.py:423
  66.9 0.5 collective-permute-start.2
  67.4 1.6 %collective-permute-done.3.third_ref = bf16[200,256]{1,0:T(8,128)(2,1)S(1)} collective-permute-done((bf16[200,256]{1,0:T(8,128)(2,1)S(1)}, bf16[200,256]{1,0:T(8,128)(2,1)S(1)}, u32[]{:S(2)}, u32[]{:S(2)}) %collective-permute-start.3) | collective-permute-done | bytes 102432 | tf_op jit(solution)/shard_map/ppermute | solution.py:423
  69.0 2.9 %collective-permute-done.2.second_ref = bf16[200,256]{1,0:T(8,128)(2,1)S(1)} collective-permute-done((bf16[200,256]{1,0:T(8,128)(2,1)S(1)}, bf16[200,256]{1,0:T(8,128)(2,1)S(1)}, u32[]{:S(2)}, u32[]{:S(2)}) %collective-permute-start.2) | collective-permute-done | bytes 102432 | tf_op jit(solution)/shard_map/ppermute | solution.py:423
  71.9 0.1 shard_map.174.own_ref
  72.0 0.0 copy-start
  72.0 6.1 %collective-permute-start.6 = (bf16[200,256]{1,0:T(8,128)(2,1)S(1)}, bf16[200,256]{1,0:T(8,128)(2,1)S(1)}, u32[]{:S(2)}, u32[]{:S(2)}) collective-permute-start(bf16[200,256]{1,0:T(8,128)(2,1)S(1)} %shard_map.174.own_ref), channel_id=1, source_target_pairs={{0,6},{1,7},{2,4},{3,5},{4,2},{5,3},{6,0},{7,1},{8,14},{9,15},{10,... | collective-permute-start | bytes 307208 | tf_op jit(solution)/shard_map/ppermute | solution.py:423
  78.0 1.0 collective-permute-start.5
  79.0 1.2 %collective-permute-start.4 = (bf16[200,256]{1,0:T(8,128)(2,1)S(1)}, bf16[200,256]{1,0:T(8,128)(2,1)S(1)}, u32[]{:S(2)}, u32[]{:S(2)}) collective-permute-start(bf16[200,256]{1,0:T(8,128)(2,1)S(1)} %shard_map.174.own_ref), channel_id=1, source_target_pairs={{0,2},{1,3},{2,0},{3,1},{4,6},{5,7},{6,4},{7,5},{8,10},{9,11},{10,... | collective-permute-start | bytes 307208 | tf_op jit(solution)/shard_map/ppermute | solution.py:423
  80.2 3.6 %collective-permute-done.6.third_ref = bf16[200,256]{1,0:T(8,128)(2,1)S(1)} collective-permute-done((bf16[200,256]{1,0:T(8,128)(2,1)S(1)}, bf16[200,256]{1,0:T(8,128)(2,1)S(1)}, u32[]{:S(2)}, u32[]{:S(2)}) %collective-permute-start.6) | collective-permute-done | bytes 102432 | tf_op jit(solution)/shard_map/ppermute | solution.py:423
  83.8 3.1 %collective-permute-done.5.second_ref = bf16[200,256]{1,0:T(8,128)(2,1)S(1)} collective-permute-done((bf16[200,256]{1,0:T(8,128)(2,1)S(1)}, bf16[200,256]{1,0:T(8,128)(2,1)S(1)}, u32[]{:S(2)}, u32[]{:S(2)}) %collective-permute-start.5) | collective-permute-done | bytes 102432 | tf_op jit(solution)/shard_map/ppermute | solution.py:423
  86.8 0.1 shard_map.175
  86.9 11.4 %all_to_all.16 = bf16[8,192,256]{2,1,0:T(8,128)(2,1)S(1)} all-to-all(bf16[8,192,256]{2,1,0:T(8,128)(2,1)S(1)} %get-tuple-element.23), channel_id=1, replica_groups={{0,32,64,96,128,160,192,224},{16,48,80,112,144,176,208,240},{1,33,65,97..., dimensions={0} | all-to-all | bytes 1572864 | tf_op jit(solution)/shard_map/all_to_all | solution.py:408
  98.3 7.0 %collective-permute-start.7 = (bf16[1536,256]{1,0:T(8,128)(2,1)S(1)}, bf16[1536,256]{1,0:T(8,128)(2,1)S(1)}, u32[]{:S(2)}, u32[]{:S(2)}) collective-permute-start(bf16[1536,256]{1,0:T(8,128)(2,1)S(1)} %bitcast.6), channel_id=1, source_target_pairs={{0,16},{16,0},{32,48},{48,32},{64,80},{80,64},{96,112},{112,96},{1... | collective-permute-start | bytes 2359304 | tf_op jit(solution)/shard_map/ppermute | solution.py:447
  105.3 1.1 %shard_map.172 = f32[4,256,256]{2,1,0:T(8,128)} custom-call(s32[1]{0:T(128)} %bitcast.core_ref, bf16[8,328,256]{2,1,0:T(8,128)(2,1)S(1)} %all_to_all.15.got_ref, bf16[4,256,256]{2,1,0:T(8,128)(2,1)S(1)} %copy-done), custom_call_target="tpu_custom_call" | custom-call | tf_op jit(solution)/shard_map/pallas_call | solution.py:394
  106.4 0.8 collective-permute-done.7.theirs_ref
  107.2 1.9 %shard_map.176 = (f32[256,256]{1,0:T(8,128)}, f32[256,256]{1,0:T(8,128)}, f32[256,256]{1,0:T(8,128)}, f32[256,256]{1,0:T(8,128)}, f32[256,1024]{1,0:T(8,128)}, /...) custom-call(s32[1]{0:T(128)} %bitcast.core_ref, bf16[1536,256]{1,0:T(8,128)(2,1)S(1)} %bitcast.7, ...), custom_call_target="tpu_custom_call" | custom-call | tf_op jit(solution)/shard_map/pallas_call | solution.py:394
  (15 shorter events, 0.1 us)
Async XLA Ops:
  3.1 7.2 %copy-start.6 = (bf16[256,256]{1,0:T(8,128)(2,1)S(1)}, bf16[256,256]{1,0:T(8,128)(2,1)}, u32[]{:S(2)}) copy-start(bf16[256,256]{1,0:T(8,128)(2,1)} %param.15) | copy-start | bytes 393220
  3.1 7.2 %copy-start.7 = (bf16[256,256]{1,0:T(8,128)(2,1)S(1)}, bf16[256,256]{1,0:T(8,128)(2,1)}, u32[]{:S(2)}) copy-start(bf16[256,256]{1,0:T(8,128)(2,1)} %param.14) | copy-start | bytes 393220
  3.1 7.1 %copy-start.8 = (bf16[256,256]{1,0:T(8,128)(2,1)S(1)}, bf16[256,256]{1,0:T(8,128)(2,1)}, u32[]{:S(2)}) copy-start(bf16[256,256]{1,0:T(8,128)(2,1)} %param.13) | copy-start | bytes 393220
  3.1 22.9 %copy-start.1 = (bf16[256,1024]{1,0:T(8,128)(2,1)S(1)}, bf16[256,1024]{1,0:T(8,128)(2,1)}, u32[]{:S(2)}) copy-start(bf16[256,1024]{1,0:T(8,128)(2,1)} %wup_ref.1) | copy-start | bytes 1572868
  3.1 22.9 %copy-start.2 = (bf16[1024,256]{1,0:T(8,128)(2,1)S(1)}, bf16[1024,256]{1,0:T(8,128)(2,1)}, u32[]{:S(2)}) copy-start(bf16[1024,256]{1,0:T(8,128)(2,1)} %wdown_ref.1) | copy-start | bytes 1572868
  3.1 22.9 %copy-start.3 = (bf16[256,256]{1,0:T(8,128)(2,1)S(1)}, bf16[256,256]{1,0:T(8,128)(2,1)}, u32[]{:S(2)}) copy-start(bf16[256,256]{1,0:T(8,128)(2,1)} %wout_ref.1) | copy-start | bytes 393220
  3.1 22.9 %copy-start.4 = (f32[256]{0:T(256)S(1)}, f32[256]{0:T(256)}, u32[]{:S(2)}) copy-start(f32[256]{0:T(256)} %param.12) | copy-start | bytes 3076
  3.2 22.9 %copy-start.5 = (f32[256]{0:T(256)S(1)}, f32[256]{0:T(256)}, u32[]{:S(2)}) copy-start(f32[256]{0:T(256)} %param.17) | copy-start | bytes 3076
  3.2 22.9 %all-to-all-start = ((bf16[16,2,4,16,256]{4,3,2,1,0:T(8,128)(2,1)}), bf16[16,2,4,16,256]{4,3,2,1,0:T(8,128)(2,1)S(1)}, u32[]{:S(2)}, u32[]{:S(2)}) async-start(bf16[16,2,4,16,256]{4,3,2,1,0:T(8,128)(2,1)} %shard_map.169), calls=%async_computation | async-start | bytes 2097152 | tf_op jit(solution)/shard_map/all_to_all | solution.py:408
  38.1 3.5 %collective-permute-start = (bf16[8,264,256]{2,1,0:T(8,128)(2,1)S(1)}, bf16[8,264,256]{2,1,0:T(8,128)(2,1)S(1)}, u32[]{:S(2)}, u32[]{:S(2)}) collective-permute-start(bf16[8,264,256]{2,1,0:T(8,128)(2,1)S(1)} %get-tuple-element.22), channel_id=1, source_target_pairs={{0,16},{16,0},{32,48},{48,32},{64,80},{80,64},{96,112},{112,96},{1... | collective-permute-start | bytes 3244040 | tf_op jit(solution)/shard_map/ppermute | solution.py:430
  63.0 6.0 %collective-permute-start.3 = (bf16[200,256]{1,0:T(8,128)(2,1)S(1)}, bf16[200,256]{1,0:T(8,128)(2,1)S(1)}, u32[]{:S(2)}, u32[]{:S(2)}) collective-permute-start(bf16[200,256]{1,0:T(8,128)(2,1)S(1)} %shard_map.173.own_ref), channel_id=1, source_target_pairs={{0,9},{1,8},{2,11},{3,10},{4,13},{5,12},{6,15},{7,14},{8,1},{9,0},... | collective-permute-start | bytes 307208 | tf_op jit(solution)/shard_map/ppermute | solution.py:423
  66.9 5.0 %collective-permute-start.2 = (bf16[200,256]{1,0:T(8,128)(2,1)S(1)}, bf16[200,256]{1,0:T(8,128)(2,1)S(1)}, u32[]{:S(2)}, u32[]{:S(2)}) collective-permute-start(bf16[200,256]{1,0:T(8,128)(2,1)S(1)} %shard_map.173.own_ref), channel_id=1, source_target_pairs={{0,8},{1,9},{2,10},{3,11},{4,12},{5,13},{6,14},{7,15},{8,0},{9,1},... | collective-permute-start | bytes 307208 | tf_op jit(solution)/shard_map/ppermute | solution.py:423
  67.4 4.5 %collective-permute-start.1 = (bf16[200,256]{1,0:T(8,128)(2,1)S(1)}, bf16[200,256]{1,0:T(8,128)(2,1)S(1)}, u32[]{:S(2)}, u32[]{:S(2)}) collective-permute-start(bf16[200,256]{1,0:T(8,128)(2,1)S(1)} %shard_map.173.own_ref), channel_id=1, source_target_pairs={{0,1},{1,0},{2,3},{3,2},{4,5},{5,4},{6,7},{7,6},{8,9},{9,8},{10,11... | collective-permute-start | bytes 307208 | tf_op jit(solution)/shard_map/ppermute | solution.py:423
  72.0 33.3 %copy-start = (bf16[4,256,256]{2,1,0:T(8,128)(2,1)S(1)}, bf16[4,256,256]{2,1,0:T(8,128)(2,1)}, u32[]{:S(2)}) copy-start(bf16[4,256,256]{2,1,0:T(8,128)(2,1)} %grad_ref.3) | copy-start | bytes 1572868
  72.0 11.8 %collective-permute-start.6 = (bf16[200,256]{1,0:T(8,128)(2,1)S(1)}, bf16[200,256]{1,0:T(8,128)(2,1)S(1)}, u32[]{:S(2)}, u32[]{:S(2)}) collective-permute-start(bf16[200,256]{1,0:T(8,128)(2,1)S(1)} %shard_map.174.own_ref), channel_id=1, source_target_pairs={{0,6},{1,7},{2,4},{3,5},{4,2},{5,3},{6,0},{7,1},{8,14},{9,15},{10,... | collective-permute-start | bytes 307208 | tf_op jit(solution)/shard_map/ppermute | solution.py:423
  78.0 8.8 %collective-permute-start.5 = (bf16[200,256]{1,0:T(8,128)(2,1)S(1)}, bf16[200,256]{1,0:T(8,128)(2,1)S(1)}, u32[]{:S(2)}, u32[]{:S(2)}) collective-permute-start(bf16[200,256]{1,0:T(8,128)(2,1)S(1)} %shard_map.174.own_ref), channel_id=1, source_target_pairs={{0,4},{1,5},{2,6},{3,7},{4,0},{5,1},{6,2},{7,3},{8,12},{9,13},{10,... | collective-permute-start | bytes 307208 | tf_op jit(solution)/shard_map/ppermute | solution.py:423
  79.0 7.8 %collective-permute-start.4 = (bf16[200,256]{1,0:T(8,128)(2,1)S(1)}, bf16[200,256]{1,0:T(8,128)(2,1)S(1)}, u32[]{:S(2)}, u32[]{:S(2)}) collective-permute-start(bf16[200,256]{1,0:T(8,128)(2,1)S(1)} %shard_map.174.own_ref), channel_id=1, source_target_pairs={{0,2},{1,3},{2,0},{3,1},{4,6},{5,7},{6,4},{7,5},{8,10},{9,11},{10,... | collective-permute-start | bytes 307208 | tf_op jit(solution)/shard_map/ppermute | solution.py:423
  98.3 8.9 %collective-permute-start.7 = (bf16[1536,256]{1,0:T(8,128)(2,1)S(1)}, bf16[1536,256]{1,0:T(8,128)(2,1)S(1)}, u32[]{:S(2)}, u32[]{:S(2)}) collective-permute-start(bf16[1536,256]{1,0:T(8,128)(2,1)S(1)} %bitcast.6), channel_id=1, source_target_pairs={{0,16},{16,0},{32,48},{48,32},{64,80},{80,64},{96,112},{112,96},{1... | collective-permute-start | bytes 2359304 | tf_op jit(solution)/shard_map/ppermute | solution.py:447

commit v4 on v3

--- a/solution.py
+++ b/solution.py
@@ -36,7 +36,7 @@
 F32 = jnp.float32
 B16 = jnp.bfloat16
 VMEM = pl.BlockSpec(memory_space=pltpu.VMEM)
-ANY = pl.BlockSpec(memory_space=pl.ANY)
+HBM = pl.BlockSpec(memory_space=pltpu.HBM)
 SMEM = pl.BlockSpec(memory_space=pltpu.SMEM)
 
 
@@ -213,6 +213,16 @@
         keep_grad(1, patch, side, jnp.dot(dscore, expanded[patch, side], preferred_element_type=F32))
         keep_grad(0, patch, side, own_heads(dot(dscore, part(qkv, 1, patch, side), (0, 0))))
 
+    def keep_part(first, total):
+        rows = total.shape[0] // 2
+        for half in range(2):
+            parts[half, first : first + rows] = total[half * rows : (half + 1) * rows].astype(B16)
+
+    for i in range(HIDDEN // WIDTH):
+        lanes = slice(i * WIDTH, (i + 1) * WIDTH)
+        keep_part(4 * HALF + i * HALF, dot(n2s[...], gpre[:, lanes], (0, 0)))
+        first = 8 * HALF + i % 2 * WIDTH
+        parts[i // 2, first : first + WIDTH] = dot(ogs[...], acts[:, lanes], (0, 0)).T.astype(B16)
     staged((meet, bend, finish))
     products[...] = dot(gqkv[...], wqkv_ref[...], (1, 1))
     gain1_sum = jnp.zeros((MEMBERS, WIDTH), F32)
@@ -223,18 +233,10 @@
         for side, lanes in enumerate(halves):
             ds[side, pl.ds(patch, MEMBERS, stride=SPREAD), :] = delta[:, lanes]
 
+    part_qkv = dot(n1s[...], gqkv[...], (0, 0))
     for i in range(3):
-        parts[i * WIDTH : (i + 1) * WIDTH] = dot(
-            n1s[...], gqkv[:, i * WIDTH : (i + 1) * WIDTH], (0, 0)
-        ).astype(B16)
-    parts[3 * WIDTH : 4 * WIDTH] = dot(mixs[...], gas[...], (0, 0)).astype(B16)
-    for i in range(4):
-        parts[(4 + i) * WIDTH : (5 + i) * WIDTH] = dot(
-            n2s[...], gpre[:, i * WIDTH : (i + 1) * WIDTH], (0, 0)
-        ).astype(B16)
-    for i in range(4):
-        part_down = dot(ogs[...], acts[:, i * WIDTH : (i + 1) * WIDTH], (0, 0))
-        parts[(8 + i) * WIDTH : (9 + i) * WIDTH] = part_down.T.astype(B16)
+        keep_part(i * HALF, part_qkv[:, i * WIDTH : (i + 1) * WIDTH])
+    keep_part(3 * HALF, dot(mixs[...], gas[...], (0, 0)))
     gain_rows = jnp.concatenate(
         [jnp.sum(total, axis=0, keepdims=True) for total in (gain1_sum, gain2_sum)]
         + [jnp.zeros((GAIN_ROWS - 2, WIDTH), F32)],
@@ -242,8 +244,7 @@
     ).astype(B16)
     for target, side in ((keep_ref, core), (give_ref, 1 - core)):
         for chip in range(CHIPS):
-            start = pl.multiple_of(side * (CHIPS * ROWS) + chip * ROWS, ROWS)
-            target[chip, :ROWS] = parts[pl.ds(start, ROWS)]
+            target[chip, :ROWS] = parts[side, chip * ROWS : (chip + 1) * ROWS]
             target[chip, ROWS:CHUNK] = gain_rows
             start = pl.multiple_of((2 * chip + side) * PIECE, PIECE)
             for half, lanes in enumerate(halves):
@@ -276,7 +277,7 @@
         pltpu.VMEM(rows, F32),
         pltpu.VMEM(rows, F32),
         pltpu.VMEM((2, 2, *rows), F32),
-        pltpu.VMEM((2 * CHIPS * ROWS, WIDTH), B16),
+        pltpu.VMEM((2, CHIPS * ROWS, WIDTH), B16),
     ]
     shape = shaped(CHIPS, CHUNK + PIECE, WIDTH)
     return pl.pallas_call(
@@ -290,27 +291,40 @@
     )(core, both, gain1, wqkv, wout, gain2, wup, wdown)
 
 
-def pack_kernel(input_ref, grad_ref, out_ref, sems):
-    copies = []
-    for group in range(GROUPS):
-        there = slice(group * SPREAD, (group + 1) * SPREAD)
+def pack_kernel(input_ref, grad_ref, out_ref, held, in_sems, out_sems):
+    pairs = []
+    for own in range(OWN):
         for side, ref in enumerate((input_ref, grad_ref)):
-            copies.append(
-                pltpu.make_async_copy(ref.at[:, there], out_ref.at[group, side], sems.at[group, side])
+            pairs.append(
+                (
+                    pltpu.make_async_copy(ref.at[own], held.at[side, own], in_sems.at[side, own]),
+                    pltpu.make_async_copy(
+                        held.at[side, own].reshape(GROUPS, SPREAD, WIDTH),
+                        out_ref.at[:, side, own],
+                        out_sems.at[side, own],
+                    ),
+                )
             )
-    for copy in copies:
-        copy.start()
-    for copy in copies:
-        copy.wait()
+    for arrive, _ in pairs:
+        arrive.start()
+    for arrive, leave in pairs:
+        arrive.wait()
+        leave.start()
+    for _, leave in pairs:
+        leave.wait()
 
 
 def pack(layer_input, out_grad):
     return pl.pallas_call(
         pack_kernel,
         out_shape=shaped(GROUPS, 2, OWN, SPREAD, WIDTH),
-        in_specs=[ANY, ANY],
-        out_specs=VMEM,
-        scratch_shapes=[pltpu.SemaphoreType.DMA((GROUPS, 2))],
+        in_specs=[HBM, HBM],
+        out_specs=HBM,
+        scratch_shapes=[
+            pltpu.VMEM((2, OWN, GROUPS * SPREAD, WIDTH), B16),
+            pltpu.SemaphoreType.DMA((2, OWN)),
+            pltpu.SemaphoreType.DMA((2, OWN)),
+        ],
     )(layer_input, out_grad)
 
 
@@ -338,14 +352,16 @@
     out_ref[...] = four((own_ref, first_ref, second_ref, third_ref))
 
 
-def last_round_kernel(own_ref, first_ref, second_ref, third_ref, out_ref, gains_ref):
+def last_round_kernel(own_ref, first_ref, second_ref, third_ref, done_ref, out_ref, gains_ref):
+    del done_ref
     total = four((own_ref, first_ref, second_ref, third_ref))
     for chip in range(CHIPS):
         out_ref[chip] = total[:ROWS]
     gains_ref[...] = total[ROWS:]
 
 
-def home_kernel(core_ref, got_ref, grad_ref, out_ref):
+def home_kernel(core_ref, got_ref, grad_ref, out_ref, done_ref):
+    done_ref[...] = jnp.zeros_like(done_ref)
     core = core_ref[0]
     for chip in range(CHIPS):
         for part in range(2):
@@ -357,37 +373,44 @@
                 out_ref[own, there] = grad_ref[own, there].astype(F32) + moved.astype(F32)
 
 
-def final_kernel(
-    scale, core_ref, mine_ref, theirs_ref, gains_ref, q_ref, k_ref, v_ref, o_ref, up_ref, down_ref, g1_ref, g2_ref
-):
-    core = core_ref[0]
-
-    def fill(low_ref, high_ref):
-        def low(index):
-            return low_ref[index * WIDTH : (index + 1) * WIDTH].astype(F32) * scale
-
-        def high(index):
-            return high_ref[index * WIDTH : (index + 1) * WIDTH].astype(F32) * scale
-
-        for index, ref in enumerate((q_ref, k_ref, v_ref, o_ref)):
-            ref[...] = low(index)
-        for index in range(2):
-            up_ref[:, index * WIDTH : (index + 1) * WIDTH] = low(4 + index)
-            up_ref[:, (2 + index) * WIDTH : (3 + index) * WIDTH] = high(index)
-        for index in range(4):
-            down_ref[index * WIDTH : (index + 1) * WIDTH] = high(2 + index)
-
-    @pl.when(core == 0)
-    def _():
-        fill(mine_ref, theirs_ref)
-
-    @pl.when(core != 0)
-    def _():
-        fill(theirs_ref, mine_ref)
-
-    gains = gains_ref[...].astype(F32) * scale
-    g1_ref[...] = gains[0:1]
-    g2_ref[...] = gains[1:2]
+def write_half(scale, side, part_ref, out_refs, held, held_up, sems):
+    copies = []
+
+    def send(source, out_ref, rows, index):
+        there = pl.ds(pl.multiple_of(side * rows, rows), rows)
+        copies.append(pltpu.make_async_copy(source, out_ref.at[there], sems.at[index]))
+        copies[-1].start()
+
+    for index in range(4):
+        rows = slice(index * HALF, (index + 1) * HALF)
+        held[rows] = part_ref[rows].astype(F32) * scale
+        send(held.at[rows], out_refs[index], HALF, index)
+    for index in range(HIDDEN // WIDTH):
+        first = (4 + index) * HALF
+        held_up[:, index * WIDTH : (index + 1) * WIDTH] = part_ref[first : first + HALF].astype(F32) * scale
+    send(held_up, out_refs[4], HALF, 4)
+    rows = slice(8 * HALF, 12 * HALF)
+    held[rows] = part_ref[rows].astype(F32) * scale
+    send(held.at[rows], out_refs[5], 4 * HALF, 5)
+    for copy in copies:
+        copy.wait()
+
+
+def mine_kernel(scale, core_ref, part_ref, gains_ref, *refs):
+    refs[6][...] = gains_ref[0:1].astype(F32) * scale
+    refs[7][...] = gains_ref[1:2].astype(F32) * scale
+    write_half(scale, core_ref[0], part_ref, refs[:6], *refs[8:])
+
+
+def theirs_kernel(scale, core_ref, part_ref, *refs):
+    write_half(scale, 1 - core_ref[0], part_ref, refs[6:12], *refs[12:])
+
+
+FINAL_SCRATCH = (
+    pltpu.VMEM((CHIPS * ROWS, WIDTH), F32),
+    pltpu.VMEM((HALF, HIDDEN), F32),
+    pltpu.SemaphoreType.DMA((6,)),
+)
 
 
 def local(kernel, out_shape, specs, *operands):
@@ -430,8 +453,13 @@
     got = lax.ppermute(give, "member", other_core)
     sent = local(pair_kernel, shaped(CHIPS, CHUNK + 2 * PIECE, WIDTH), [VMEM] * 2, keep, got)
     got = swap(sent, "member", same_core)
-    input_grad = local(
-        home_kernel, shaped(OWN, GROUPS * SPREAD, WIDTH, dtype=F32), [SMEM, VMEM, VMEM], core, got, out_grad
+    input_grad, done = local(
+        home_kernel,
+        (shaped(OWN, GROUPS * SPREAD, WIDTH, dtype=F32), shaped(8, HALF, dtype=F32)),
+        [SMEM, VMEM, VMEM],
+        core,
+        got,
+        out_grad,
     )
     chunk = shaped(CHUNK, WIDTH)
     total = local(sum_kernel, chunk, [VMEM], got)
@@ -439,25 +467,36 @@
     sent, gains = local(
         last_round_kernel,
         (shaped(CHIPS, ROWS, WIDTH), shaped(GAIN_ROWS, WIDTH)),
-        [VMEM] * 4,
+        [VMEM] * 5,
         total,
         *across(total, (2, 4, 6)),
+        done,
     )
     mine = swap(sent, "member", same_core).reshape(CHIPS * ROWS, WIDTH)
     theirs = lax.ppermute(mine, "member", other_core)
     scale = 1.0 / math.sqrt(MEMBERS * GROUPS * SPREAD * spaces)
     square = shaped(WIDTH, WIDTH, dtype=F32)
     row = shaped(1, WIDTH, dtype=F32)
-    grads = local(
-        functools.partial(final_kernel, scale),
-        (square, square, square, square, shaped(WIDTH, HIDDEN, dtype=F32), shaped(HIDDEN, WIDTH, dtype=F32), row, row),
-        [SMEM, VMEM, VMEM, VMEM],
-        core,
-        mine,
-        theirs,
-        gains,
-    )
-    return (input_grad, *grads[:6], grads[6].reshape(WIDTH), grads[7].reshape(WIDTH))
+    grads_shape = (square, square, square, square, shaped(WIDTH, HIDDEN, dtype=F32), shaped(HIDDEN, WIDTH, dtype=F32))
+    params = pltpu.CompilerParams(vmem_limit_bytes=32 * 1024 * 1024)
+    *grads, gain1, gain2 = pl.pallas_call(
+        functools.partial(mine_kernel, scale),
+        out_shape=(*grads_shape, row, row),
+        in_specs=[SMEM, VMEM, VMEM],
+        out_specs=(*[HBM] * 6, VMEM, VMEM),
+        scratch_shapes=FINAL_SCRATCH,
+        compiler_params=params,
+    )(core, mine, gains)
+    grads = pl.pallas_call(
+        functools.partial(theirs_kernel, scale),
+        out_shape=grads_shape,
+        in_specs=[SMEM, VMEM, *[HBM] * 6],
+        out_specs=(HBM,) * 6,
+        input_output_aliases={2 + index: index for index in range(6)},
+        scratch_shapes=FINAL_SCRATCH,
+        compiler_params=params,
+    )(core, theirs, *grads)
+    return (input_grad, *grads, gain1.reshape(WIDTH), gain2.reshape(WIDTH))
 
 
 def solution(mesh):

time: 109 us -> 108 us (level)
  waiting for transfers between devices: 30 us -> 28.3 us
    pallas_call x0 -> x2, Pallas kernels: none -> 2.96 us  [the longest x1 1.76 us: on_device(): pl.pallas_call(functools.partial(mine_kernel, scale), out_shape=(*grads_s...]
    pallas_call x6 -> x5, Pallas kernels: 3.38 us -> 1.5 us  [local(): pl.pallas_call(kernel, out_shape=out_shape, in_specs=specs, out_specs=jax...]
  transfers between devices with their start and end apart: 9 -> 9, of which waited for: 7 -> 7; matrix products, arithmetic and copies ran while one was open for 0% -> 0% of each run, Pallas kernels for 1% -> 3%
where the time goes in v4:
time: 108 us
  blocking collectives  32.5 us (30%)
  waiting for transfers between devices  28.3 us (26%)
  starting transfers between devices  27.9 us (26%)
  Pallas kernels  18.2 us (17%)
    all_to_all x2, blocking collectives, swap(): lax.all_to_all(array, axis, split_axis=0, concat_axis=0, tiled=True, axis...  32.5 us
    all_to_all x1, waiting for transfers between devices, swap(): lax.all_to_all(array, axis, split_axis=0, concat_axis=0, tiled=True, axis...  15.8 us
    ppermute x6, starting transfers between devices, across(): lax.ppermute(array, 'space', [(k, k ^ step) for k in range(spaces)])  12.6 us
    pallas_call x1, Pallas kernels, run_layer(): pl.pallas_call(layer_kernel, out_shape=(shape, shape), in_specs=[SMEM] +...  11.7 us
    ppermute x6, waiting for transfers between devices, across(): lax.ppermute(array, 'space', [(k, k ^ step) for k in range(spaces)])  10 us
    all_to_all x1, starting transfers between devices, swap(): lax.all_to_all(array, axis, split_axis=0, concat_axis=0, tiled=True, axis...  7.06 us
    ppermute x1, starting transfers between devices, on_device(): theirs = lax.ppermute(mine, 'member', other_core)  7.03 us
    ppermute x1, waiting for transfers between devices, on_device(): got = lax.ppermute(give, 'member', other_core)  2.33 us
  transfers between devices with their start and end apart: 9, of which 7 were waited for; matrix products, arithmetic and copies ran while one was open for 0% of the time, Pallas kernels for 3%

profile of v4, /device:TPU:1, one launch (start us, length us, event | category | flops | bytes accessed | tf_op | source)
XLA Modules:
  0.0 107.9 jit_solution(14228054467614035478)
XLA Ops:
  0.6 2.1 %shard_map.169 = bf16[16,2,4,16,256]{4,3,2,1,0:T(8,128)(2,1)} custom-call(bf16[4,256,256]{2,1,0:T(8,128)(2,1)} %input_ref.1, bf16[4,256,256]{2,1,0:T(8,128)(2,1)} %grad_ref.3), custom_call_target="tpu_custom_call" | custom-call | tf_op jit(solution)/shard_map/pallas_call | solution.py:318
  2.7 0.0 copy-start.6
  2.7 0.0 copy-start.7
  2.8 0.0 copy-start.8
  2.8 0.0 copy-start.1
  2.8 0.0 copy-start.4
  2.8 0.0 copy-start.5
  2.8 7.1 %all-to-all-start = ((bf16[16,2,4,16,256]{4,3,2,1,0:T(8,128)(2,1)}), bf16[16,2,4,16,256]{4,3,2,1,0:T(8,128)(2,1)S(1)}, u32[]{:S(2)}, u32[]{:S(2)}) async-start(bf16[16,2,4,16,256]{4,3,2,1,0:T(8,128)(2,1)} %shard_map.169), calls=%async_computation | async-start | bytes 2097152 | tf_op jit(solution)/shard_map/all_to_all | solution.py:431
  10.0 15.8 %all-to-all-done.both_ref = bf16[16,2,4,16,256]{4,3,2,1,0:T(8,128)(2,1)S(1)} async-done(((bf16[16,2,4,16,256]{4,3,2,1,0:T(8,128)(2,1)}), bf16[16,2,4,16,256]{4,3,2,1,0:T(8,128)(2,1)S(1)}, u32[]{:S(2)}, u32[]{:S(2)}) %all-to-all-start) | async-done | bytes 1048608 | tf_op jit(solution)/shard_map/all_to_all | solution.py:431
  25.7 11.7 %shard_map.170 = (bf16[8,264,256]{2,1,0:T(8,128)(2,1)S(1)}, bf16[8,264,256]{2,1,0:T(8,128)(2,1)S(1)}) custom-call(s32[1]{0:T(128)} %bitcast.core_ref, bf16[16,2,4,16,256]{4,3,2,1,0:T(8,128)(2,1)S(1)} %all-to-all-done.both_ref, f32[1,256]{1,0:T(1,128)S(1)} %bitcast.8, bf16[256,768]{1,0:T(8,128)(2,1)S(1)} %pad_maximum_fusion.wqkv_ref, ...), custom_call_target="tpu_custom_call" | custom-call | flops 5000000000 | bytes 6000000 | tf_op jit(solution)/shard_map/pallas_call | solution.py:283
  37.5 1.1 %collective-permute-start = (bf16[8,264,256]{2,1,0:T(8,128)(2,1)S(1)}, bf16[8,264,256]{2,1,0:T(8,128)(2,1)S(1)}, u32[]{:S(2)}, u32[]{:S(2)}) collective-permute-start(bf16[8,264,256]{2,1,0:T(8,128)(2,1)S(1)} %get-tuple-element.30), channel_id=1, source_target_pairs={{0,16},{16,0},{32,48},{48,32},{64,80},{80,64},{96,112},{112,96},{1... | collective-permute-start | bytes 3244040 | tf_op jit(solution)/shard_map/ppermute | solution.py:453
  38.6 2.3 %collective-permute-done.got_ref = bf16[8,264,256]{2,1,0:T(8,128)(2,1)S(1)} collective-permute-done((bf16[8,264,256]{2,1,0:T(8,128)(2,1)S(1)}, bf16[8,264,256]{2,1,0:T(8,128)(2,1)S(1)}, u32[]{:S(2)}, u32[]{:S(2)}) %collective-permute-start) | collective-permute-done | bytes 1081376 | tf_op jit(solution)/shard_map/ppermute | solution.py:453
  40.9 0.2 shard_map.171
  41.1 21.1 %all_to_all.15.got_ref = bf16[8,328,256]{2,1,0:T(8,128)(2,1)S(1)} all-to-all(bf16[8,328,256]{2,1,0:T(8,128)(2,1)S(1)} %shard_map.171), channel_id=1, replica_groups={{0,32,64,96,128,160,192,224},{16,48,80,112,144,176,208,240},{1,33,65,97..., dimensions={0} | all-to-all | bytes 2686976 | tf_op jit(solution)/shard_map/all_to_all | solution.py:431
  62.2 0.1 shard_map.173.own_ref
  62.4 3.9 %collective-permute-start.3 = (bf16[200,256]{1,0:T(8,128)(2,1)S(1)}, bf16[200,256]{1,0:T(8,128)(2,1)S(1)}, u32[]{:S(2)}, u32[]{:S(2)}) collective-permute-start(bf16[200,256]{1,0:T(8,128)(2,1)S(1)} %shard_map.173.own_ref), channel_id=1, source_target_pairs={{0,9},{1,8},{2,11},{3,10},{4,13},{5,12},{6,15},{7,14},{8,1},{9,0},... | collective-permute-start | bytes 307208 | tf_op jit(solution)/shard_map/ppermute | solution.py:446
  66.2 0.5 collective-permute-start.2
  66.8 1.6 %collective-permute-done.3.third_ref = bf16[200,256]{1,0:T(8,128)(2,1)S(1)} collective-permute-done((bf16[200,256]{1,0:T(8,128)(2,1)S(1)}, bf16[200,256]{1,0:T(8,128)(2,1)S(1)}, u32[]{:S(2)}, u32[]{:S(2)}) %collective-permute-start.3) | collective-permute-done | bytes 102432 | tf_op jit(solution)/shard_map/ppermute | solution.py:446
  68.4 2.9 %collective-permute-done.2.second_ref = bf16[200,256]{1,0:T(8,128)(2,1)S(1)} collective-permute-done((bf16[200,256]{1,0:T(8,128)(2,1)S(1)}, bf16[200,256]{1,0:T(8,128)(2,1)S(1)}, u32[]{:S(2)}, u32[]{:S(2)}) %collective-permute-start.2) | collective-permute-done | bytes 102432 | tf_op jit(solution)/shard_map/ppermute | solution.py:446
  71.3 0.1 shard_map.174.own_ref
  71.3 6.0 %collective-permute-start.6 = (bf16[200,256]{1,0:T(8,128)(2,1)S(1)}, bf16[200,256]{1,0:T(8,128)(2,1)S(1)}, u32[]{:S(2)}, u32[]{:S(2)}) collective-permute-start(bf16[200,256]{1,0:T(8,128)(2,1)S(1)} %shard_map.174.own_ref), channel_id=1, source_target_pairs={{0,6},{1,7},{2,4},{3,5},{4,2},{5,3},{6,0},{7,1},{8,14},{9,15},{10,... | collective-permute-start | bytes 307208 | tf_op jit(solution)/shard_map/ppermute | solution.py:446
  77.4 1.0 collective-permute-start.5
  78.4 1.2 %collective-permute-start.4 = (bf16[200,256]{1,0:T(8,128)(2,1)S(1)}, bf16[200,256]{1,0:T(8,128)(2,1)S(1)}, u32[]{:S(2)}, u32[]{:S(2)}) collective-permute-start(bf16[200,256]{1,0:T(8,128)(2,1)S(1)} %shard_map.174.own_ref), channel_id=1, source_target_pairs={{0,2},{1,3},{2,0},{3,1},{4,6},{5,7},{6,4},{7,5},{8,10},{9,11},{10,... | collective-permute-start | bytes 307208 | tf_op jit(solution)/shard_map/ppermute | solution.py:446
  79.6 1.1 %shard_map.172 = (f32[4,256,256]{2,1,0:T(8,128)}, f32[8,128]{1,0:T(8,128)S(1)}) custom-call(s32[1]{0:T(128)} %bitcast.core_ref, bf16[8,328,256]{2,1,0:T(8,128)(2,1)S(1)} %all_to_all.15.got_ref, bf16[4,256,256]{2,1,0:T(8,128)(2,1)S(1)} %copy-done), custom_call_target="tpu_custom_call" | custom-call | tf_op jit(solution)/shard_map/pallas_call | solution.py:417
  80.6 2.5 %collective-permute-done.6.third_ref = bf16[200,256]{1,0:T(8,128)(2,1)S(1)} collective-permute-done((bf16[200,256]{1,0:T(8,128)(2,1)S(1)}, bf16[200,256]{1,0:T(8,128)(2,1)S(1)}, u32[]{:S(2)}, u32[]{:S(2)}) %collective-permute-start.6) | collective-permute-done | bytes 102432 | tf_op jit(solution)/shard_map/ppermute | solution.py:446
  83.1 3.1 %collective-permute-done.5.second_ref = bf16[200,256]{1,0:T(8,128)(2,1)S(1)} collective-permute-done((bf16[200,256]{1,0:T(8,128)(2,1)S(1)}, bf16[200,256]{1,0:T(8,128)(2,1)S(1)}, u32[]{:S(2)}, u32[]{:S(2)}) %collective-permute-start.5) | collective-permute-done | bytes 102432 | tf_op jit(solution)/shard_map/ppermute | solution.py:446
  86.2 0.1 shard_map.175
  86.3 11.4 %all_to_all.16 = bf16[8,192,256]{2,1,0:T(8,128)(2,1)S(1)} all-to-all(bf16[8,192,256]{2,1,0:T(8,128)(2,1)S(1)} %get-tuple-element.33), channel_id=1, replica_groups={{0,32,64,96,128,160,192,224},{16,48,80,112,144,176,208,240},{1,33,65,97..., dimensions={0} | all-to-all | bytes 1572864 | tf_op jit(solution)/shard_map/all_to_all | solution.py:431
  97.6 7.0 %collective-permute-start.7 = (bf16[1536,256]{1,0:T(8,128)(2,1)S(1)}, bf16[1536,256]{1,0:T(8,128)(2,1)S(1)}, u32[]{:S(2)}, u32[]{:S(2)}) collective-permute-start(bf16[1536,256]{1,0:T(8,128)(2,1)S(1)} %bitcast.6), channel_id=1, source_target_pairs={{0,16},{16,0},{32,48},{48,32},{64,80},{80,64},{96,112},{112,96},{1... | collective-permute-start | bytes 2359304 | tf_op jit(solution)/shard_map/ppermute | solution.py:476
  104.6 1.8 %shard_map.176 = (f32[256,256]{1,0:T(8,128)}, f32[256,256]{1,0:T(8,128)}, f32[256,256]{1,0:T(8,128)}, f32[256,256]{1,0:T(8,128)}, f32[256,1024]{1,0:T(8,128)}, /...) custom-call(s32[1]{0:T(128)} %bitcast.core_ref, bf16[1536,256]{1,0:T(8,128)(2,1)S(1)} %bitcast.7, ...), custom_call_target="tpu_custom_call" | custom-call | tf_op jit(solution)/shard_map/pallas_call | solution.py:482
  106.4 0.1 collective-permute-done.7.part_ref
  106.6 1.2 %shard_map.177 = (f32[256,256]{1,0:T(8,128)}, f32[256,256]{1,0:T(8,128)}, f32[256,256]{1,0:T(8,128)}, f32[256,256]{1,0:T(8,128)}, f32[256,1024]{1,0:T(8,128)}, /*index=5*/f32[1024,256]{1,0:T(8,128)}) custom-call(s32[1]{0:T(128)} %bitcast.core_ref, ...), custom_call_target="tpu_custom_call", output_to_operand_aliasing={{0}: (2, {}), {1}: (3, {}), {2}: (4, {}), {3}: (5, {}), {4}... | custom-call | tf_op jit(solution)/shard_map/pallas_call | solution.py:490
  (16 shorter events, 0.1 us)
Async XLA Ops:
  2.7 7.2 %copy-start.6 = (bf16[256,256]{1,0:T(8,128)(2,1)S(1)}, bf16[256,256]{1,0:T(8,128)(2,1)}, u32[]{:S(2)}) copy-start(bf16[256,256]{1,0:T(8,128)(2,1)} %param.15) | copy-start | bytes 393220
  2.7 7.2 %copy-start.7 = (bf16[256,256]{1,0:T(8,128)(2,1)S(1)}, bf16[256,256]{1,0:T(8,128)(2,1)}, u32[]{:S(2)}) copy-start(bf16[256,256]{1,0:T(8,128)(2,1)} %param.14) | copy-start | bytes 393220
  2.8 7.1 %copy-start.8 = (bf16[256,256]{1,0:T(8,128)(2,1)S(1)}, bf16[256,256]{1,0:T(8,128)(2,1)}, u32[]{:S(2)}) copy-start(bf16[256,256]{1,0:T(8,128)(2,1)} %param.13) | copy-start | bytes 393220
  2.8 22.9 %copy-start.1 = (bf16[256,1024]{1,0:T(8,128)(2,1)S(1)}, bf16[256,1024]{1,0:T(8,128)(2,1)}, u32[]{:S(2)}) copy-start(bf16[256,1024]{1,0:T(8,128)(2,1)} %wup_ref.1) | copy-start | bytes 1572868
  2.8 22.9 %copy-start.2 = (bf16[1024,256]{1,0:T(8,128)(2,1)S(1)}, bf16[1024,256]{1,0:T(8,128)(2,1)}, u32[]{:S(2)}) copy-start(bf16[1024,256]{1,0:T(8,128)(2,1)} %wdown_ref.1) | copy-start | bytes 1572868
  2.8 22.9 %copy-start.3 = (bf16[256,256]{1,0:T(8,128)(2,1)S(1)}, bf16[256,256]{1,0:T(8,128)(2,1)}, u32[]{:S(2)}) copy-start(bf16[256,256]{1,0:T(8,128)(2,1)} %wout_ref.1) | copy-start | bytes 393220
  2.8 22.9 %copy-start.4 = (f32[256]{0:T(256)S(1)}, f32[256]{0:T(256)}, u32[]{:S(2)}) copy-start(f32[256]{0:T(256)} %param.12) | copy-start | bytes 3076
  2.8 22.9 %copy-start.5 = (f32[256]{0:T(256)S(1)}, f32[256]{0:T(256)}, u32[]{:S(2)}) copy-start(f32[256]{0:T(256)} %param.17) | copy-start | bytes 3076
  2.8 22.9 %all-to-all-start = ((bf16[16,2,4,16,256]{4,3,2,1,0:T(8,128)(2,1)}), bf16[16,2,4,16,256]{4,3,2,1,0:T(8,128)(2,1)S(1)}, u32[]{:S(2)}, u32[]{:S(2)}) async-start(bf16[16,2,4,16,256]{4,3,2,1,0:T(8,128)(2,1)} %shard_map.169), calls=%async_computation | async-start | bytes 2097152 | tf_op jit(solution)/shard_map/all_to_all | solution.py:431
  37.5 3.5 %collective-permute-start = (bf16[8,264,256]{2,1,0:T(8,128)(2,1)S(1)}, bf16[8,264,256]{2,1,0:T(8,128)(2,1)S(1)}, u32[]{:S(2)}, u32[]{:S(2)}) collective-permute-start(bf16[8,264,256]{2,1,0:T(8,128)(2,1)S(1)} %get-tuple-element.30), channel_id=1, source_target_pairs={{0,16},{16,0},{32,48},{48,32},{64,80},{80,64},{96,112},{112,96},{1... | collective-permute-start | bytes 3244040 | tf_op jit(solution)/shard_map/ppermute | solution.py:453
  62.2 17.3 %copy-start = (bf16[4,256,256]{2,1,0:T(8,128)(2,1)S(1)}, bf16[4,256,256]{2,1,0:T(8,128)(2,1)}, u32[]{:S(2)}) copy-start(bf16[4,256,256]{2,1,0:T(8,128)(2,1)} %grad_ref.3) | copy-start | bytes 1572868
  62.4 6.0 %collective-permute-start.3 = (bf16[200,256]{1,0:T(8,128)(2,1)S(1)}, bf16[200,256]{1,0:T(8,128)(2,1)S(1)}, u32[]{:S(2)}, u32[]{:S(2)}) collective-permute-start(bf16[200,256]{1,0:T(8,128)(2,1)S(1)} %shard_map.173.own_ref), channel_id=1, source_target_pairs={{0,9},{1,8},{2,11},{3,10},{4,13},{5,12},{6,15},{7,14},{8,1},{9,0},... | collective-permute-start | bytes 307208 | tf_op jit(solution)/shard_map/ppermute | solution.py:446
  66.2 5.0 %collective-permute-start.2 = (bf16[200,256]{1,0:T(8,128)(2,1)S(1)}, bf16[200,256]{1,0:T(8,128)(2,1)S(1)}, u32[]{:S(2)}, u32[]{:S(2)}) collective-permute-start(bf16[200,256]{1,0:T(8,128)(2,1)S(1)} %shard_map.173.own_ref), channel_id=1, source_target_pairs={{0,8},{1,9},{2,10},{3,11},{4,12},{5,13},{6,14},{7,15},{8,0},{9,1},... | collective-permute-start | bytes 307208 | tf_op jit(solution)/shard_map/ppermute | solution.py:446
  66.8 4.5 %collective-permute-start.1 = (bf16[200,256]{1,0:T(8,128)(2,1)S(1)}, bf16[200,256]{1,0:T(8,128)(2,1)S(1)}, u32[]{:S(2)}, u32[]{:S(2)}) collective-permute-start(bf16[200,256]{1,0:T(8,128)(2,1)S(1)} %shard_map.173.own_ref), channel_id=1, source_target_pairs={{0,1},{1,0},{2,3},{3,2},{4,5},{5,4},{6,7},{7,6},{8,9},{9,8},{10,11... | collective-permute-start | bytes 307208 | tf_op jit(solution)/shard_map/ppermute | solution.py:446
  71.3 11.8 %collective-permute-start.6 = (bf16[200,256]{1,0:T(8,128)(2,1)S(1)}, bf16[200,256]{1,0:T(8,128)(2,1)S(1)}, u32[]{:S(2)}, u32[]{:S(2)}) collective-permute-start(bf16[200,256]{1,0:T(8,128)(2,1)S(1)} %shard_map.174.own_ref), channel_id=1, source_target_pairs={{0,6},{1,7},{2,4},{3,5},{4,2},{5,3},{6,0},{7,1},{8,14},{9,15},{10,... | collective-permute-start | bytes 307208 | tf_op jit(solution)/shard_map/ppermute | solution.py:446
  77.4 8.8 %collective-permute-start.5 = (bf16[200,256]{1,0:T(8,128)(2,1)S(1)}, bf16[200,256]{1,0:T(8,128)(2,1)S(1)}, u32[]{:S(2)}, u32[]{:S(2)}) collective-permute-start(bf16[200,256]{1,0:T(8,128)(2,1)S(1)} %shard_map.174.own_ref), channel_id=1, source_target_pairs={{0,4},{1,5},{2,6},{3,7},{4,0},{5,1},{6,2},{7,3},{8,12},{9,13},{10,... | collective-permute-start | bytes 307208 | tf_op jit(solution)/shard_map/ppermute | solution.py:446
  78.4 7.8 %collective-permute-start.4 = (bf16[200,256]{1,0:T(8,128)(2,1)S(1)}, bf16[200,256]{1,0:T(8,128)(2,1)S(1)}, u32[]{:S(2)}, u32[]{:S(2)}) collective-permute-start(bf16[200,256]{1,0:T(8,128)(2,1)S(1)} %shard_map.174.own_ref), channel_id=1, source_target_pairs={{0,2},{1,3},{2,0},{3,1},{4,6},{5,7},{6,4},{7,5},{8,10},{9,11},{10,... | collective-permute-start | bytes 307208 | tf_op jit(solution)/shard_map/ppermute | solution.py:446
  97.6 8.9 %collective-permute-start.7 = (bf16[1536,256]{1,0:T(8,128)(2,1)S(1)}, bf16[1536,256]{1,0:T(8,128)(2,1)S(1)}, u32[]{:S(2)}, u32[]{:S(2)}) collective-permute-start(bf16[1536,256]{1,0:T(8,128)(2,1)S(1)} %bitcast.6), channel_id=1, source_target_pairs={{0,16},{16,0},{32,48},{48,32},{64,80},{80,64},{96,112},{112,96},{1... | collective-permute-start | bytes 2359304 | tf_op jit(solution)/shard_map/ppermute | solution.py:476

commit v5 on v4

--- a/solution.py
+++ b/solution.py
@@ -22,6 +22,7 @@
 HALF = WIDTH // 2
 HALF_HEADS = HEADS // 2
 LANES = HALF_HEADS * MEMBERS
+GROUP = 8
 ROWS = 192
 GAIN_ROWS = 8
 CHUNK = ROWS + GAIN_ROWS
@@ -128,110 +129,155 @@
     def spread_heads(rows):
         return jnp.concatenate([rows] * HALF_HEADS, axis=0) * mask[...]
 
-    inverse1 = []
-    for patch, rows in enumerate(blocks):
-        unit, inverse = norm_rows(patch_rows(xs, patch))
-        unit1s[rows] = unit
-        inverse1.append(inverse)
-        n1s[rows] = (unit * gain1).astype(B16)
-        ogs[rows] = patch_rows(gs, patch).astype(B16)
-    for i in range(3):
-        lanes = slice(i * WIDTH, (i + 1) * WIDTH)
-        qkv[:, lanes] = jnp.dot(n1s[...], wqkv_ref[:, lanes], preferred_element_type=F32).astype(B16)
-
-    units = [(patch, side) for patch in range(SPREAD) for side in range(2)]
+    inverse1, inverse2 = {}, {}
+    gain_sums = [jnp.zeros((MEMBERS, WIDTH), F32), jnp.zeros((MEMBERS, WIDTH), F32)]
+    rows_of = [slice(first, first + GROUP * MEMBERS) for first in range(0, TOKENS, GROUP * MEMBERS)]
+    groups = [range(first, first + GROUP) for first in range(0, SPREAD, GROUP)]
 
     def part(ref, index, patch, side):
         return ref[blocks[patch], index * WIDTH + side * HALF : index * WIDTH + (side + 1) * HALF]
 
-    def staged(stages):
-        lag = 4
-        for step in range(0, len(units) + lag * (len(stages) - 1), lag):
-            for late, stage in enumerate(stages):
-                for unit in units[max(step - lag * late, 0) : max(step - lag * late + lag, 0)]:
-                    stage(*unit)
-
-    def score(patch, side):
-        spread_query = spread_heads(part(qkv, 0, patch, side))
-        expanded[patch, side] = spread_query
-        probs[patch, side] = dot(part(qkv, 1, patch, side), spread_query, (1, 1)) * SCALE
-
-    def soften(patch, side):
-        scores = probs[patch, side]
-        scores = jnp.exp(scores - jnp.max(scores, axis=0, keepdims=True))
-        weights = scores * (1.0 / jnp.sum(scores, axis=0, keepdims=True))
-        probs[patch, side] = weights
-        rounded[patch, side] = weights.astype(B16)
-
-    def mix(patch, side):
-        mixed = own_heads(dot(rounded[patch, side], part(qkv, 2, patch, side), (0, 0)))
-        mixs[blocks[patch], halves[side]] = mixed.astype(B16)
-
-    staged((score, soften, mix))
-    products[...] = jnp.dot(mixs[...], wout_ref[...], preferred_element_type=F32)
-    inverse2 = []
-    for patch, rows in enumerate(blocks):
-        unit, inverse = norm_rows(patch_rows(xs, patch) + products[rows])
-        unit2s[rows] = unit
-        inverse2.append(inverse)
-        n2s[rows] = (unit * gain2).astype(B16)
-
-    for i in range(HIDDEN // WIDTH):
-        lanes = slice(i * WIDTH, (i + 1) * WIDTH)
-        wide_products[i % 2, 0] = jnp.dot(n2s[...], wup_ref[:, lanes], preferred_element_type=F32)
-        wide_products[i % 2, 1] = dot(ogs[...], wdown_ref[lanes], (1, 1))
-        for rows in blocks:
-            activated, slopes = gelu_pair(wide_products[i % 2, 0, rows])
-            acts[rows, lanes] = activated.astype(B16)
-            gpre[rows, lanes] = (wide_products[i % 2, 1, rows] * slopes).astype(B16)
-    products[...] = dot(gpre[...], wup_ref[...], (1, 1))
-    gain2_sum = jnp.zeros((MEMBERS, WIDTH), F32)
-    for patch, rows in enumerate(blocks):
-        unit, grad = unit2s[rows], products[rows]
-        gain2_sum = gain2_sum + grad * unit
-        back = norm_back(unit, inverse2[patch], gain2, grad)
-        backs[rows] = back
-        gas[rows] = (ogs[rows].astype(F32) + back).astype(B16)
-    gmix[...] = dot(gas[...], wout_ref[...], (1, 1)).astype(B16)
-
     def keep_grad(index, patch, side, grad):
         gqkv[blocks[patch], index * WIDTH + side * HALF : index * WIDTH + (side + 1) * HALF] = grad.astype(B16)
-
-    def meet(patch, side):
-        spread_grad = spread_heads(gmix[blocks[patch], halves[side]])
-        dprobs[patch, side] = dot(part(qkv, 2, patch, side), spread_grad, (1, 1))
-        keep_grad(2, patch, side, jnp.dot(rounded[patch, side], spread_grad, preferred_element_type=F32))
-
-    def bend(patch, side):
-        weights = probs[patch, side]
-        product = weights * dprobs[patch, side]
-        dscore = (product - weights * jnp.sum(product, axis=0, keepdims=True)) * SCALE
-        rounded[patch, side] = dscore.astype(B16)
-
-    def finish(patch, side):
-        dscore = rounded[patch, side]
-        keep_grad(1, patch, side, jnp.dot(dscore, expanded[patch, side], preferred_element_type=F32))
-        keep_grad(0, patch, side, own_heads(dot(dscore, part(qkv, 1, patch, side), (0, 0))))
 
     def keep_part(first, total):
         rows = total.shape[0] // 2
         for half in range(2):
             parts[half, first : first + rows] = total[half * rows : (half + 1) * rows].astype(B16)
 
-    for i in range(HIDDEN // WIDTH):
+    def first_norm(group):
+        for patch in groups[group]:
+            rows = blocks[patch]
+            unit, inverse1[patch] = norm_rows(patch_rows(xs, patch))
+            unit1s[rows] = unit
+            n1s[rows] = (unit * gain1).astype(B16)
+            ogs[rows] = patch_rows(gs, patch).astype(B16)
+
+    def project(group):
+        rows = rows_of[group]
+        for i in range(3):
+            lanes = slice(i * WIDTH, (i + 1) * WIDTH)
+            qkv[rows, lanes] = jnp.dot(n1s[rows], wqkv_ref[:, lanes], preferred_element_type=F32).astype(B16)
+
+    def score(group):
+        for patch in groups[group]:
+            for side in range(2):
+                spread_query = spread_heads(part(qkv, 0, patch, side))
+                expanded[patch, side] = spread_query
+                probs[patch, side] = dot(part(qkv, 1, patch, side), spread_query, (1, 1)) * SCALE
+
+    def soften(group):
+        for patch in groups[group]:
+            for side in range(2):
+                scores = probs[patch, side]
+                scores = jnp.exp(scores - jnp.max(scores, axis=0, keepdims=True))
+                weights = scores * (1.0 / jnp.sum(scores, axis=0, keepdims=True))
+                probs[patch, side] = weights
+                rounded[patch, side] = weights.astype(B16)
+
+    def mix(group):
+        for patch in groups[group]:
+            for side in range(2):
+                mixed = own_heads(dot(rounded[patch, side], part(qkv, 2, patch, side), (0, 0)))
+                mixs[blocks[patch], halves[side]] = mixed.astype(B16)
+
+    def join(group):
+        rows = rows_of[group]
+        products[rows] = jnp.dot(mixs[rows], wout_ref[...], preferred_element_type=F32)
+
+    def second_norm(group):
+        for patch in groups[group]:
+            rows = blocks[patch]
+            unit, inverse2[patch] = norm_rows(patch_rows(xs, patch) + products[rows])
+            unit2s[rows] = unit
+            n2s[rows] = (unit * gain2).astype(B16)
+
+    def rise(group):
+        rows = rows_of[group]
+        for i in range(HIDDEN // WIDTH):
+            lanes = slice(i * WIDTH, (i + 1) * WIDTH)
+            wide_products[group % 2, 0, :, lanes] = jnp.dot(n2s[rows], wup_ref[:, lanes], preferred_element_type=F32)
+            wide_products[group % 2, 1, :, lanes] = dot(ogs[rows], wdown_ref[lanes], (1, 1))
+
+    def curve(group):
+        for i in range(HIDDEN // WIDTH):
+            lanes = slice(i * WIDTH, (i + 1) * WIDTH)
+            for index, patch in enumerate(groups[group]):
+                here = slice(index * MEMBERS, (index + 1) * MEMBERS)
+                activated, slopes = gelu_pair(wide_products[group % 2, 0, here, lanes])
+                acts[blocks[patch], lanes] = activated.astype(B16)
+                gpre[blocks[patch], lanes] = (wide_products[group % 2, 1, here, lanes] * slopes).astype(B16)
+
+    def fall(group):
+        rows = rows_of[group]
+        products[rows] = dot(gpre[rows], wup_ref[...], (1, 1))
+
+    def second_back(group):
+        for patch in groups[group]:
+            rows = blocks[patch]
+            unit, grad = unit2s[rows], products[rows]
+            gain_sums[1] = gain_sums[1] + grad * unit
+            back = norm_back(unit, inverse2[patch], gain2, grad)
+            backs[rows] = back
+            gas[rows] = (ogs[rows].astype(F32) + back).astype(B16)
+
+    def part_back(group):
+        rows = rows_of[group]
+        gmix[rows] = dot(gas[rows], wout_ref[...], (1, 1)).astype(B16)
+
+    def meet(group):
+        for patch in groups[group]:
+            for side in range(2):
+                spread_grad = spread_heads(gmix[blocks[patch], halves[side]])
+                dprobs[patch, side] = dot(part(qkv, 2, patch, side), spread_grad, (1, 1))
+                keep_grad(2, patch, side, jnp.dot(rounded[patch, side], spread_grad, preferred_element_type=F32))
+
+    def bend(group):
+        for patch in groups[group]:
+            for side in range(2):
+                weights = probs[patch, side]
+                product = weights * dprobs[patch, side]
+                dscore = (product - weights * jnp.sum(product, axis=0, keepdims=True)) * SCALE
+                rounded[patch, side] = dscore.astype(B16)
+
+    def finish(group):
+        for patch in groups[group]:
+            for side in range(2):
+                dscore = rounded[patch, side]
+                keep_grad(1, patch, side, jnp.dot(dscore, expanded[patch, side], preferred_element_type=F32))
+                keep_grad(0, patch, side, own_heads(dot(dscore, part(qkv, 1, patch, side), (0, 0))))
+
+    def first_fall(group):
+        rows = rows_of[group]
+        products[rows] = dot(gqkv[rows], wqkv_ref[...], (1, 1))
+
+    def first_back(group):
+        for patch in groups[group]:
+            rows = blocks[patch]
+            unit, grad = unit1s[rows], products[rows]
+            gain_sums[0] = gain_sums[0] + grad * unit
+            delta = backs[rows] + norm_back(unit, inverse1[patch], gain1, grad)
+            for side, lanes in enumerate(halves):
+                ds[side, pl.ds(patch, MEMBERS, stride=SPREAD), :] = delta[:, lanes]
+
+    def weigh(i):
         lanes = slice(i * WIDTH, (i + 1) * WIDTH)
         keep_part(4 * HALF + i * HALF, dot(n2s[...], gpre[:, lanes], (0, 0)))
         first = 8 * HALF + i % 2 * WIDTH
         parts[i // 2, first : first + WIDTH] = dot(ogs[...], acts[:, lanes], (0, 0)).T.astype(B16)
-    staged((meet, bend, finish))
-    products[...] = dot(gqkv[...], wqkv_ref[...], (1, 1))
-    gain1_sum = jnp.zeros((MEMBERS, WIDTH), F32)
-    for patch, rows in enumerate(blocks):
-        unit, grad = unit1s[rows], products[rows]
-        gain1_sum = gain1_sum + grad * unit
-        delta = backs[rows] + norm_back(unit, inverse1[patch], gain1, grad)
-        for side, lanes in enumerate(halves):
-            ds[side, pl.ds(patch, MEMBERS, stride=SPREAD), :] = delta[:, lanes]
+
+    stages = (
+        first_norm, project, score, soften, mix, join, second_norm, rise, curve,
+        fall, second_back, part_back, meet, bend, finish, first_fall, first_back,
+    )
+    weigh_from = len(groups) + stages.index(curve)
+    for step in range(len(groups) + len(stages) - 1):
+        for late, stage in enumerate(stages):
+            if 0 <= step - late < len(groups):
+                stage(step - late)
+        if 0 <= step - weigh_from < HIDDEN // WIDTH:
+            weigh(step - weigh_from)
+    gain1_sum, gain2_sum = gain_sums
 
     part_qkv = dot(n1s[...], gqkv[...], (0, 0))
     for i in range(3):
@@ -276,7 +322,7 @@
         pltpu.VMEM(rows, F32),
         pltpu.VMEM(rows, F32),
         pltpu.VMEM(rows, F32),
-        pltpu.VMEM((2, 2, *rows), F32),
+        pltpu.VMEM((2, 2, GROUP * MEMBERS, HIDDEN), F32),
         pltpu.VMEM((2, CHIPS * ROWS, WIDTH), B16),
     ]
     shape = shaped(CHIPS, CHUNK + PIECE, WIDTH)
@@ -463,13 +509,13 @@
     )
     chunk = shaped(CHUNK, WIDTH)
     total = local(sum_kernel, chunk, [VMEM], got)
-    total = local(round_kernel, chunk, [VMEM] * 4, total, *across(total, (1, 8, 9)))
+    total = local(round_kernel, chunk, [VMEM] * 4, total, *across(total, (2, 4, 6) ))
     sent, gains = local(
         last_round_kernel,
         (shaped(CHIPS, ROWS, WIDTH), shaped(GAIN_ROWS, WIDTH)),
         [VMEM] * 5,
         total,
-        *across(total, (2, 4, 6)),
+        *across(total, (1, 8, 9)),
         done,
     )
     mine = swap(sent, "member", same_core).reshape(CHIPS * ROWS, WIDTH)

time: 108 us -> 107 us (level)
  starting transfers between devices: 27.9 us -> 26.2 us
    ppermute x1, starting transfers between devices: 7.03 us -> 5.5 us  [on_device(): theirs = lax.ppermute(mine, 'member', other_core)]
  transfers between devices with their start and end apart: 9 -> 9, of which waited for: 7 -> 9; matrix products, arithmetic and copies ran while one was open for 0% -> 0% of each run, Pallas kernels for 3% -> 3%
where the time goes in v5:
time: 107 us
  blocking collectives  32.5 us (30%)
  waiting for transfers between devices  29.2 us (27%)
  starting transfers between devices  26.2 us (24%)
  Pallas kernels  17.7 us (17%)
    all_to_all x2, blocking collectives, swap(): lax.all_to_all(array, axis, split_axis=0, concat_axis=0, tiled=True, axis...  32.5 us
    all_to_all x1, waiting for transfers between devices, swap(): lax.all_to_all(array, axis, split_axis=0, concat_axis=0, tiled=True, axis...  15.8 us
    ppermute x6, starting transfers between devices, across(): lax.ppermute(array, 'space', [(k, k ^ step) for k in range(spaces)])  12.5 us
    pallas_call x1, Pallas kernels, run_layer(): pl.pallas_call(layer_kernel, out_shape=(shape, shape), in_specs=[SMEM] +...  11.2 us
    ppermute x6, waiting for transfers between devices, across(): lax.ppermute(array, 'space', [(k, k ^ step) for k in range(spaces)])  10.9 us
    all_to_all x1, starting transfers between devices, swap(): lax.all_to_all(array, axis, split_axis=0, concat_axis=0, tiled=True, axis...  7.06 us
    ppermute x1, starting transfers between devices, on_device(): theirs = lax.ppermute(mine, 'member', other_core)  5.5 us
    ppermute x1, waiting for transfers between devices, on_device(): got = lax.ppermute(give, 'member', other_core)  2.33 us
  transfers between devices with their start and end apart: 9, of which 9 were waited for; matrix products, arithmetic and copies ran while one was open for 0% of the time, Pallas kernels for 3%

profile of v5, /device:TPU:1, one launch (start us, length us, event | category | flops | bytes accessed | tf_op | source)
XLA Modules:
  0.0 106.6 jit_solution(16452051240580059139)
XLA Ops:
  0.6 2.1 %shard_map.169 = bf16[16,2,4,16,256]{4,3,2,1,0:T(8,128)(2,1)} custom-call(bf16[4,256,256]{2,1,0:T(8,128)(2,1)} %input_ref.1, bf16[4,256,256]{2,1,0:T(8,128)(2,1)} %grad_ref.3), custom_call_target="tpu_custom_call" | custom-call | tf_op jit(solution)/shard_map/pallas_call | solution.py:364
  2.7 0.0 copy-start.6
  2.8 0.0 copy-start.1
  2.8 0.0 copy-start.2
  2.8 7.1 %all-to-all-start = ((bf16[16,2,4,16,256]{4,3,2,1,0:T(8,128)(2,1)}), bf16[16,2,4,16,256]{4,3,2,1,0:T(8,128)(2,1)S(1)}, u32[]{:S(2)}, u32[]{:S(2)}) async-start(bf16[16,2,4,16,256]{4,3,2,1,0:T(8,128)(2,1)} %shard_map.169), calls=%async_computation | async-start | bytes 2097152 | tf_op jit(solution)/shard_map/all_to_all | solution.py:477
  10.0 15.8 %all-to-all-done.both_ref = bf16[16,2,4,16,256]{4,3,2,1,0:T(8,128)(2,1)S(1)} async-done(((bf16[16,2,4,16,256]{4,3,2,1,0:T(8,128)(2,1)}), bf16[16,2,4,16,256]{4,3,2,1,0:T(8,128)(2,1)S(1)}, u32[]{:S(2)}, u32[]{:S(2)}) %all-to-all-start) | async-done | bytes 1048608 | tf_op jit(solution)/shard_map/all_to_all | solution.py:477
  25.7 11.2 %shard_map.170 = (bf16[8,264,256]{2,1,0:T(8,128)(2,1)S(1)}, bf16[8,264,256]{2,1,0:T(8,128)(2,1)S(1)}) custom-call(s32[1]{0:T(128)} %bitcast.core_ref, bf16[16,2,4,16,256]{4,3,2,1,0:T(8,128)(2,1)S(1)} %all-to-all-done.both_ref, f32[1,256]{1,0:T(1,128)S(1)} %bitcast.8, bf16[256,768]{1,0:T(8,128)(2,1)S(1)} %pad_maximum_fusion.wqkv_ref, ...), custom_call_target="tpu_custom_call" | custom-call | flops 5000000000 | bytes 6000000 | tf_op jit(solution)/shard_map/pallas_call | solution.py:329
  36.9 1.1 %collective-permute-start = (bf16[8,264,256]{2,1,0:T(8,128)(2,1)S(1)}, bf16[8,264,256]{2,1,0:T(8,128)(2,1)S(1)}, u32[]{:S(2)}, u32[]{:S(2)}) collective-permute-start(bf16[8,264,256]{2,1,0:T(8,128)(2,1)S(1)} %get-tuple-element.30), channel_id=1, source_target_pairs={{0,16},{16,0},{32,48},{48,32},{64,80},{80,64},{96,112},{112,96},{1... | collective-permute-start | bytes 3244040 | tf_op jit(solution)/shard_map/ppermute | solution.py:499
  38.1 2.3 %collective-permute-done.got_ref = bf16[8,264,256]{2,1,0:T(8,128)(2,1)S(1)} collective-permute-done((bf16[8,264,256]{2,1,0:T(8,128)(2,1)S(1)}, bf16[8,264,256]{2,1,0:T(8,128)(2,1)S(1)}, u32[]{:S(2)}, u32[]{:S(2)}) %collective-permute-start) | collective-permute-done | bytes 1081376 | tf_op jit(solution)/shard_map/ppermute | solution.py:499
  40.4 0.2 shard_map.171
  40.6 21.1 %all_to_all.15.got_ref = bf16[8,328,256]{2,1,0:T(8,128)(2,1)S(1)} all-to-all(bf16[8,328,256]{2,1,0:T(8,128)(2,1)S(1)} %shard_map.171), channel_id=1, replica_groups={{0,32,64,96,128,160,192,224},{16,48,80,112,144,176,208,240},{1,33,65,97..., dimensions={0} | all-to-all | bytes 2686976 | tf_op jit(solution)/shard_map/all_to_all | solution.py:477
  61.7 0.1 shard_map.173.own_ref
  61.8 6.1 %collective-permute-start.3 = (bf16[200,256]{1,0:T(8,128)(2,1)S(1)}, bf16[200,256]{1,0:T(8,128)(2,1)S(1)}, u32[]{:S(2)}, u32[]{:S(2)}) collective-permute-start(bf16[200,256]{1,0:T(8,128)(2,1)S(1)} %shard_map.173.own_ref), channel_id=1, source_target_pairs={{0,6},{1,7},{2,4},{3,5},{4,2},{5,3},{6,0},{7,1},{8,14},{9,15},{10,... | collective-permute-start | bytes 307208 | tf_op jit(solution)/shard_map/ppermute | solution.py:492
  67.9 1.0 collective-permute-start.2
  68.9 1.2 %collective-permute-start.1 = (bf16[200,256]{1,0:T(8,128)(2,1)S(1)}, bf16[200,256]{1,0:T(8,128)(2,1)S(1)}, u32[]{:S(2)}, u32[]{:S(2)}) collective-permute-start(bf16[200,256]{1,0:T(8,128)(2,1)S(1)} %shard_map.173.own_ref), channel_id=1, source_target_pairs={{0,2},{1,3},{2,0},{3,1},{4,6},{5,7},{6,4},{7,5},{8,10},{9,11},{10,... | collective-permute-start | bytes 307208 | tf_op jit(solution)/shard_map/ppermute | solution.py:492
  70.1 3.4 %collective-permute-done.3.third_ref = bf16[200,256]{1,0:T(8,128)(2,1)S(1)} collective-permute-done((bf16[200,256]{1,0:T(8,128)(2,1)S(1)}, bf16[200,256]{1,0:T(8,128)(2,1)S(1)}, u32[]{:S(2)}, u32[]{:S(2)}) %collective-permute-start.3) | collective-permute-done | bytes 102432 | tf_op jit(solution)/shard_map/ppermute | solution.py:492
  73.5 2.9 %collective-permute-done.2.second_ref = bf16[200,256]{1,0:T(8,128)(2,1)S(1)} collective-permute-done((bf16[200,256]{1,0:T(8,128)(2,1)S(1)}, bf16[200,256]{1,0:T(8,128)(2,1)S(1)}, u32[]{:S(2)}, u32[]{:S(2)}) %collective-permute-start.2) | collective-permute-done | bytes 102432 | tf_op jit(solution)/shard_map/ppermute | solution.py:492
  76.4 3.0 %collective-permute-done.1.first_ref = bf16[200,256]{1,0:T(8,128)(2,1)S(1)} collective-permute-done((bf16[200,256]{1,0:T(8,128)(2,1)S(1)}, bf16[200,256]{1,0:T(8,128)(2,1)S(1)}, u32[]{:S(2)}, u32[]{:S(2)}) %collective-permute-start.1) | collective-permute-done | bytes 102432 | tf_op jit(solution)/shard_map/ppermute | solution.py:492
  79.5 0.1 shard_map.174.own_ref
  79.5 0.7 collective-permute-start.6
  80.2 2.0 %collective-permute-start.5 = (bf16[200,256]{1,0:T(8,128)(2,1)S(1)}, bf16[200,256]{1,0:T(8,128)(2,1)S(1)}, u32[]{:S(2)}, u32[]{:S(2)}) collective-permute-start(bf16[200,256]{1,0:T(8,128)(2,1)S(1)} %shard_map.174.own_ref), channel_id=1, source_target_pairs={{0,8},{1,9},{2,10},{3,11},{4,12},{5,13},{6,14},{7,15},{8,0},{9,1},... | collective-permute-start | bytes 307208 | tf_op jit(solution)/shard_map/ppermute | solution.py:492
  82.2 1.6 %collective-permute-start.4 = (bf16[200,256]{1,0:T(8,128)(2,1)S(1)}, bf16[200,256]{1,0:T(8,128)(2,1)S(1)}, u32[]{:S(2)}, u32[]{:S(2)}) collective-permute-start(bf16[200,256]{1,0:T(8,128)(2,1)S(1)} %shard_map.174.own_ref), channel_id=1, source_target_pairs={{0,1},{1,0},{2,3},{3,2},{4,5},{5,4},{6,7},{7,6},{8,9},{9,8},{10,11... | collective-permute-start | bytes 307208 | tf_op jit(solution)/shard_map/ppermute | solution.py:492
  83.8 1.1 %shard_map.172 = (f32[4,256,256]{2,1,0:T(8,128)}, f32[8,128]{1,0:T(8,128)S(1)}) custom-call(s32[1]{0:T(128)} %bitcast.core_ref, bf16[8,328,256]{2,1,0:T(8,128)(2,1)S(1)} %all_to_all.15.got_ref, bf16[4,256,256]{2,1,0:T(8,128)(2,1)S(1)} %copy-done), custom_call_target="tpu_custom_call" | custom-call | tf_op jit(solution)/shard_map/pallas_call | solution.py:463
  84.9 0.8 collective-permute-done.6.third_ref
  85.6 0.7 collective-permute-done.5.second_ref
  86.3 0.1 collective-permute-done.4.first_ref
  86.4 0.1 shard_map.175
  86.5 11.4 %all_to_all.16 = bf16[8,192,256]{2,1,0:T(8,128)(2,1)S(1)} all-to-all(bf16[8,192,256]{2,1,0:T(8,128)(2,1)S(1)} %get-tuple-element.33), channel_id=1, replica_groups={{0,32,64,96,128,160,192,224},{16,48,80,112,144,176,208,240},{1,33,65,97..., dimensions={0} | all-to-all | bytes 1572864 | tf_op jit(solution)/shard_map/all_to_all | solution.py:477
  97.9 5.5 %collective-permute-start.7 = (bf16[1536,256]{1,0:T(8,128)(2,1)S(1)}, bf16[1536,256]{1,0:T(8,128)(2,1)S(1)}, u32[]{:S(2)}, u32[]{:S(2)}) collective-permute-start(bf16[1536,256]{1,0:T(8,128)(2,1)S(1)} %bitcast.6), channel_id=1, source_target_pairs={{0,16},{16,0},{32,48},{48,32},{64,80},{80,64},{96,112},{112,96},{1... | collective-permute-start | bytes 2359304 | tf_op jit(solution)/shard_map/ppermute | solution.py:522
  103.4 1.8 %shard_map.176 = (f32[256,256]{1,0:T(8,128)}, f32[256,256]{1,0:T(8,128)}, f32[256,256]{1,0:T(8,128)}, f32[256,256]{1,0:T(8,128)}, f32[256,1024]{1,0:T(8,128)}, /...) custom-call(s32[1]{0:T(128)} %bitcast.core_ref, bf16[1536,256]{1,0:T(8,128)(2,1)S(1)} %bitcast.7, ...), custom_call_target="tpu_custom_call" | custom-call | tf_op jit(solution)/shard_map/pallas_call | solution.py:528
  105.1 0.1 collective-permute-done.7.part_ref
  105.3 1.2 %shard_map.177 = (f32[256,256]{1,0:T(8,128)}, f32[256,256]{1,0:T(8,128)}, f32[256,256]{1,0:T(8,128)}, f32[256,256]{1,0:T(8,128)}, f32[256,1024]{1,0:T(8,128)}, /*index=5*/f32[1024,256]{1,0:T(8,128)}) custom-call(s32[1]{0:T(128)} %bitcast.core_ref, ...), custom_call_target="tpu_custom_call", output_to_operand_aliasing={{0}: (2, {}), {1}: (3, {}), {2}: (4, {}), {3}: (5, {}), {4}... | custom-call | tf_op jit(solution)/shard_map/pallas_call | solution.py:536
  (16 shorter events, 0.1 us)
Async XLA Ops:
  2.7 7.2 %copy-start.6 = (bf16[256,256]{1,0:T(8,128)(2,1)S(1)}, bf16[256,256]{1,0:T(8,128)(2,1)}, u32[]{:S(2)}) copy-start(bf16[256,256]{1,0:T(8,128)(2,1)} %param.15) | copy-start | bytes 393220
  2.7 7.2 %copy-start.7 = (bf16[256,256]{1,0:T(8,128)(2,1)S(1)}, bf16[256,256]{1,0:T(8,128)(2,1)}, u32[]{:S(2)}) copy-start(bf16[256,256]{1,0:T(8,128)(2,1)} %param.14) | copy-start | bytes 393220
  2.8 7.1 %copy-start.8 = (bf16[256,256]{1,0:T(8,128)(2,1)S(1)}, bf16[256,256]{1,0:T(8,128)(2,1)}, u32[]{:S(2)}) copy-start(bf16[256,256]{1,0:T(8,128)(2,1)} %param.13) | copy-start | bytes 393220
  2.8 22.9 %copy-start.1 = (bf16[256,1024]{1,0:T(8,128)(2,1)S(1)}, bf16[256,1024]{1,0:T(8,128)(2,1)}, u32[]{:S(2)}) copy-start(bf16[256,1024]{1,0:T(8,128)(2,1)} %wup_ref.1) | copy-start | bytes 1572868
  2.8 22.9 %copy-start.2 = (bf16[1024,256]{1,0:T(8,128)(2,1)S(1)}, bf16[1024,256]{1,0:T(8,128)(2,1)}, u32[]{:S(2)}) copy-start(bf16[1024,256]{1,0:T(8,128)(2,1)} %wdown_ref.1) | copy-start | bytes 1572868
  2.8 22.9 %copy-start.3 = (bf16[256,256]{1,0:T(8,128)(2,1)S(1)}, bf16[256,256]{1,0:T(8,128)(2,1)}, u32[]{:S(2)}) copy-start(bf16[256,256]{1,0:T(8,128)(2,1)} %wout_ref.1) | copy-start | bytes 393220
  2.8 22.9 %copy-start.4 = (f32[256]{0:T(256)S(1)}, f32[256]{0:T(256)}, u32[]{:S(2)}) copy-start(f32[256]{0:T(256)} %param.12) | copy-start | bytes 3076
  2.8 22.9 %copy-start.5 = (f32[256]{0:T(256)S(1)}, f32[256]{0:T(256)}, u32[]{:S(2)}) copy-start(f32[256]{0:T(256)} %param.17) | copy-start | bytes 3076
  2.8 22.9 %all-to-all-start = ((bf16[16,2,4,16,256]{4,3,2,1,0:T(8,128)(2,1)}), bf16[16,2,4,16,256]{4,3,2,1,0:T(8,128)(2,1)S(1)}, u32[]{:S(2)}, u32[]{:S(2)}) async-start(bf16[16,2,4,16,256]{4,3,2,1,0:T(8,128)(2,1)} %shard_map.169), calls=%async_computation | async-start | bytes 2097152 | tf_op jit(solution)/shard_map/all_to_all | solution.py:477
  36.9 3.5 %collective-permute-start = (bf16[8,264,256]{2,1,0:T(8,128)(2,1)S(1)}, bf16[8,264,256]{2,1,0:T(8,128)(2,1)S(1)}, u32[]{:S(2)}, u32[]{:S(2)}) collective-permute-start(bf16[8,264,256]{2,1,0:T(8,128)(2,1)S(1)} %get-tuple-element.30), channel_id=1, source_target_pairs={{0,16},{16,0},{32,48},{48,32},{64,80},{80,64},{96,112},{112,96},{1... | collective-permute-start | bytes 3244040 | tf_op jit(solution)/shard_map/ppermute | solution.py:499
  61.7 22.1 %copy-start = (bf16[4,256,256]{2,1,0:T(8,128)(2,1)S(1)}, bf16[4,256,256]{2,1,0:T(8,128)(2,1)}, u32[]{:S(2)}) copy-start(bf16[4,256,256]{2,1,0:T(8,128)(2,1)} %grad_ref.3) | copy-start | bytes 1572868
  61.8 11.7 %collective-permute-start.3 = (bf16[200,256]{1,0:T(8,128)(2,1)S(1)}, bf16[200,256]{1,0:T(8,128)(2,1)S(1)}, u32[]{:S(2)}, u32[]{:S(2)}) collective-permute-start(bf16[200,256]{1,0:T(8,128)(2,1)S(1)} %shard_map.173.own_ref), channel_id=1, source_target_pairs={{0,6},{1,7},{2,4},{3,5},{4,2},{5,3},{6,0},{7,1},{8,14},{9,15},{10,... | collective-permute-start | bytes 307208 | tf_op jit(solution)/shard_map/ppermute | solution.py:492
  67.9 8.5 %collective-permute-start.2 = (bf16[200,256]{1,0:T(8,128)(2,1)S(1)}, bf16[200,256]{1,0:T(8,128)(2,1)S(1)}, u32[]{:S(2)}, u32[]{:S(2)}) collective-permute-start(bf16[200,256]{1,0:T(8,128)(2,1)S(1)} %shard_map.173.own_ref), channel_id=1, source_target_pairs={{0,4},{1,5},{2,6},{3,7},{4,0},{5,1},{6,2},{7,3},{8,12},{9,13},{10,... | collective-permute-start | bytes 307208 | tf_op jit(solution)/shard_map/ppermute | solution.py:492
  68.9 10.5 %collective-permute-start.1 = (bf16[200,256]{1,0:T(8,128)(2,1)S(1)}, bf16[200,256]{1,0:T(8,128)(2,1)S(1)}, u32[]{:S(2)}, u32[]{:S(2)}) collective-permute-start(bf16[200,256]{1,0:T(8,128)(2,1)S(1)} %shard_map.173.own_ref), channel_id=1, source_target_pairs={{0,2},{1,3},{2,0},{3,1},{4,6},{5,7},{6,4},{7,5},{8,10},{9,11},{10,... | collective-permute-start | bytes 307208 | tf_op jit(solution)/shard_map/ppermute | solution.py:492
  79.5 6.1 %collective-permute-start.6 = (bf16[200,256]{1,0:T(8,128)(2,1)S(1)}, bf16[200,256]{1,0:T(8,128)(2,1)S(1)}, u32[]{:S(2)}, u32[]{:S(2)}) collective-permute-start(bf16[200,256]{1,0:T(8,128)(2,1)S(1)} %shard_map.174.own_ref), channel_id=1, source_target_pairs={{0,9},{1,8},{2,11},{3,10},{4,13},{5,12},{6,15},{7,14},{8,1},{9,0},... | collective-permute-start | bytes 307208 | tf_op jit(solution)/shard_map/ppermute | solution.py:492
  80.2 6.1 %collective-permute-start.5 = (bf16[200,256]{1,0:T(8,128)(2,1)S(1)}, bf16[200,256]{1,0:T(8,128)(2,1)S(1)}, u32[]{:S(2)}, u32[]{:S(2)}) collective-permute-start(bf16[200,256]{1,0:T(8,128)(2,1)S(1)} %shard_map.174.own_ref), channel_id=1, source_target_pairs={{0,8},{1,9},{2,10},{3,11},{4,12},{5,13},{6,14},{7,15},{8,0},{9,1},... | collective-permute-start | bytes 307208 | tf_op jit(solution)/shard_map/ppermute | solution.py:492
  82.2 4.3 %collective-permute-start.4 = (bf16[200,256]{1,0:T(8,128)(2,1)S(1)}, bf16[200,256]{1,0:T(8,128)(2,1)S(1)}, u32[]{:S(2)}, u32[]{:S(2)}) collective-permute-start(bf16[200,256]{1,0:T(8,128)(2,1)S(1)} %shard_map.174.own_ref), channel_id=1, source_target_pairs={{0,1},{1,0},{2,3},{3,2},{4,5},{5,4},{6,7},{7,6},{8,9},{9,8},{10,11... | collective-permute-start | bytes 307208 | tf_op jit(solution)/shard_map/ppermute | solution.py:492
  97.9 7.4 %collective-permute-start.7 = (bf16[1536,256]{1,0:T(8,128)(2,1)S(1)}, bf16[1536,256]{1,0:T(8,128)(2,1)S(1)}, u32[]{:S(2)}, u32[]{:S(2)}) collective-permute-start(bf16[1536,256]{1,0:T(8,128)(2,1)S(1)} %bitcast.6), channel_id=1, source_target_pairs={{0,16},{16,0},{32,48},{48,32},{64,80},{80,64},{96,112},{112,96},{1... | collective-permute-start | bytes 2359304 | tf_op jit(solution)/shard_map/ppermute | solution.py:522

commit v6 on v5

--- a/solution.py
+++ b/solution.py
@@ -24,7 +24,7 @@
 LANES = HALF_HEADS * MEMBERS
 GROUP = 8
 ROWS = 192
-GAIN_ROWS = 8
+GAIN_ROWS = 16
 CHUNK = ROWS + GAIN_ROWS
 SLAB = 24
 SMALL = SLAB + GAIN_ROWS

time: 107 us -> 107 us (level)
  blocking collectives: 32.5 us -> 33.6 us
    all_to_all x2, blocking collectives: 32.5 us -> 33.6 us  [swap(): lax.all_to_all(array, axis, split_axis=0, concat_axis=0, tiled=True, axis...]
  transfers between devices with their start and end apart: 9 -> 9, of which waited for: 9 -> 7; matrix products, arithmetic and copies ran while one was open for 0% -> 0% of each run, Pallas kernels for 3% -> 3%
where the time goes in v6:
time: 107 us
  blocking collectives  33.6 us (31%)
  waiting for transfers between devices  28.3 us (26%)
  starting transfers between devices  26.5 us (25%)
  Pallas kernels  17.7 us (17%)
    all_to_all x2, blocking collectives, swap(): lax.all_to_all(array, axis, split_axis=0, concat_axis=0, tiled=True, axis...  33.6 us
    all_to_all x1, waiting for transfers between devices, swap(): lax.all_to_all(array, axis, split_axis=0, concat_axis=0, tiled=True, axis...  15.8 us
    ppermute x6, starting transfers between devices, across(): lax.ppermute(array, 'space', [(k, k ^ step) for k in range(spaces)])  12.6 us
    pallas_call x1, Pallas kernels, run_layer(): pl.pallas_call(layer_kernel, out_shape=(shape, shape), in_specs=[SMEM] +...  11.2 us
    ppermute x6, waiting for transfers between devices, across(): lax.ppermute(array, 'space', [(k, k ^ step) for k in range(spaces)])  9.97 us
    all_to_all x1, starting transfers between devices, swap(): lax.all_to_all(array, axis, split_axis=0, concat_axis=0, tiled=True, axis...  7.06 us
    ppermute x1, starting transfers between devices, on_device(): theirs = lax.ppermute(mine, 'member', other_core)  5.8 us
    ppermute x1, waiting for transfers between devices, on_device(): got = lax.ppermute(give, 'member', other_core)  2.38 us
  transfers between devices with their start and end apart: 9, of which 7 were waited for; matrix products, arithmetic and copies ran while one was open for 0% of the time, Pallas kernels for 3%

profile of v6, /device:TPU:1, one launch (start us, length us, event | category | flops | bytes accessed | tf_op | source)
XLA Modules:
  0.0 107.2 jit_solution(12017326118274607848)
XLA Ops:
  0.6 2.1 %shard_map.169 = bf16[16,2,4,16,256]{4,3,2,1,0:T(8,128)(2,1)} custom-call(bf16[4,256,256]{2,1,0:T(8,128)(2,1)} %input_ref.1, bf16[4,256,256]{2,1,0:T(8,128)(2,1)} %grad_ref.3), custom_call_target="tpu_custom_call" | custom-call | tf_op jit(solution)/shard_map/pallas_call | solution.py:364
  2.7 0.0 copy-start.6
  2.7 0.0 copy-start.7
  2.8 0.0 copy-start.8
  2.8 0.0 copy-start.1
  2.8 0.0 copy-start.2
  2.8 0.0 copy-start.3
  2.8 7.1 %all-to-all-start = ((bf16[16,2,4,16,256]{4,3,2,1,0:T(8,128)(2,1)}), bf16[16,2,4,16,256]{4,3,2,1,0:T(8,128)(2,1)S(1)}, u32[]{:S(2)}, u32[]{:S(2)}) async-start(bf16[16,2,4,16,256]{4,3,2,1,0:T(8,128)(2,1)} %shard_map.169), calls=%async_computation | async-start | bytes 2097152 | tf_op jit(solution)/shard_map/all_to_all | solution.py:477
  10.0 15.8 %all-to-all-done.both_ref = bf16[16,2,4,16,256]{4,3,2,1,0:T(8,128)(2,1)S(1)} async-done(((bf16[16,2,4,16,256]{4,3,2,1,0:T(8,128)(2,1)}), bf16[16,2,4,16,256]{4,3,2,1,0:T(8,128)(2,1)S(1)}, u32[]{:S(2)}, u32[]{:S(2)}) %all-to-all-start) | async-done | bytes 1048608 | tf_op jit(solution)/shard_map/all_to_all | solution.py:477
  25.7 11.2 %shard_map.170 = (bf16[8,272,256]{2,1,0:T(8,128)(2,1)S(1)}, bf16[8,272,256]{2,1,0:T(8,128)(2,1)S(1)}) custom-call(s32[1]{0:T(128)} %bitcast.core_ref, bf16[16,2,4,16,256]{4,3,2,1,0:T(8,128)(2,1)S(1)} %all-to-all-done.both_ref, f32[1,256]{1,0:T(1,128)S(1)} %bitcast.8, bf16[256,768]{1,0:T(8,128)(2,1)S(1)} %pad_maximum_fusion.wqkv_ref, ...), custom_call_target="tpu_custom_call" | custom-call | flops 5000000000 | bytes 6000000 | tf_op jit(solution)/shard_map/pallas_call | solution.py:329
  36.9 1.1 %collective-permute-start = (bf16[8,272,256]{2,1,0:T(8,128)(2,1)S(1)}, bf16[8,272,256]{2,1,0:T(8,128)(2,1)S(1)}, u32[]{:S(2)}, u32[]{:S(2)}) collective-permute-start(bf16[8,272,256]{2,1,0:T(8,128)(2,1)S(1)} %get-tuple-element.30), channel_id=1, source_target_pairs={{0,16},{16,0},{32,48},{48,32},{64,80},{80,64},{96,112},{112,96},{1... | collective-permute-start | bytes 3342344 | tf_op jit(solution)/shard_map/ppermute | solution.py:499
  38.1 2.4 %collective-permute-done.got_ref = bf16[8,272,256]{2,1,0:T(8,128)(2,1)S(1)} collective-permute-done((bf16[8,272,256]{2,1,0:T(8,128)(2,1)S(1)}, bf16[8,272,256]{2,1,0:T(8,128)(2,1)S(1)}, u32[]{:S(2)}, u32[]{:S(2)}) %collective-permute-start) | collective-permute-done | bytes 1114144 | tf_op jit(solution)/shard_map/ppermute | solution.py:499
  40.4 0.2 shard_map.171
  40.6 21.2 %all_to_all.15.got_ref = bf16[8,336,256]{2,1,0:T(8,128)(2,1)S(1)} all-to-all(bf16[8,336,256]{2,1,0:T(8,128)(2,1)S(1)} %shard_map.171), channel_id=1, replica_groups={{0,32,64,96,128,160,192,224},{16,48,80,112,144,176,208,240},{1,33,65,97..., dimensions={0} | all-to-all | bytes 2752512 | tf_op jit(solution)/shard_map/all_to_all | solution.py:477
  61.8 0.1 shard_map.173.own_ref
  61.9 6.1 %collective-permute-start.3 = (bf16[208,256]{1,0:T(8,128)(2,1)S(1)}, bf16[208,256]{1,0:T(8,128)(2,1)S(1)}, u32[]{:S(2)}, u32[]{:S(2)}) collective-permute-start(bf16[208,256]{1,0:T(8,128)(2,1)S(1)} %shard_map.173.own_ref), channel_id=1, source_target_pairs={{0,6},{1,7},{2,4},{3,5},{4,2},{5,3},{6,0},{7,1},{8,14},{9,15},{10,... | collective-permute-start | bytes 319496 | tf_op jit(solution)/shard_map/ppermute | solution.py:492
  68.0 1.0 collective-permute-start.2
  69.0 1.2 %collective-permute-start.1 = (bf16[208,256]{1,0:T(8,128)(2,1)S(1)}, bf16[208,256]{1,0:T(8,128)(2,1)S(1)}, u32[]{:S(2)}, u32[]{:S(2)}) collective-permute-start(bf16[208,256]{1,0:T(8,128)(2,1)S(1)} %shard_map.173.own_ref), channel_id=1, source_target_pairs={{0,2},{1,3},{2,0},{3,1},{4,6},{5,7},{6,4},{7,5},{8,10},{9,11},{10,... | collective-permute-start | bytes 319496 | tf_op jit(solution)/shard_map/ppermute | solution.py:492
  70.2 3.5 %collective-permute-done.3.third_ref = bf16[208,256]{1,0:T(8,128)(2,1)S(1)} collective-permute-done((bf16[208,256]{1,0:T(8,128)(2,1)S(1)}, bf16[208,256]{1,0:T(8,128)(2,1)S(1)}, u32[]{:S(2)}, u32[]{:S(2)}) %collective-permute-start.3) | collective-permute-done | bytes 106528 | tf_op jit(solution)/shard_map/ppermute | solution.py:492
  73.7 3.0 %collective-permute-done.2.second_ref = bf16[208,256]{1,0:T(8,128)(2,1)S(1)} collective-permute-done((bf16[208,256]{1,0:T(8,128)(2,1)S(1)}, bf16[208,256]{1,0:T(8,128)(2,1)S(1)}, u32[]{:S(2)}, u32[]{:S(2)}) %collective-permute-start.2) | collective-permute-done | bytes 106528 | tf_op jit(solution)/shard_map/ppermute | solution.py:492
  76.7 0.1 shard_map.174.own_ref
  76.8 3.7 %collective-permute-start.6 = (bf16[208,256]{1,0:T(8,128)(2,1)S(1)}, bf16[208,256]{1,0:T(8,128)(2,1)S(1)}, u32[]{:S(2)}, u32[]{:S(2)}) collective-permute-start(bf16[208,256]{1,0:T(8,128)(2,1)S(1)} %shard_map.174.own_ref), channel_id=1, source_target_pairs={{0,9},{1,8},{2,11},{3,10},{4,13},{5,12},{6,15},{7,14},{8,1},{9,0},... | collective-permute-start | bytes 319496 | tf_op jit(solution)/shard_map/ppermute | solution.py:492
  80.5 0.5 collective-permute-start.5
  81.1 1.1 %shard_map.172 = (f32[4,256,256]{2,1,0:T(8,128)}, f32[8,128]{1,0:T(8,128)S(1)}) custom-call(s32[1]{0:T(128)} %bitcast.core_ref, bf16[8,336,256]{2,1,0:T(8,128)(2,1)S(1)} %all_to_all.15.got_ref, bf16[4,256,256]{2,1,0:T(8,128)(2,1)S(1)} %copy-done), custom_call_target="tpu_custom_call" | custom-call | tf_op jit(solution)/shard_map/pallas_call | solution.py:463
  82.2 1.5 %collective-permute-done.6.third_ref = bf16[208,256]{1,0:T(8,128)(2,1)S(1)} collective-permute-done((bf16[208,256]{1,0:T(8,128)(2,1)S(1)}, bf16[208,256]{1,0:T(8,128)(2,1)S(1)}, u32[]{:S(2)}, u32[]{:S(2)}) %collective-permute-start.6) | collective-permute-done | bytes 106528 | tf_op jit(solution)/shard_map/ppermute | solution.py:492
  83.7 1.9 %collective-permute-done.5.second_ref = bf16[208,256]{1,0:T(8,128)(2,1)S(1)} collective-permute-done((bf16[208,256]{1,0:T(8,128)(2,1)S(1)}, bf16[208,256]{1,0:T(8,128)(2,1)S(1)}, u32[]{:S(2)}, u32[]{:S(2)}) %collective-permute-start.5) | collective-permute-done | bytes 106528 | tf_op jit(solution)/shard_map/ppermute | solution.py:492
  85.6 0.1 shard_map.175
  85.7 12.5 %all_to_all.16 = bf16[8,192,256]{2,1,0:T(8,128)(2,1)S(1)} all-to-all(bf16[8,192,256]{2,1,0:T(8,128)(2,1)S(1)} %get-tuple-element.33), channel_id=1, replica_groups={{0,32,64,96,128,160,192,224},{16,48,80,112,144,176,208,240},{1,33,65,97..., dimensions={0} | all-to-all | bytes 1572864 | tf_op jit(solution)/shard_map/all_to_all | solution.py:477
  98.2 5.8 %collective-permute-start.7 = (bf16[1536,256]{1,0:T(8,128)(2,1)S(1)}, bf16[1536,256]{1,0:T(8,128)(2,1)S(1)}, u32[]{:S(2)}, u32[]{:S(2)}) collective-permute-start(bf16[1536,256]{1,0:T(8,128)(2,1)S(1)} %bitcast.6), channel_id=1, source_target_pairs={{0,16},{16,0},{32,48},{48,32},{64,80},{80,64},{96,112},{112,96},{1... | collective-permute-start | bytes 2359304 | tf_op jit(solution)/shard_map/ppermute | solution.py:522
  103.9 1.8 %shard_map.176 = (f32[256,256]{1,0:T(8,128)}, f32[256,256]{1,0:T(8,128)}, f32[256,256]{1,0:T(8,128)}, f32[256,256]{1,0:T(8,128)}, f32[256,1024]{1,0:T(8,128)}, /...) custom-call(s32[1]{0:T(128)} %bitcast.core_ref, bf16[1536,256]{1,0:T(8,128)(2,1)S(1)} %bitcast.7, ...), custom_call_target="tpu_custom_call" | custom-call | tf_op jit(solution)/shard_map/pallas_call | solution.py:528
  105.7 0.1 collective-permute-done.7.part_ref
  105.9 1.2 %shard_map.177 = (f32[256,256]{1,0:T(8,128)}, f32[256,256]{1,0:T(8,128)}, f32[256,256]{1,0:T(8,128)}, f32[256,256]{1,0:T(8,128)}, f32[256,1024]{1,0:T(8,128)}, /*index=5*/f32[1024,256]{1,0:T(8,128)}) custom-call(s32[1]{0:T(128)} %bitcast.core_ref, ...), custom_call_target="tpu_custom_call", output_to_operand_aliasing={{0}: (2, {}), {1}: (3, {}), {2}: (4, {}), {3}: (5, {}), {4}... | custom-call | tf_op jit(solution)/shard_map/pallas_call | solution.py:536
  (16 shorter events, 0.1 us)
Async XLA Ops:
  2.7 7.2 %copy-start.6 = (bf16[256,256]{1,0:T(8,128)(2,1)S(1)}, bf16[256,256]{1,0:T(8,128)(2,1)}, u32[]{:S(2)}) copy-start(bf16[256,256]{1,0:T(8,128)(2,1)} %param.15) | copy-start | bytes 393220
  2.7 7.2 %copy-start.7 = (bf16[256,256]{1,0:T(8,128)(2,1)S(1)}, bf16[256,256]{1,0:T(8,128)(2,1)}, u32[]{:S(2)}) copy-start(bf16[256,256]{1,0:T(8,128)(2,1)} %param.14) | copy-start | bytes 393220
  2.8 7.1 %copy-start.8 = (bf16[256,256]{1,0:T(8,128)(2,1)S(1)}, bf16[256,256]{1,0:T(8,128)(2,1)}, u32[]{:S(2)}) copy-start(bf16[256,256]{1,0:T(8,128)(2,1)} %param.13) | copy-start | bytes 393220
  2.8 22.9 %copy-start.1 = (bf16[256,1024]{1,0:T(8,128)(2,1)S(1)}, bf16[256,1024]{1,0:T(8,128)(2,1)}, u32[]{:S(2)}) copy-start(bf16[256,1024]{1,0:T(8,128)(2,1)} %wup_ref.1) | copy-start | bytes 1572868
  2.8 22.9 %copy-start.2 = (bf16[1024,256]{1,0:T(8,128)(2,1)S(1)}, bf16[1024,256]{1,0:T(8,128)(2,1)}, u32[]{:S(2)}) copy-start(bf16[1024,256]{1,0:T(8,128)(2,1)} %wdown_ref.1) | copy-start | bytes 1572868
  2.8 22.9 %copy-start.3 = (bf16[256,256]{1,0:T(8,128)(2,1)S(1)}, bf16[256,256]{1,0:T(8,128)(2,1)}, u32[]{:S(2)}) copy-start(bf16[256,256]{1,0:T(8,128)(2,1)} %wout_ref.1) | copy-start | bytes 393220
  2.8 22.9 %copy-start.4 = (f32[256]{0:T(256)S(1)}, f32[256]{0:T(256)}, u32[]{:S(2)}) copy-start(f32[256]{0:T(256)} %param.12) | copy-start | bytes 3076
  2.8 22.9 %copy-start.5 = (f32[256]{0:T(256)S(1)}, f32[256]{0:T(256)}, u32[]{:S(2)}) copy-start(f32[256]{0:T(256)} %param.17) | copy-start | bytes 3076
  2.8 22.9 %all-to-all-start = ((bf16[16,2,4,16,256]{4,3,2,1,0:T(8,128)(2,1)}), bf16[16,2,4,16,256]{4,3,2,1,0:T(8,128)(2,1)S(1)}, u32[]{:S(2)}, u32[]{:S(2)}) async-start(bf16[16,2,4,16,256]{4,3,2,1,0:T(8,128)(2,1)} %shard_map.169), calls=%async_computation | async-start | bytes 2097152 | tf_op jit(solution)/shard_map/all_to_all | solution.py:477
  36.9 3.5 %collective-permute-start = (bf16[8,272,256]{2,1,0:T(8,128)(2,1)S(1)}, bf16[8,272,256]{2,1,0:T(8,128)(2,1)S(1)}, u32[]{:S(2)}, u32[]{:S(2)}) collective-permute-start(bf16[8,272,256]{2,1,0:T(8,128)(2,1)S(1)} %get-tuple-element.30), channel_id=1, source_target_pairs={{0,16},{16,0},{32,48},{48,32},{64,80},{80,64},{96,112},{112,96},{1... | collective-permute-start | bytes 3342344 | tf_op jit(solution)/shard_map/ppermute | solution.py:499
  61.8 19.3 %copy-start = (bf16[4,256,256]{2,1,0:T(8,128)(2,1)S(1)}, bf16[4,256,256]{2,1,0:T(8,128)(2,1)}, u32[]{:S(2)}) copy-start(bf16[4,256,256]{2,1,0:T(8,128)(2,1)} %grad_ref.3) | copy-start | bytes 1572868
  61.9 11.8 %collective-permute-start.3 = (bf16[208,256]{1,0:T(8,128)(2,1)S(1)}, bf16[208,256]{1,0:T(8,128)(2,1)S(1)}, u32[]{:S(2)}, u32[]{:S(2)}) collective-permute-start(bf16[208,256]{1,0:T(8,128)(2,1)S(1)} %shard_map.173.own_ref), channel_id=1, source_target_pairs={{0,6},{1,7},{2,4},{3,5},{4,2},{5,3},{6,0},{7,1},{8,14},{9,15},{10,... | collective-permute-start | bytes 319496 | tf_op jit(solution)/shard_map/ppermute | solution.py:492
  68.0 8.7 %collective-permute-start.2 = (bf16[208,256]{1,0:T(8,128)(2,1)S(1)}, bf16[208,256]{1,0:T(8,128)(2,1)S(1)}, u32[]{:S(2)}, u32[]{:S(2)}) collective-permute-start(bf16[208,256]{1,0:T(8,128)(2,1)S(1)} %shard_map.173.own_ref), channel_id=1, source_target_pairs={{0,4},{1,5},{2,6},{3,7},{4,0},{5,1},{6,2},{7,3},{8,12},{9,13},{10,... | collective-permute-start | bytes 319496 | tf_op jit(solution)/shard_map/ppermute | solution.py:492
  69.0 7.7 %collective-permute-start.1 = (bf16[208,256]{1,0:T(8,128)(2,1)S(1)}, bf16[208,256]{1,0:T(8,128)(2,1)S(1)}, u32[]{:S(2)}, u32[]{:S(2)}) collective-permute-start(bf16[208,256]{1,0:T(8,128)(2,1)S(1)} %shard_map.173.own_ref), channel_id=1, source_target_pairs={{0,2},{1,3},{2,0},{3,1},{4,6},{5,7},{6,4},{7,5},{8,10},{9,11},{10,... | collective-permute-start | bytes 319496 | tf_op jit(solution)/shard_map/ppermute | solution.py:492
  76.8 6.9 %collective-permute-start.6 = (bf16[208,256]{1,0:T(8,128)(2,1)S(1)}, bf16[208,256]{1,0:T(8,128)(2,1)S(1)}, u32[]{:S(2)}, u32[]{:S(2)}) collective-permute-start(bf16[208,256]{1,0:T(8,128)(2,1)S(1)} %shard_map.174.own_ref), channel_id=1, source_target_pairs={{0,9},{1,8},{2,11},{3,10},{4,13},{5,12},{6,15},{7,14},{8,1},{9,0},... | collective-permute-start | bytes 319496 | tf_op jit(solution)/shard_map/ppermute | solution.py:492
  80.5 5.1 %collective-permute-start.5 = (bf16[208,256]{1,0:T(8,128)(2,1)S(1)}, bf16[208,256]{1,0:T(8,128)(2,1)S(1)}, u32[]{:S(2)}, u32[]{:S(2)}) collective-permute-start(bf16[208,256]{1,0:T(8,128)(2,1)S(1)} %shard_map.174.own_ref), channel_id=1, source_target_pairs={{0,8},{1,9},{2,10},{3,11},{4,12},{5,13},{6,14},{7,15},{8,0},{9,1},... | collective-permute-start | bytes 319496 | tf_op jit(solution)/shard_map/ppermute | solution.py:492
  81.1 4.5 %collective-permute-start.4 = (bf16[208,256]{1,0:T(8,128)(2,1)S(1)}, bf16[208,256]{1,0:T(8,128)(2,1)S(1)}, u32[]{:S(2)}, u32[]{:S(2)}) collective-permute-start(bf16[208,256]{1,0:T(8,128)(2,1)S(1)} %shard_map.174.own_ref), channel_id=1, source_target_pairs={{0,1},{1,0},{2,3},{3,2},{4,5},{5,4},{6,7},{7,6},{8,9},{9,8},{10,11... | collective-permute-start | bytes 319496 | tf_op jit(solution)/shard_map/ppermute | solution.py:492
  98.2 7.7 %collective-permute-start.7 = (bf16[1536,256]{1,0:T(8,128)(2,1)S(1)}, bf16[1536,256]{1,0:T(8,128)(2,1)S(1)}, u32[]{:S(2)}, u32[]{:S(2)}) collective-permute-start(bf16[1536,256]{1,0:T(8,128)(2,1)S(1)} %bitcast.6), channel_id=1, source_target_pairs={{0,16},{16,0},{32,48},{48,32},{64,80},{80,64},{96,112},{112,96},{1... | collective-permute-start | bytes 2359304 | tf_op jit(solution)/shard_map/ppermute | solution.py:522
